TPU v7x, 32 devices: a whole 2x2x4 slice. The times are simulated.
32 devices in a mesh: row: 8 (over y, x, core), col: 4 (over z).
Axes of the slice: x: 2, y: 2, z: 4, core: 2. Of those that a mesh axis runs over, the one named last changes fastest.
Arguments:
- activations: bfloat16 [768, 16384], P(('row', 'col')), may hold values from -14 to 14
- tenant_ids: int32 [768], P(('row', 'col')), may hold values from 0 to 63
- concept_labels: int32 [768], P(('row', 'col')), may hold values from 0 to 1
Outputs:
- covariance: float32 [16384, 16384], P('row', 'col')
- cross: float32 [128, 16384], P(None, ('row', 'col'))
All inputs are finite; a program needn't handle non-finite values.
Results may differ from a plain program's by a relative error of at most 0.0003.
Values may be sent and summed in bfloat16 or wider, within the bound.
No kernel may reach another device: no remote copies, remote signals or barrier semaphores. Data moves between devices by JAX's collectives and lax.ppermute only.
A program may use at most 128 MiB of HBM per device.

v0:
```python
import jax
import jax.numpy as jnp
from jax import lax
from jax.sharding import PartitionSpec as P

TENANTS = 64
LABELS = 2


def shards(activations, tenant_ids, concept_labels):
    local_tokens = activations.shape[0]
    width = activations.shape[1]
    row_count = lax.axis_size("row")
    col_count = lax.axis_size("col")
    groups = TENANTS * LABELS
    codes = tenant_ids * LABELS + concept_labels
    codes_rows = lax.all_gather(codes, "row", axis=0, tiled=True)
    row_piece = lax.all_to_all(activations, "row", split_axis=1, concat_axis=0, tiled=True)
    row_panel, codes_all = (
        lax.all_gather(row_piece, "col", axis=0, tiled=True),
        lax.all_gather(codes_rows, "col", axis=0, tiled=True),
    )
    total = row_panel.shape[0]
    row_width = row_panel.shape[1]
    row_view = row_panel.reshape(col_count, row_count, local_tokens, row_width)
    col_piece = lax.all_to_all(activations, "col", split_axis=1, concat_axis=0, tiled=True)
    col_panel = lax.all_gather(col_piece, "row", axis=0, tiled=True)
    col_view = col_panel.reshape(row_count, col_count, local_tokens, col_panel.shape[1])
    gram = jnp.einsum("abtf,batg->fg", row_view, col_view, preferred_element_type=jnp.float32)
    mean_row = jnp.sum(row_panel, axis=0, dtype=jnp.float32) / total
    mean_col = jnp.sum(col_panel, axis=0, dtype=jnp.float32) / total
    covariance = gram / total - mean_row[:, None] * mean_col[None, :]
    slice_width = width // (row_count * col_count)
    slice_start = lax.axis_index("col") * slice_width
    mean_slice = lax.dynamic_slice_in_dim(mean_row, slice_start, slice_width)
    group_ids = jnp.arange(groups, dtype=jnp.int32)
    onehot_all = codes_all[:, None] == group_ids[None, :]
    counts = jnp.sum(onehot_all.astype(jnp.float32), axis=0)
    panel_slice = lax.dynamic_slice_in_dim(row_panel, slice_start, slice_width, 1)
    sums = lax.dot_general(
        onehot_all.astype(jnp.bfloat16),
        panel_slice,
        (((0,), (0,)), ((), ())),
        preferred_element_type=jnp.float32,
    )
    cross = groups / total * (sums - counts[:, None] * mean_slice[None, :])
    return (covariance, cross)


def solution(mesh):
    placed = (P(("row", "col"), None), P(("row", "col")), P(("row", "col")))
    return jax.shard_map(
        shards,
        mesh=mesh,
        in_specs=placed,
        out_specs=(P("row", "col"), P(None, ("row", "col"))),
        check_vma=False,
    )
```

profile of v0, /device:TPU:0, one launch (start us, length us, event | category | flops | bytes accessed | tf_op | source)
XLA Modules:
  0.0 179.2 jit_solution(11825131425559418900)
XLA Ops:
  7.2 0.0 copy-start.4
  7.2 0.0 copy-start.3
  7.2 0.0 copy-start.1
  7.2 0.0 copy-start.2
  7.2 0.0 all-gather.3.cloned.1.call-start
  7.3 1.2 copy.27
  8.5 17.6 %all_to_all.38 = bf16[24,8,2048]{2,0,1:T(8,128)(2,1)} all-to-all(bf16[24,8,2048]{2,0,1:T(8,128)(2,1)S(1)} %bitcast.31), channel_id=1, replica_groups=mesh['row'=8,'col'=4] {'row'}, dimensions={1} | all-to-all | bytes 1572864 | tf_op jit(solution)/shard_map/all_to_all | solution.py:18
  26.1 0.0 all-gather.3.cloned.1.call-update
  26.1 0.0 all-gather.5.cloned.1.call-start
  26.2 1.2 copy.26
  27.4 45.1 %all_to_all.39 = bf16[24,4,4096]{2,0,1:T(8,128)(2,1)} all-to-all(bf16[24,4,4096]{2,0,1:T(8,128)(2,1)S(1)} %bitcast.32), channel_id=1, replica_groups=mesh['row'=8,'col'=4] {'col'}, dimensions={1} | all-to-all | bytes 1572864 | tf_op jit(solution)/shard_map/all_to_all | solution.py:26
  72.5 0.0 all-gather.5.cloned.1.call-update
  72.5 0.0 copy-done.4
  72.5 0.6 dynamic-slice
  73.1 0.0 copy-done.3
  73.1 0.6 dynamic-slice.1
  75.0 0.0 copy-done.1
  75.0 0.0 copy-done.2
  75.0 0.1 add_dynamic-update-slice_fusion
  75.1 6.1 %all-reduce = s32[192]{0:T(256)S(1)} all-reduce(s32[192]{0:T(256)S(1)} %add_dynamic-update-slice_fusion), channel_id=1, replica_groups=mesh['row'=8,'col'=4] {'row'}, use_global_device_ids=true, to_apply=%add | all-reduce | flops 192 | bytes 1536
  81.2 0.2 dynamic-update-slice.1
  81.4 7.4 %all-reduce.1 = s32[768]{0:T(1024)S(1)} all-reduce(s32[768]{0:T(1024)S(1)} %dynamic-update-slice.1), channel_id=1, replica_groups=mesh['row'=8,'col'=4] {'col'}, use_global_device_ids=true, to_apply=%add.1 | all-reduce | flops 768 | bytes 6144
  88.8 0.2 convert_reduce_fusion.2
  89.0 13.8 %all-gather.3.cloned.1.call-done = bf16[768,2048]{1,0:T(8,128)(2,1)} async-done(((bf16[192,2048]{1,0:T(8,128)(2,1)}), bf16[768,2048]{1,0:T(8,128)(2,1)}) %all-gather.3.cloned.1.call-update) | async-done | bytes 3145744 | tf_op jit(solution)/shard_map/all_gather | solution.py:20
  102.8 2.4 %convert_reduce_fusion.1 = f32[2048]{0:T(1024)S(1)} fusion(bf16[768,2048]{1,0:T(8,128)(2,1)} %all-gather.3.cloned.1.call-done), kind=kLoop, calls=%fused_computation.4 | loop fusion | flops 3143680 | bytes 3153920 | tf_op jit(solution)/shard_map/reduce_sum | solution.py:30
  105.2 0.1 dynamic_slice.7
  105.3 2.3 %fusion.2 = f32[128,512]{1,0:T(8,128)} fusion(bf16[768,2048]{1,0:T(8,128)(2,1)} %all-gather.3.cloned.1.call-done, s32[]{:T(128)S(6)} %select_n.4, s32[768]{0:T(1024)S(1)} %all-reduce.1, f32[512]{0:T(512)S(1)} %dynamic_slice.7, f32[128]{0:T(128)S(1)} %convert_reduce_fusion.2), kind=kOutput, calls=%fused_computation.6 | convolution fusion | flops 100958208 | bytes 1054212 | tf_op jit(solution)/shard_map/dot_general | solution.py:40
  107.6 40.6 %all-gather.5.cloned.1.call-done = bf16[768,4096]{1,0:T(8,128)(2,1)} async-done(((bf16[96,4096]{1,0:T(8,128)(2,1)}), bf16[768,4096]{1,0:T(8,128)(2,1)}) %all-gather.5.cloned.1.call-update) | async-done | bytes 6291472 | tf_op jit(solution)/shard_map/all_gather | solution.py:27
  148.2 0.0 copy-start
  148.2 4.0 %convert_reduce_fusion = f32[4096]{0:T(1024)S(1)} fusion(bf16[768,4096]{1,0:T(8,128)(2,1)} %all-gather.5.cloned.1.call-done), kind=kLoop, calls=%fused_computation.2 | loop fusion | flops 6287360 | bytes 6307840 | tf_op jit(solution)/shard_map/reduce_sum | solution.py:31
  152.2 0.6 copy-done
  152.8 19.5 %fusion = f32[2048,4096]{1,0:T(8,128)} fusion(bf16[4,8,24,2048]{3,2,1,0:T(8,128)(2,1)} %bitcast.26, f32[4096]{0:T(1024)S(1)} %broadcast_multiply_fusion, f32[2048]{0:T(1024)S(1)} %broadcast_multiply_fusion.1, bf16[8,4,24,4096]{3,2,1,0:T(8,128)(2,1)S(1)} %bitcast.25), kind=kOutput, calls=%fused_computation.1 | convolution fusion | flops 12910067712 | bytes 43016192 | tf_op jit(solution)/shard_map/abtf,batg->fg/dot_general | solution.py:29
  (4 shorter events, 0.0 us)
Async XLA Ops:
  7.2 65.4 %copy-start.4 = (u32[32]{0:T(128)S(1)}, u32[32]{0:T(128)}, u32[]{:S(2)}) copy-start(u32[32]{0:T(128)} %constant.28) | copy-start | bytes 388
  7.2 65.9 %copy-start.3 = (u32[32]{0:T(128)S(1)}, u32[32]{0:T(128)}, u32[]{:S(2)}) copy-start(u32[32]{0:T(128)} %constant.33) | copy-start | bytes 388
  7.2 67.8 %copy-start.1 = (s32[24]{0:T(128)S(1)}, s32[24]{0:T(128)}, u32[]{:S(2)}) copy-start(s32[24]{0:T(128)} %param.5) | copy-start | bytes 292
  7.2 67.8 %copy-start.2 = (s32[24]{0:T(128)S(1)}, s32[24]{0:T(128)}, u32[]{:S(2)}) copy-start(s32[24]{0:T(128)} %param.4) | copy-start | bytes 292
  7.2 95.6 %all-gather.3.cloned.1.call-start = ((), (), s32[]{:S(2)}) async-start(), calls=%async_computation.2 | async-start | bytes 3932160 | tf_op jit(solution)/shard_map/all_gather | solution.py:20
  26.1 122.1 %all-gather.5.cloned.1.call-start = ((), (), s32[]{:S(2)}) async-start(), calls=%async_computation.3 | async-start | bytes 7077888 | tf_op jit(solution)/shard_map/all_gather | solution.py:27
  148.2 4.6 %copy-start = (bf16[768,4096]{1,0:T(8,128)(2,1)S(1)}, bf16[768,4096]{1,0:T(8,128)(2,1)}, u32[]{:S(2)}) copy-start(bf16[768,4096]{1,0:T(8,128)(2,1)} %all-gather.5.cloned.1.call-done) | copy-start | bytes 18874372
Sparse Core Ops, SparseCore 0:
  26.2 76.5 all-gather.2
  104.7 43.4 all-gather.4
where the time goes:
time: 180 us; the launch traced here: 179 us
  blocking collectives  76.3 us (42%)
  waiting for transfers between devices  54.4 us (30%)
  matrix products  21.9 us (12%)
  between operations  15.4 us (9%)
  other arithmetic  6.71 us (4%)
  local copies, waits for them, and re-layouts  4.39 us (2%)
    all_to_all x1, blocking collectives, shards(): lax.all_to_all(activations, 'col', split_axis=1, concat_axis=0, tiled=True)  45.1 us
    all_gather x1, waiting for transfers between devices, shards(): col_panel = lax.all_gather(col_piece, 'row', axis=0, tiled=True)  40.6 us
    dot_general x1, matrix products, shards(): jnp.einsum('abtf,batg->fg', row_view, col_view, preferred_element_type=jn...  19.5 us
    all_to_all x1, blocking collectives, shards(): lax.all_to_all(activations, 'row', split_axis=1, concat_axis=0, tiled=True)  17.6 us
    all_gather x1, waiting for transfers between devices, shards(): lax.all_gather(row_piece, 'col', axis=0, tiled=True)  13.8 us
    unnamed x2, blocking collectives  13.5 us
    reduce_sum x1, other arithmetic, shards(): mean_col = jnp.sum(col_panel, axis=0, dtype=jnp.float32) / total  4.03 us
  transfers between devices with their start and end apart: 2, of which 2 were waited for; matrix products, arithmetic and copies ran while one was open for 4% of the time, Pallas kernels for 0%

commit v1 on v0

v1 whole, which is shorter than its diff:
```python
import functools

import jax
import jax.numpy as jnp
from jax import lax
from jax.experimental import pallas as pl
from jax.experimental.pallas import tpu as pltpu
from jax.sharding import PartitionSpec as P

TENANTS = 64
LABELS = 2
LANES = 128
MIB = 1024 * 1024

COST = pl.CostEstimate(flops=0, bytes_accessed=0, transcendentals=0)

ANY = pl.BlockSpec(memory_space=pl.ANY)
WHOLE = pl.BlockSpec(memory_space=pltpu.VMEM)
SCALARS = pl.BlockSpec(memory_space=pltpu.SMEM)


def params(mib):
    return pltpu.CompilerParams(vmem_limit_bytes=mib * MIB)


def swap_rows(x, mask):
    return lax.ppermute(x, "row", [(i, i ^ mask) for i in range(lax.axis_size("row"))])


def swap_cols(x, mask):
    return lax.ppermute(x, "col", [(i, i ^ mask) for i in range(lax.axis_size("col"))])


def pair_cols(x, first):
    pairs = []
    for low in range(first, lax.axis_size("col") - 1, 2):
        pairs += [(low, low + 1), (low + 1, low)]
    return lax.ppermute(x, "col", pairs)


def place():
    row = lax.axis_index("row")
    return row // 2, row % 2, lax.axis_index("col")


def deal_kernel(chips, tenants, labels, features, *outs):
    local, total = features.shape
    chip, _, col = place()
    row_outs, col_outs = outs[:chips], outs[chips:]
    width = total // len(col_outs)
    token = lax.broadcasted_iota(jnp.int32, (local, LANES), 0)
    codes = jnp.zeros((local, LANES), jnp.int32)
    for index in range(local):
        codes = jnp.where(token == index, tenants[index] * LABELS + labels[index], codes)
    codes = codes.astype(jnp.float32).astype(jnp.bfloat16)
    for mask, out in enumerate(col_outs):
        start = pl.multiple_of((col ^ mask) * width, LANES)
        out[:, :width] = features[:, pl.ds(start, width)]
        out[:, width:] = codes
    for mask, out in enumerate(row_outs):
        block = out.shape[1]
        start = pl.multiple_of((chip ^ mask) * block, LANES)
        out[...] = features[:, pl.ds(start, block)]


def share_kernel(*refs):
    *parts, out = refs
    _, core, _ = place()
    width = out.shape[2]
    start = pl.multiple_of((1 - core) * width, LANES)
    for index, part in enumerate(parts):
        out[index] = part[:, pl.ds(start, width)]


def rows_kernel(parts, *refs):
    shared = refs[parts]
    _, core, _ = place()
    rows = 2 * shared.shape[1]
    for index in range(parts):
        start = 0
        for out in refs[parts + 1 :]:
            width = out.shape[1]
            begin = pl.multiple_of(core * shared.shape[2] + start, LANES)
            both = jnp.concatenate([refs[index][:, pl.ds(begin, width)], shared[index, :, pl.ds(start, width)]], axis=0)
            out[index * rows : (index + 1) * rows, :] = both
            start += width


def stack_kernel(*refs):
    *parts, out = refs
    for index, part in enumerate(parts):
        out[index] = part[...]


def column_kernel(chips, *refs):
    near, far = refs[:chips], refs[chips : 2 * chips]
    panel, mean, member = refs[2 * chips :]
    total, columns = panel.shape
    planes, local, _ = near[0].shape
    step = min(512, columns)
    ones = jnp.ones((16, total), jnp.bfloat16)
    lanes = lax.broadcasted_iota(jnp.int32, (2 * local, LANES), 1).astype(jnp.float32)
    for start in range(0, columns, step):
        span = pl.ds(start, step)
        for plane in range(planes):
            for chip in range(chips):
                both = jnp.concatenate([near[chip][plane, :, span], far[chip][plane, :, span]], axis=0)
                target = (plane * chips + chip) * 2 * local
                panel[target : target + 2 * local, span] = both
                if start == 0:
                    code = pl.ds(columns, LANES)
                    both = jnp.concatenate([near[chip][plane, :, code], far[chip][plane, :, code]], axis=0)
                    member[target : target + 2 * local, :] = (both.astype(jnp.float32) == lanes).astype(jnp.bfloat16)
        sums = jnp.dot(ones, panel[:, span], preferred_element_type=jnp.float32)
        mean[:, span] = sums[:8] / total


def gram_kernel(pairs, first, tile, *refs):
    planes = len(pairs)
    parts, refs = refs[: sum(pairs)], refs[sum(pairs) :]
    panel, mean, member = refs[:3]
    cov, cross, rows_ref, out_ref, cross_ref, in_sem, out_sem, cross_sem = refs[-8:]
    _, _, col = place()
    total, columns = panel.shape
    shard, width = parts[0].shape
    slice_width = cross_ref.shape[1]
    chunk = out_ref.shape[2]

    def load(part, plane):
        return pltpu.make_async_copy(part, rows_ref.at[pl.ds(plane * shard, shard), :], in_sem.at[plane])

    index = 0
    for plane, count in enumerate(pairs):
        if count == 1:
            load(parts[index], plane).start()
        else:
            inside = (col > 0) & (col < planes - 1)
            pl.when(inside)(load(parts[index], plane).start)
            pl.when(jnp.logical_not(inside))(load(parts[index + 1], plane).start)
        index += count
    for plane in range(planes):
        load(parts[0], plane).wait()

    ones = jnp.ones((total, LANES), jnp.bfloat16)
    across = (((0,), (0,)), ((), ()))
    slots = out_ref.shape[0]
    per_row = columns // chunk
    steps = width // tile * per_row

    def store(step):
        slot = step % slots
        target = cov.at[pl.ds(first + step // per_row * tile, tile), pl.ds(step % per_row * chunk, chunk)]
        return pltpu.make_async_copy(out_ref.at[slot], target, out_sem.at[slot])

    for step in range(steps):
        if step >= slots:
            store(step - slots).wait()
        if step % per_row == 0:
            index = step // per_row
            left = rows_ref[:, index * tile : (index + 1) * tile]
            row_mean = lax.dot_general(left, ones, across, preferred_element_type=jnp.float32)[:, :1] / total
            left = left.T
        span = pl.ds(step % per_row * chunk, chunk)
        gram = jnp.dot(left, panel[:, span], preferred_element_type=jnp.float32)
        out_ref[step % slots] = gram * (1.0 / total) - row_mean * mean[:1, span]
        store(step).start()

    begin = col * slice_width - first
    mine = (begin >= 0) & (begin < width)
    save = pltpu.make_async_copy(cross_ref, cross, cross_sem)

    @pl.when(mine)
    def _():
        features = rows_ref[:, pl.ds(pl.multiple_of(begin, LANES), slice_width)]
        sums = lax.dot_general(member[...], features, across, preferred_element_type=jnp.float32)
        counts = lax.dot_general(member[...], ones, across, preferred_element_type=jnp.float32)[:, :1]
        slice_mean = jnp.dot(jnp.ones((16, total), jnp.bfloat16), features, preferred_element_type=jnp.float32)[:1] / total
        groups = member.shape[1]
        cross_ref[...] = (groups / total) * (sums - counts * slice_mean)
        save.start()

    for step in range(max(0, steps - slots), steps):
        store(step).wait()
    pl.when(mine)(save.wait)


def gram(own, received, panel, mean, member, first, outs):
    total, columns = panel.shape
    shard, width = own.shape
    tile = min(256, width)
    chunk = min(1024, columns)
    groups = [(own,)] + [part if isinstance(part, tuple) else (part,) for part in received]
    parts = [part for group in groups for part in group]
    inputs = [*parts, panel, mean, member]
    specs = [ANY] * len(parts) + [WHOLE] * 3
    aliases = {}
    if first:
        aliases = {len(inputs): 0, len(inputs) + 1: 1}
        inputs += outs
        specs += [ANY] * 2
    cov, cross = outs
    return pl.pallas_call(
        functools.partial(gram_kernel, tuple(map(len, groups)), first, tile),
        out_shape=[jax.ShapeDtypeStruct(cov.shape, cov.dtype), jax.ShapeDtypeStruct(cross.shape, cross.dtype)],
        in_specs=specs,
        out_specs=[ANY, ANY],
        scratch_shapes=[
            pltpu.VMEM((total, width), jnp.bfloat16),
            pltpu.VMEM((6, tile, chunk), jnp.float32),
            pltpu.VMEM(cross.shape, jnp.float32),
            pltpu.SemaphoreType.DMA((len(groups),)),
            pltpu.SemaphoreType.DMA((6,)),
            pltpu.SemaphoreType.DMA,
        ],
        input_output_aliases=aliases,
        compiler_params=params(24),
        cost_estimate=COST,
    )(*inputs)


def kernel(body, shapes, inputs, specs=None, mib=8):
    return pl.pallas_call(
        body,
        out_shape=[jax.ShapeDtypeStruct(shape, dtype) for shape, dtype in shapes],
        in_specs=specs or [WHOLE] * len(inputs),
        out_specs=[WHOLE] * len(shapes),
        compiler_params=params(mib),
        cost_estimate=COST,
    )(*inputs)


def gather_line(pieces, shard):
    half = shard.shape[0] // 2
    with jax.named_scope("planes_far"):
        far = [swap_cols(piece, 2) for piece in pieces]
    with jax.named_scope("planes_near"):
        near = [swap_cols(piece, 1) for piece in pieces]
    with jax.named_scope("chips_near"):
        sides = [swap_rows(shard, 2), swap_rows(shard, 4)]
    outer, inner, last = [], [], []
    (far[0], near[0], first), sides = lax.optimization_barrier(((far[0], near[0], pieces[0]), sides))
    with jax.named_scope("planes_last"):
        outer.append(swap_cols(far[0], 1))
        inner.append(pair_cols(first, 1))
    with jax.named_scope("chips_far"):
        corner = [swap_rows(sides[1][:half], 2), swap_rows(sides[0][half:], 4)]
    with jax.named_scope("cores"):
        others = [swap_rows(part, 1) for part in (shard, *sides)]
    (far[1], near[1], second), corner = lax.optimization_barrier(((far[1], near[1], pieces[1]), corner))
    with jax.named_scope("planes_last"):
        outer.append(swap_cols(far[1], 1))
        inner.append(pair_cols(second, 1))
    corner = jnp.concatenate(corner, axis=0)
    with jax.named_scope("cores"):
        others.append(swap_rows(corner, 1))
    arrays = [[near[i], far[i], (inner[i], outer[i])] for i in range(2)]
    return arrays, [shard, *sides, corner], others


def gather(pieces, shard):
    chips = lax.axis_size("row") // 2
    planes = lax.axis_size("col")
    if chips == 4 and planes == 4:
        return gather_line(pieces, shard)
    arrays = [[swap_cols(piece, mask) for mask in range(1, planes)] for piece in pieces]
    shards = [shard] + [swap_rows(shard, 2 * mask) for mask in range(1, chips)]
    return arrays, shards, [swap_rows(part, 1) for part in shards]


def shards(activations, tenant_ids, concept_labels):
    local, width = activations.shape
    rows = lax.axis_size("row")
    planes = lax.axis_size("col")
    chips = rows // 2
    block = width // rows
    panel_width = width // planes
    total = local * rows * planes
    groups = TENANTS * LABELS
    half = jnp.bfloat16

    dealt = kernel(
        functools.partial(deal_kernel, chips),
        [((local, 2 * block), half)] * chips + [((local, panel_width + LANES), half)] * planes,
        [tenant_ids, concept_labels, activations],
        [SCALARS, SCALARS, WHOLE],
    )
    to_rows, to_cols = dealt[:chips], dealt[chips:]
    col_parts = [to_cols[0]] + [swap_cols(to_cols[mask], mask) for mask in range(1, planes)]
    row_parts = [to_rows[0]] + [swap_rows(to_rows[mask], 2 * mask) for mask in range(1, chips)]
    (shared,) = kernel(share_kernel, [((chips, local, block), half)], row_parts)
    shared = swap_rows(shared, 1)

    slice_width = block // planes
    cut = slice_width * (planes // 4)
    pieces = kernel(
        functools.partial(rows_kernel, chips),
        [((rows * local, cut), half), ((rows * local, block - cut), half)],
        [*row_parts, shared],
    )
    (col_shard,) = kernel(stack_kernel, [((planes, local, panel_width + LANES), half)], col_parts)
    *pieces, col_shard = lax.optimization_barrier((*pieces, col_shard))
    chains, near, far = gather(pieces, col_shard)
    panel, mean, member = kernel(
        functools.partial(column_kernel, chips),
        [((total, panel_width), half), ((8, panel_width), jnp.float32), ((total, groups), half)],
        [*near, *far],
        mib=24,
    )

    outs = (
        jax.ShapeDtypeStruct((block, panel_width), jnp.float32),
        jax.ShapeDtypeStruct((groups, slice_width), jnp.float32),
    )
    first = 0
    for piece, arrays in zip(pieces, chains):
        outs = gram(piece, arrays, panel, mean, member, first, outs)
        first += piece.shape[1]
    return tuple(outs)


def solution(mesh):
    placed = (P(("row", "col"), None), P(("row", "col")), P(("row", "col")))
    return jax.shard_map(
        shards,
        mesh=mesh,
        in_specs=placed,
        out_specs=(P("row", "col"), P(None, ("row", "col"))),
        check_vma=False,
    )
```

time: 180 us -> 122 us (0.68)
  blocking collectives: 76.3 us -> 0 us
  starting transfers between devices: 0.08 us -> 27.2 us
  Pallas kernels: 0 us -> 23.9 us
  matrix products: 21.9 us -> 0 us
  between operations: 15.4 us -> 0.94 us
  waiting for transfers between devices: 54.4 us -> 67.4 us
  other arithmetic: 6.71 us -> 0 us
  local copies, waits for them, and re-layouts: 4.39 us -> 2.56 us
    ppermute x0 -> x23, waiting for transfers between devices: none -> 67.4 us  [the longest x9 56.2 us: swap_cols(): lax.ppermute(x, 'col', [(i, i ^ mask) for i in range(lax.axis_size('col'))])]
    all_to_all x2 -> x0, blocking collectives: 62.8 us -> none  [the longest x1 45.1 us: shards(): lax.all_to_all(activations, 'col', split_axis=1, concat_axis=0, tiled=True)]
    all_gather x2 -> x0, waiting for transfers between devices: 54.4 us -> none  [the longest x1 40.6 us: shards(): col_panel = lax.all_gather(col_piece, 'row', axis=0, tiled=True)]
    ppermute x0 -> x23, starting transfers between devices: none -> 27.2 us  [the longest x9 16.7 us: swap_cols(): lax.ppermute(x, 'col', [(i, i ^ mask) for i in range(lax.axis_size('col'))])]
    pallas_call x0 -> x7, Pallas kernels: none -> 23.9 us  [the longest x2 22 us: gram(): pl.pallas_call(functools.partial(gram_kernel, tuple(map(len, groups)), fi...]
    dot_general x2 -> x0, matrix products: 21.9 us -> none  [the longest x1 19.5 us: shards(): jnp.einsum('abtf,batg->fg', row_view, col_view, preferred_element_type=jn...]
    unnamed x2 -> x0, blocking collectives: 13.5 us -> none
    reduce_sum x3 -> x0, other arithmetic: 6.6 us -> none  [the longest x1 4.03 us: shards(): mean_col = jnp.sum(col_panel, axis=0, dtype=jnp.float32) / total]
  transfers between devices with their start and end apart: 2 -> 23, of which waited for: 2 -> 11; matrix products, arithmetic and copies ran while one was open for 4% -> 0% of each run, Pallas kernels for 0% -> 6%
where the time goes in v1:
time: 122 us
  waiting for transfers between devices  67.4 us (55%)
  starting transfers between devices  27.2 us (22%)
  Pallas kernels  23.9 us (20%)
  local copies, waits for them, and re-layouts  2.56 us (2%)
    ppermute x9, waiting for transfers between devices, swap_cols(): lax.ppermute(x, 'col', [(i, i ^ mask) for i in range(lax.axis_size('col'))])  56.2 us
    pallas_call x2, Pallas kernels, gram(): pl.pallas_call(functools.partial(gram_kernel, tuple(map(len, groups)), fi...  22 us
    ppermute x9, starting transfers between devices, swap_cols(): lax.ppermute(x, 'col', [(i, i ^ mask) for i in range(lax.axis_size('col'))])  16.7 us
    ppermute x12, waiting for transfers between devices, swap_rows(): lax.ppermute(x, 'row', [(i, i ^ mask) for i in range(lax.axis_size('row'))])  11.1 us
    ppermute x12, starting transfers between devices, swap_rows(): lax.ppermute(x, 'row', [(i, i ^ mask) for i in range(lax.axis_size('row'))])  9.11 us
    unnamed x7, local copies, waits for them, and re-layouts  2.47 us
  transfers between devices with their start and end apart: 23, of which 11 were waited for; matrix products, arithmetic and copies ran while one was open for 0% of the time, Pallas kernels for 6%

profile of v1, /device:TPU:0, one launch (start us, length us, event | category | flops | bytes accessed | tf_op | source)
XLA Modules:
  0.0 121.9 jit_solution(1976267551283410176)
XLA Ops:
  0.6 1.1 copy-done
  1.8 0.7 copy-done.1
  2.4 0.7 copy-done.2
  3.1 0.7 shard_map.50
  3.7 3.0 %collective-permute-start = (bf16[24,4096]{1,0:T(8,128)(2,1)S(1)}, bf16[24,4096]{1,0:T(8,128)(2,1)S(1)}, u32[]{:S(2)}, u32[]{:S(2)}) collective-permute-start(bf16[24,4096]{1,0:T(8,128)(2,1)S(1)} %get-tuple-element.31), channel_id=1, source_target_pairs={{0,8},{4,12},{8,0},{12,4},{16,24},{20,28},{24,16},{28,20},{1,9},{5... | collective-permute-start | bytes 589832 | tf_op jit(solution)/shard_map/ppermute | solution.py:27
  6.7 1.5 %collective-permute-start.1 = (bf16[24,4096]{1,0:T(8,128)(2,1)S(1)}, bf16[24,4096]{1,0:T(8,128)(2,1)S(1)}, u32[]{:S(2)}, u32[]{:S(2)}) collective-permute-start(bf16[24,4096]{1,0:T(8,128)(2,1)S(1)} %get-tuple-element.32), channel_id=1, source_target_pairs={{0,16},{4,20},{8,24},{12,28},{16,0},{20,4},{24,8},{28,12},{1,17},{... | collective-permute-start | bytes 589832 | tf_op jit(solution)/shard_map/ppermute | solution.py:27
  8.3 4.2 %collective-permute-done.refs_1_ = bf16[24,4096]{1,0:T(8,128)(2,1)S(1)} collective-permute-done((bf16[24,4096]{1,0:T(8,128)(2,1)S(1)}, bf16[24,4096]{1,0:T(8,128)(2,1)S(1)}, u32[]{:S(2)}, u32[]{:S(2)}) %collective-permute-start) | collective-permute-done | bytes 196640 | tf_op jit(solution)/shard_map/ppermute | solution.py:27
  12.5 4.8 %collective-permute-done.1.refs_2_ = bf16[24,4096]{1,0:T(8,128)(2,1)S(1)} collective-permute-done((bf16[24,4096]{1,0:T(8,128)(2,1)S(1)}, bf16[24,4096]{1,0:T(8,128)(2,1)S(1)}, u32[]{:S(2)}, u32[]{:S(2)}) %collective-permute-start.1) | collective-permute-done | bytes 196640 | tf_op jit(solution)/shard_map/ppermute | solution.py:27
  17.4 1.6 %collective-permute-start.4 = (bf16[24,4224]{1,0:T(8,128)(2,1)S(1)}, bf16[24,4224]{1,0:T(8,128)(2,1)S(1)}, u32[]{:S(2)}, u32[]{:S(2)}) collective-permute-start(bf16[24,4224]{1,0:T(8,128)(2,1)S(1)} %get-tuple-element.37), channel_id=1, source_target_pairs={{0,1},{1,0},{2,3},{3,2},{4,5},{5,4},{6,7},{7,6},{8,9},{9,8},{10,11... | collective-permute-start | bytes 608264 | tf_op jit(solution)/shard_map/ppermute | solution.py:31
  19.1 2.6 %collective-permute-start.5 = (bf16[24,4224]{1,0:T(8,128)(2,1)S(1)}, bf16[24,4224]{1,0:T(8,128)(2,1)S(1)}, u32[]{:S(2)}, u32[]{:S(2)}) collective-permute-start(bf16[24,4224]{1,0:T(8,128)(2,1)S(1)} %get-tuple-element.38), channel_id=1, source_target_pairs={{0,2},{1,3},{2,0},{3,1},{4,6},{5,7},{6,4},{7,5},{8,10},{9,11},{10,... | collective-permute-start | bytes 608264 | tf_op jit(solution)/shard_map/ppermute | solution.py:31
  21.9 6.9 %collective-permute-done.4.refs_1_ = bf16[24,4224]{1,0:T(8,128)(2,1)S(1)} collective-permute-done((bf16[24,4224]{1,0:T(8,128)(2,1)S(1)}, bf16[24,4224]{1,0:T(8,128)(2,1)S(1)}, u32[]{:S(2)}, u32[]{:S(2)}) %collective-permute-start.4) | collective-permute-done | bytes 202784 | tf_op jit(solution)/shard_map/ppermute | solution.py:31
  28.8 7.8 %collective-permute-done.5.refs_2_ = bf16[24,4224]{1,0:T(8,128)(2,1)S(1)} collective-permute-done((bf16[24,4224]{1,0:T(8,128)(2,1)S(1)}, bf16[24,4224]{1,0:T(8,128)(2,1)S(1)}, u32[]{:S(2)}, u32[]{:S(2)}) %collective-permute-start.5) | collective-permute-done | bytes 202784 | tf_op jit(solution)/shard_map/ppermute | solution.py:31
  36.7 1.6 %collective-permute-start.12 = (bf16[4,24,4224]{2,1,0:T(8,128)(2,1)S(1)}, bf16[4,24,4224]{2,1,0:T(8,128)(2,1)S(1)}, u32[]{:S(2)}, u32[]{:S(2)}) collective-permute-start(bf16[4,24,4224]{2,1,0:T(8,128)(2,1)S(1)} %shard_map.53.refs_0_), channel_id=1, source_target_pairs={{0,16},{4,20},{8,24},{12,28},{16,0},{20,4},{24,8},{28,12},{1,17},{... | collective-permute-start | bytes 2433032 | tf_op jit(solution)/shard_map/chips_near/ppermute | solution.py:27
  38.9 4.1 %collective-permute-start.10 = (bf16[192,512]{1,0:T(8,128)(2,1)S(1)}, bf16[192,512]{1,0:T(8,128)(2,1)S(1)}, u32[]{:S(2)}, u32[]{:S(2)}) collective-permute-start(bf16[192,512]{1,0:T(8,128)(2,1)S(1)} %get-tuple-element.55.refs_0_), channel_id=1, source_target_pairs={{0,1},{1,0},{2,3},{3,2},{4,5},{5,4},{6,7},{7,6},{8,9},{9,8},{10,11... | collective-permute-start | bytes 589832 | tf_op jit(solution)/shard_map/planes_near/ppermute | solution.py:31
  43.0 1.0 collective-permute-start.9
  44.0 2.0 %collective-permute-start.8 = (bf16[192,1536]{1,0:T(8,128)(2,1)S(1)}, bf16[192,1536]{1,0:T(8,128)(2,1)S(1)}, u32[]{:S(2)}, u32[]{:S(2)}) collective-permute-start(bf16[192,1536]{1,0:T(8,128)(2,1)S(1)} %get-tuple-element.47.refs_0_), channel_id=1, source_target_pairs={{0,1},{1,0},{2,3},{3,2},{4,5},{5,4},{6,7},{7,6},{8,9},{9,8},{10,11... | collective-permute-start | bytes 1769480 | tf_op jit(solution)/shard_map/planes_near/ppermute | solution.py:31
  46.0 8.3 %collective-permute-done.10.refs_1_ = bf16[192,512]{1,0:T(8,128)(2,1)S(1)} collective-permute-done((bf16[192,512]{1,0:T(8,128)(2,1)S(1)}, bf16[192,512]{1,0:T(8,128)(2,1)S(1)}, u32[]{:S(2)}, u32[]{:S(2)}) %collective-permute-start.10) | collective-permute-done | bytes 196640 | tf_op jit(solution)/shard_map/planes_near/ppermute | solution.py:31
  54.7 0.8 collective-permute-done.12.refs_2_
  55.5 1.2 %collective-permute-done.11.refs_1_ = bf16[4,24,4224]{2,1,0:T(8,128)(2,1)S(1)} collective-permute-done((bf16[4,24,4224]{2,1,0:T(8,128)(2,1)S(1)}, bf16[4,24,4224]{2,1,0:T(8,128)(2,1)S(1)}, u32[]{:S(2)}, u32[]{:S(2)}) %collective-permute-start.11) | collective-permute-done | bytes 811040 | tf_op jit(solution)/shard_map/chips_near/ppermute | solution.py:27
  56.8 0.6 collective-permute-start.14
  57.4 1.2 %collective-permute-start.13 = (bf16[2,24,4224]{2,1,0:T(8,128)(2,1)S(1)}, bf16[2,24,4224]{2,1,0:T(8,128)(2,1)S(1)}, u32[]{:S(2)}, u32[]{:S(2)}) collective-permute-start(bf16[2,24,4224]{2,1,0:T(8,128)(2,1)S(1)} %slice.6), channel_id=1, source_target_pairs={{0,8},{4,12},{8,0},{12,4},{16,24},{20,28},{24,16},{28,20},{1,9},{5... | collective-permute-start | bytes 1216520 | tf_op jit(solution)/shard_map/chips_far/ppermute | solution.py:27
  58.6 17.6 %collective-permute-done.8.refs_1_ = bf16[192,1536]{1,0:T(8,128)(2,1)S(1)} collective-permute-done((bf16[192,1536]{1,0:T(8,128)(2,1)S(1)}, bf16[192,1536]{1,0:T(8,128)(2,1)S(1)}, u32[]{:S(2)}, u32[]{:S(2)}) %collective-permute-start.8) | collective-permute-done | bytes 589856 | tf_op jit(solution)/shard_map/planes_near/ppermute | solution.py:31
  76.2 2.5 %collective-permute-done.7.refs_2_ = bf16[192,1536]{1,0:T(8,128)(2,1)S(1)} collective-permute-done((bf16[192,1536]{1,0:T(8,128)(2,1)S(1)}, bf16[192,1536]{1,0:T(8,128)(2,1)S(1)}, u32[]{:S(2)}, u32[]{:S(2)}) %collective-permute-start.7) | collective-permute-done | bytes 589856 | tf_op jit(solution)/shard_map/planes_far/ppermute | solution.py:31
  78.8 0.6 collective-permute-start.20
  79.4 0.7 collective-permute-start.15
  80.1 2.2 %collective-permute-start.16 = (bf16[192,1536]{1,0:T(8,128)(2,1)S(1)}, bf16[192,1536]{1,0:T(8,128)(2,1)S(1)}, u32[]{:S(2)}, u32[]{:S(2)}) collective-permute-start(bf16[192,1536]{1,0:T(8,128)(2,1)S(1)} %collective-permute-done.7.refs_2_), channel_id=1, source_target_pairs={{0,1},{1,0},{2,3},{3,2},{4,5},{5,4},{6,7},{7,6},{8,9},{9,8},{10,11... | collective-permute-start | bytes 1769480 | tf_op jit(solution)/shard_map/planes_last/ppermute | solution.py:31
  82.3 0.7 collective-permute-start.21
  83.0 2.9 %collective-permute-start.22 = (bf16[192,512]{1,0:T(8,128)(2,1)S(1)}, bf16[192,512]{1,0:T(8,128)(2,1)S(1)}, u32[]{:S(2)}, u32[]{:S(2)}) collective-permute-start(bf16[192,512]{1,0:T(8,128)(2,1)S(1)} %collective-permute-done.9.refs_2_), channel_id=1, source_target_pairs={{0,1},{1,0},{2,3},{3,2},{4,5},{5,4},{6,7},{7,6},{8,9},{9,8},{10,11... | collective-permute-start | bytes 589832 | tf_op jit(solution)/shard_map/planes_last/ppermute | solution.py:31
  85.9 1.1 shard_map.54
  87.0 12.8 %collective-permute-done.22.refs_4_ = bf16[192,512]{1,0:T(8,128)(2,1)S(1)} collective-permute-done((bf16[192,512]{1,0:T(8,128)(2,1)S(1)}, bf16[192,512]{1,0:T(8,128)(2,1)S(1)}, u32[]{:S(2)}, u32[]{:S(2)}) %collective-permute-start.22) | collective-permute-done | bytes 196640 | tf_op jit(solution)/shard_map/planes_last/ppermute | solution.py:31
  99.7 6.3 %shard_map.55 = (f32[2048,4096]{1,0:T(8,128)}, f32[128,512]{1,0:T(8,128)}) custom-call(bf16[192,512]{1,0:T(8,128)(2,1)S(1)} %get-tuple-element.55.refs_0_, bf16[192,512]{1,0:T(8,128)(2,1)S(1)} %collective-permute-done.10.refs_1_, bf16[192,512]{1,0:T(8,128)(2,1)S(1)} %collective-permute-done.9.refs_2_, bf16[192,512]{1,0:T(8,128)(2,1)S(1)} %collective-permute-done.21.refs_3_, ...), custom_call_target="tpu_custom_call" | custom-call | tf_op jit(solution)/shard_map/pallas_call | solution.py:202
  106.0 15.7 %shard_map.56 = (f32[2048,4096]{1,0:T(8,128)}, f32[128,512]{1,0:T(8,128)}) custom-call(bf16[192,1536]{1,0:T(8,128)(2,1)S(1)} %get-tuple-element.47.refs_0_, bf16[192,1536]{1,0:T(8,128)(2,1)S(1)} %collective-permute-done.8.refs_1_, bf16[192,1536]{1,0:T(8,128)(2,1)S(1)} %collective-permute-done.7.refs_2_, ...), custom_call_target="tpu_custom_call", output_to_operand_aliasing={{0}: (8, {}), {1}: (9, {})} | custom-call | tf_op jit(solution)/shard_map/pallas_call | solution.py:202
  (31 shorter events, 1.5 us)
Async XLA Ops:
  0.6 1.1 copy-start
  1.8 0.7 copy-start.1
  2.4 0.7 copy-start.2
  3.7 8.7 %collective-permute-start = (bf16[24,4096]{1,0:T(8,128)(2,1)S(1)}, bf16[24,4096]{1,0:T(8,128)(2,1)S(1)}, u32[]{:S(2)}, u32[]{:S(2)}) collective-permute-start(bf16[24,4096]{1,0:T(8,128)(2,1)S(1)} %get-tuple-element.31), channel_id=1, source_target_pairs={{0,8},{4,12},{8,0},{12,4},{16,24},{20,28},{24,16},{28,20},{1,9},{5... | collective-permute-start | bytes 589832 | tf_op jit(solution)/shard_map/ppermute | solution.py:27
  6.7 10.6 %collective-permute-start.1 = (bf16[24,4096]{1,0:T(8,128)(2,1)S(1)}, bf16[24,4096]{1,0:T(8,128)(2,1)S(1)}, u32[]{:S(2)}, u32[]{:S(2)}) collective-permute-start(bf16[24,4096]{1,0:T(8,128)(2,1)S(1)} %get-tuple-element.32), channel_id=1, source_target_pairs={{0,16},{4,20},{8,24},{12,28},{16,0},{20,4},{24,8},{28,12},{1,17},{... | collective-permute-start | bytes 589832 | tf_op jit(solution)/shard_map/ppermute | solution.py:27
  8.3 9.1 %collective-permute-start.2 = (bf16[24,4096]{1,0:T(8,128)(2,1)S(1)}, bf16[24,4096]{1,0:T(8,128)(2,1)S(1)}, u32[]{:S(2)}, u32[]{:S(2)}) collective-permute-start(bf16[24,4096]{1,0:T(8,128)(2,1)S(1)} %get-tuple-element.33), channel_id=1, source_target_pairs={{0,24},{4,28},{8,16},{12,20},{16,8},{20,12},{24,0},{28,4},{1,25},{... | collective-permute-start | bytes 589832 | tf_op jit(solution)/shard_map/ppermute | solution.py:27
  17.4 19.3 %collective-permute-start.3 = (bf16[4,24,2048]{2,1,0:T(8,128)(2,1)S(1)}, bf16[4,24,2048]{2,1,0:T(8,128)(2,1)S(1)}, u32[]{:S(2)}, u32[]{:S(2)}) collective-permute-start(bf16[4,24,2048]{2,1,0:T(8,128)(2,1)S(1)} %shard_map.51), channel_id=1, source_target_pairs={{0,4},{4,0},{8,12},{12,8},{16,20},{20,16},{24,28},{28,24},{1,5},{5... | collective-permute-start | bytes 1179656 | tf_op jit(solution)/shard_map/ppermute | solution.py:27
  17.4 11.3 %collective-permute-start.4 = (bf16[24,4224]{1,0:T(8,128)(2,1)S(1)}, bf16[24,4224]{1,0:T(8,128)(2,1)S(1)}, u32[]{:S(2)}, u32[]{:S(2)}) collective-permute-start(bf16[24,4224]{1,0:T(8,128)(2,1)S(1)} %get-tuple-element.37), channel_id=1, source_target_pairs={{0,1},{1,0},{2,3},{3,2},{4,5},{5,4},{6,7},{7,6},{8,9},{9,8},{10,11... | collective-permute-start | bytes 608264 | tf_op jit(solution)/shard_map/ppermute | solution.py:31
  19.1 17.5 %collective-permute-start.5 = (bf16[24,4224]{1,0:T(8,128)(2,1)S(1)}, bf16[24,4224]{1,0:T(8,128)(2,1)S(1)}, u32[]{:S(2)}, u32[]{:S(2)}) collective-permute-start(bf16[24,4224]{1,0:T(8,128)(2,1)S(1)} %get-tuple-element.38), channel_id=1, source_target_pairs={{0,2},{1,3},{2,0},{3,1},{4,6},{5,7},{6,4},{7,5},{8,10},{9,11},{10,... | collective-permute-start | bytes 608264 | tf_op jit(solution)/shard_map/ppermute | solution.py:31
  21.7 14.9 %collective-permute-start.6 = (bf16[24,4224]{1,0:T(8,128)(2,1)S(1)}, bf16[24,4224]{1,0:T(8,128)(2,1)S(1)}, u32[]{:S(2)}, u32[]{:S(2)}) collective-permute-start(bf16[24,4224]{1,0:T(8,128)(2,1)S(1)} %get-tuple-element.39), channel_id=1, source_target_pairs={{0,3},{1,2},{2,1},{3,0},{4,7},{5,6},{6,5},{7,4},{8,11},{9,10},{10,... | collective-permute-start | bytes 608264 | tf_op jit(solution)/shard_map/ppermute | solution.py:31
  36.7 18.8 %collective-permute-start.12 = (bf16[4,24,4224]{2,1,0:T(8,128)(2,1)S(1)}, bf16[4,24,4224]{2,1,0:T(8,128)(2,1)S(1)}, u32[]{:S(2)}, u32[]{:S(2)}) collective-permute-start(bf16[4,24,4224]{2,1,0:T(8,128)(2,1)S(1)} %shard_map.53.refs_0_), channel_id=1, source_target_pairs={{0,16},{4,20},{8,24},{12,28},{16,0},{20,4},{24,8},{28,12},{1,17},{... | collective-permute-start | bytes 2433032 | tf_op jit(solution)/shard_map/chips_near/ppermute | solution.py:27
  38.3 18.4 %collective-permute-start.11 = (bf16[4,24,4224]{2,1,0:T(8,128)(2,1)S(1)}, bf16[4,24,4224]{2,1,0:T(8,128)(2,1)S(1)}, u32[]{:S(2)}, u32[]{:S(2)}) collective-permute-start(bf16[4,24,4224]{2,1,0:T(8,128)(2,1)S(1)} %shard_map.53.refs_0_), channel_id=1, source_target_pairs={{0,8},{4,12},{8,0},{12,4},{16,24},{20,28},{24,16},{28,20},{1,9},{5... | collective-permute-start | bytes 2433032 | tf_op jit(solution)/shard_map/chips_near/ppermute | solution.py:27
  38.9 15.4 %collective-permute-start.10 = (bf16[192,512]{1,0:T(8,128)(2,1)S(1)}, bf16[192,512]{1,0:T(8,128)(2,1)S(1)}, u32[]{:S(2)}, u32[]{:S(2)}) collective-permute-start(bf16[192,512]{1,0:T(8,128)(2,1)S(1)} %get-tuple-element.55.refs_0_), channel_id=1, source_target_pairs={{0,1},{1,0},{2,3},{3,2},{4,5},{5,4},{6,7},{7,6},{8,9},{9,8},{10,11... | collective-permute-start | bytes 589832 | tf_op jit(solution)/shard_map/planes_near/ppermute | solution.py:31
  43.0 11.7 %collective-permute-start.9 = (bf16[192,512]{1,0:T(8,128)(2,1)S(1)}, bf16[192,512]{1,0:T(8,128)(2,1)S(1)}, u32[]{:S(2)}, u32[]{:S(2)}) collective-permute-start(bf16[192,512]{1,0:T(8,128)(2,1)S(1)} %get-tuple-element.55.refs_0_), channel_id=1, source_target_pairs={{0,2},{1,3},{2,0},{3,1},{4,6},{5,7},{6,4},{7,5},{8,10},{9,11},{10,... | collective-permute-start | bytes 589832 | tf_op jit(solution)/shard_map/planes_far/ppermute | solution.py:31
  44.0 32.2 %collective-permute-start.8 = (bf16[192,1536]{1,0:T(8,128)(2,1)S(1)}, bf16[192,1536]{1,0:T(8,128)(2,1)S(1)}, u32[]{:S(2)}, u32[]{:S(2)}) collective-permute-start(bf16[192,1536]{1,0:T(8,128)(2,1)S(1)} %get-tuple-element.47.refs_0_), channel_id=1, source_target_pairs={{0,1},{1,0},{2,3},{3,2},{4,5},{5,4},{6,7},{7,6},{8,9},{9,8},{10,11... | collective-permute-start | bytes 1769480 | tf_op jit(solution)/shard_map/planes_near/ppermute | solution.py:31
  54.3 24.4 %collective-permute-start.7 = (bf16[192,1536]{1,0:T(8,128)(2,1)S(1)}, bf16[192,1536]{1,0:T(8,128)(2,1)S(1)}, u32[]{:S(2)}, u32[]{:S(2)}) collective-permute-start(bf16[192,1536]{1,0:T(8,128)(2,1)S(1)} %get-tuple-element.47.refs_0_), channel_id=1, source_target_pairs={{0,2},{1,3},{2,0},{3,1},{4,6},{5,7},{6,4},{7,5},{8,10},{9,11},{10,... | collective-permute-start | bytes 1769480 | tf_op jit(solution)/shard_map/planes_far/ppermute | solution.py:31
  56.8 21.9 %collective-permute-start.14 = (bf16[2,24,4224]{2,1,0:T(8,128)(2,1)S(1)}, bf16[2,24,4224]{2,1,0:T(8,128)(2,1)S(1)}, u32[]{:S(2)}, u32[]{:S(2)}) collective-permute-start(bf16[2,24,4224]{2,1,0:T(8,128)(2,1)S(1)} %slice.7), channel_id=1, source_target_pairs={{0,16},{4,20},{8,24},{12,28},{16,0},{20,4},{24,8},{28,12},{1,17},{... | collective-permute-start | bytes 1216520 | tf_op jit(solution)/shard_map/chips_far/ppermute | solution.py:27
  57.4 21.4 %collective-permute-start.13 = (bf16[2,24,4224]{2,1,0:T(8,128)(2,1)S(1)}, bf16[2,24,4224]{2,1,0:T(8,128)(2,1)S(1)}, u32[]{:S(2)}, u32[]{:S(2)}) collective-permute-start(bf16[2,24,4224]{2,1,0:T(8,128)(2,1)S(1)} %slice.6), channel_id=1, source_target_pairs={{0,8},{4,12},{8,0},{12,4},{16,24},{20,28},{24,16},{28,20},{1,9},{5... | collective-permute-start | bytes 1216520 | tf_op jit(solution)/shard_map/chips_far/ppermute | solution.py:27
  58.6 21.5 %collective-permute-start.17 = (bf16[4,24,4224]{2,1,0:T(8,128)(2,1)S(1)}, bf16[4,24,4224]{2,1,0:T(8,128)(2,1)S(1)}, u32[]{:S(2)}, u32[]{:S(2)}) collective-permute-start(bf16[4,24,4224]{2,1,0:T(8,128)(2,1)S(1)} %shard_map.53.refs_0_), channel_id=1, source_target_pairs={{0,4},{4,0},{8,12},{12,8},{16,20},{20,16},{24,28},{28,24},{1,5},{5... | collective-permute-start | bytes 2433032 | tf_op jit(solution)/shard_map/cores/ppermute | solution.py:27
  76.2 6.1 %collective-permute-start.19 = (bf16[4,24,4224]{2,1,0:T(8,128)(2,1)S(1)}, bf16[4,24,4224]{2,1,0:T(8,128)(2,1)S(1)}, u32[]{:S(2)}, u32[]{:S(2)}) collective-permute-start(bf16[4,24,4224]{2,1,0:T(8,128)(2,1)S(1)} %collective-permute-done.12.refs_2_), channel_id=1, source_target_pairs={{0,4},{4,0},{8,12},{12,8},{16,20},{20,16},{24,28},{28,24},{1,5},{5... | collective-permute-start | bytes 2433032 | tf_op jit(solution)/shard_map/cores/ppermute | solution.py:27
  78.7 4.2 %collective-permute-start.18 = (bf16[4,24,4224]{2,1,0:T(8,128)(2,1)S(1)}, bf16[4,24,4224]{2,1,0:T(8,128)(2,1)S(1)}, u32[]{:S(2)}, u32[]{:S(2)}) collective-permute-start(bf16[4,24,4224]{2,1,0:T(8,128)(2,1)S(1)} %collective-permute-done.11.refs_1_), channel_id=1, source_target_pairs={{0,4},{4,0},{8,12},{12,8},{16,20},{20,16},{24,28},{28,24},{1,5},{5... | collective-permute-start | bytes 2433032 | tf_op jit(solution)/shard_map/cores/ppermute | solution.py:27
  78.8 7.0 %collective-permute-start.20 = (bf16[4,24,4224]{2,1,0:T(8,128)(2,1)S(1)}, bf16[4,24,4224]{2,1,0:T(8,128)(2,1)S(1)}, u32[]{:S(2)}, u32[]{:S(2)}) collective-permute-start(bf16[4,24,4224]{2,1,0:T(8,128)(2,1)S(1)} %constant_dynamic-update-slice_fusion.refs_3_), channel_id=1, source_target_pairs={{0,4},{4,0},{8,12},{12,8},{16,20},{20,16},{24,28},{28,24},{1,5},{5... | collective-permute-start | bytes 2433032 | tf_op jit(solution)/shard_map/cores/ppermute | solution.py:27
  79.4 26.6 %collective-permute-start.15 = (bf16[192,1536]{1,0:T(8,128)(2,1)S(1)}, bf16[192,1536]{1,0:T(8,128)(2,1)S(1)}, u32[]{:S(2)}, u32[]{:S(2)}) collective-permute-start(bf16[192,1536]{1,0:T(8,128)(2,1)S(1)} %get-tuple-element.47.refs_0_), channel_id=1, source_target_pairs={{1,2},{2,1},{5,6},{6,5},{9,10},{10,9},{13,14},{14,13},{17,18},{18,... | collective-permute-start | bytes 1769480 | tf_op jit(solution)/shard_map/planes_last/ppermute | solution.py:38
  80.1 25.9 %collective-permute-start.16 = (bf16[192,1536]{1,0:T(8,128)(2,1)S(1)}, bf16[192,1536]{1,0:T(8,128)(2,1)S(1)}, u32[]{:S(2)}, u32[]{:S(2)}) collective-permute-start(bf16[192,1536]{1,0:T(8,128)(2,1)S(1)} %collective-permute-done.7.refs_2_), channel_id=1, source_target_pairs={{0,1},{1,0},{2,3},{3,2},{4,5},{5,4},{6,7},{7,6},{8,9},{9,8},{10,11... | collective-permute-start | bytes 1769480 | tf_op jit(solution)/shard_map/planes_last/ppermute | solution.py:31
  82.3 4.7 %collective-permute-start.21 = (bf16[192,512]{1,0:T(8,128)(2,1)S(1)}, bf16[192,512]{1,0:T(8,128)(2,1)S(1)}, u32[]{:S(2)}, u32[]{:S(2)}) collective-permute-start(bf16[192,512]{1,0:T(8,128)(2,1)S(1)} %get-tuple-element.55.refs_0_), channel_id=1, source_target_pairs={{1,2},{2,1},{5,6},{6,5},{9,10},{10,9},{13,14},{14,13},{17,18},{18,... | collective-permute-start | bytes 589832 | tf_op jit(solution)/shard_map/planes_last/ppermute | solution.py:38
  83.0 16.8 %collective-permute-start.22 = (bf16[192,512]{1,0:T(8,128)(2,1)S(1)}, bf16[192,512]{1,0:T(8,128)(2,1)S(1)}, u32[]{:S(2)}, u32[]{:S(2)}) collective-permute-start(bf16[192,512]{1,0:T(8,128)(2,1)S(1)} %collective-permute-done.9.refs_2_), channel_id=1, source_target_pairs={{0,1},{1,0},{2,3},{3,2},{4,5},{5,4},{6,7},{7,6},{8,9},{9,8},{10,11... | collective-permute-start | bytes 589832 | tf_op jit(solution)/shard_map/planes_last/ppermute | solution.py:31

commit v2 on v1

v2 whole, which is shorter than its diff:
```python
import functools

import jax
import jax.numpy as jnp
from jax import lax
from jax.experimental import pallas as pl
from jax.experimental.pallas import tpu as pltpu
from jax.sharding import PartitionSpec as P

TENANTS = 64
LABELS = 2
LANES = 128
MIB = 1024 * 1024

COST = pl.CostEstimate(flops=0, bytes_accessed=0, transcendentals=0)

ANY = pl.BlockSpec(memory_space=pl.ANY)
WHOLE = pl.BlockSpec(memory_space=pltpu.VMEM)


def params(mib):
    return pltpu.CompilerParams(vmem_limit_bytes=mib * MIB)


def swap_rows(x, mask):
    return lax.ppermute(x, "row", [(i, i ^ mask) for i in range(lax.axis_size("row"))])


def swap_cols(x, mask):
    return lax.ppermute(x, "col", [(i, i ^ mask) for i in range(lax.axis_size("col"))])


def pair_cols(x, first):
    count = lax.axis_size("col")
    partner = {i: i for i in range(count)}
    for low in range(first, count - 1, 2):
        partner[low], partner[low + 1] = low + 1, low
    return lax.ppermute(x, "col", list(partner.items()))


def place():
    row = lax.axis_index("row")
    return row // 2, row % 2, lax.axis_index("col")


def deal_kernel(chips, tenants_hbm, labels_hbm, features_hbm, *refs):
    *outs, features, tenants, labels, sems = refs
    loads = [
        pltpu.make_async_copy(features_hbm, features, sems.at[0]),
        pltpu.make_async_copy(tenants_hbm, tenants, sems.at[1]),
        pltpu.make_async_copy(labels_hbm, labels, sems.at[2]),
    ]
    for load in loads:
        load.start()
    for load in loads:
        load.wait()
    local, total = features.shape
    chip, _, col = place()
    row_outs, col_outs = outs[:chips], outs[chips:]
    width = total // len(col_outs)
    token = lax.broadcasted_iota(jnp.int32, (local, LANES), 0)
    codes = jnp.zeros((local, LANES), jnp.int32)
    for index in range(local):
        codes = jnp.where(token == index, tenants[index] * LABELS + labels[index], codes)
    codes = codes.astype(jnp.float32).astype(jnp.bfloat16)
    for mask, out in enumerate(col_outs):
        start = pl.multiple_of((col ^ mask) * width, LANES)
        out[:, :width] = features[:, pl.ds(start, width)]
        out[:, width:] = codes
    for mask, out in enumerate(row_outs):
        block = out.shape[1]
        start = pl.multiple_of((chip ^ mask) * block, LANES)
        out[...] = features[:, pl.ds(start, block)]


def share_kernel(*refs):
    *parts, out = refs
    _, core, _ = place()
    width = out.shape[2]
    start = pl.multiple_of((1 - core) * width, LANES)
    for index, part in enumerate(parts):
        out[index] = part[:, pl.ds(start, width)]


def rows_kernel(*refs):
    *parts, shared, out = refs
    _, core, _ = place()
    local, width = shared.shape[1:]
    begin = pl.multiple_of(core * width, LANES)
    for index, part in enumerate(parts):
        both = jnp.concatenate([part[:, pl.ds(begin, width)], shared[index]], axis=0)
        out[index * 2 * local : (index + 1) * 2 * local, :] = both


def cut_kernel(arrays, *refs):
    outs = refs[arrays:]
    for index, array in enumerate(refs[:arrays]):
        start = 0
        for out in outs[index * len(outs) // arrays : (index + 1) * len(outs) // arrays]:
            out[...] = array[:, start : start + out.shape[1]]
            start += out.shape[1]


def stack_kernel(*refs):
    *parts, out = refs
    start = 0
    for part in parts:
        rows = part.shape[0]
        out[start : start + rows] = part[...]
        start += rows


def column_kernel(chips, *refs):
    near, far, panel, mean, member, counts = refs
    total, columns = panel.shape
    _, local, _ = near.shape
    planes = near.shape[0] // chips
    step = min(512, columns)
    ones = jnp.ones((16, total), jnp.bfloat16)
    lanes = lax.broadcasted_iota(jnp.int32, (2 * local, LANES), 1).astype(jnp.float32)
    for start in range(0, columns, step):
        span = pl.ds(start, step)
        for plane in range(planes):
            for chip in range(chips):
                both = jnp.concatenate([near[chip * planes + plane, :, span], far[chip * planes + plane, :, span]], axis=0)
                target = (plane * chips + chip) * 2 * local
                panel[target : target + 2 * local, span] = both
                if start == 0:
                    code = pl.ds(columns, LANES)
                    both = jnp.concatenate([near[chip * planes + plane, :, code], far[chip * planes + plane, :, code]], axis=0)
                    member[target : target + 2 * local, :] = (both.astype(jnp.float32) == lanes).astype(jnp.bfloat16)
        sums = jnp.dot(ones, panel[:, span], preferred_element_type=jnp.float32)
        mean[:, span] = sums[:8] / total
    ones = jnp.ones((total, LANES), jnp.bfloat16)
    counts[...] = lax.dot_general(member[...], ones, (((0,), (0,)), ((), ())), preferred_element_type=jnp.float32)


def gram_kernel(pairs, first, tile, *refs):
    parts, refs = refs[: sum(pairs)], refs[sum(pairs) :]
    panel, mean, member, counts = refs[:4]
    cov, cross, left_ref, out_ref, cross_ref, out_sem, cross_sem = refs[-7:]
    _, _, col = place()
    total, columns = panel.shape
    width = left_ref.shape[0]
    slice_width = cross_ref.shape[1]
    chunk = out_ref.shape[2]
    inside = (col > 0) & (col < len(pairs) - 1)

    def features(start, size):
        blocks, index = [], 0
        for count in pairs:
            both = []
            for part in parts[index : index + count]:
                offset = first if part.shape[1] > width else 0
                both.append(part[:, pl.ds(start + offset, size)])
            blocks.append(both[0] if count == 1 else jnp.where(inside, both[0], both[1]))
            index += count
        return jnp.concatenate(blocks, axis=0)

    slots = out_ref.shape[0]
    per_row = columns // chunk
    steps = width // tile * per_row

    def store(step):
        slot = step % slots
        target = cov.at[pl.ds(first + step // per_row * tile, tile), pl.ds(step % per_row * chunk, chunk)]
        return pltpu.make_async_copy(out_ref.at[slot], target, out_sem.at[slot])

    for start in range(0, width, tile):
        left_ref[start : start + tile, :] = features(start, tile).T
    ones = jnp.ones((total, LANES), jnp.bfloat16)
    for step in range(steps):
        if step >= slots:
            store(step - slots).wait()
        left = left_ref[pl.ds(step // per_row * tile, tile), :]
        if step % per_row == 0:
            row_mean = jnp.dot(left, ones, preferred_element_type=jnp.float32)[:, :1] / total
        span = pl.ds(step % per_row * chunk, chunk)
        gram = jnp.dot(left, panel[:, span], preferred_element_type=jnp.float32)
        out_ref[step % slots] = gram * (1.0 / total) - row_mean * mean[:1, span]
        store(step).start()

    begin = col * slice_width - first
    mine = (begin >= 0) & (begin < width)
    save = pltpu.make_async_copy(cross_ref, cross, cross_sem)

    @pl.when(mine)
    def _():
        own = features(pl.multiple_of(begin, LANES), slice_width)
        sums = lax.dot_general(member[...], own, (((0,), (0,)), ((), ())), preferred_element_type=jnp.float32)
        slice_mean = jnp.dot(jnp.ones((16, total), jnp.bfloat16), own, preferred_element_type=jnp.float32)[:1] / total
        groups = member.shape[1]
        cross_ref[...] = (groups / total) * (sums - counts[:, :1] * slice_mean)
        save.start()

    for step in range(max(0, steps - slots), steps):
        store(step).wait()
    pl.when(mine)(save.wait)


def gram(groups, panel, mean, member, counts, first, width, outs):
    total, columns = panel.shape
    tile = min(256, width)
    chunk = min(2048, columns)
    slots = min(8, width // tile * (columns // chunk))
    parts = [part for group in groups for part in group]
    inputs = [*parts, panel, mean, member, counts]
    specs = [WHOLE] * len(inputs)
    aliases = {}
    if first:
        aliases = {len(inputs): 0, len(inputs) + 1: 1}
        inputs += outs
        specs += [ANY] * 2
    cov, cross = outs
    return pl.pallas_call(
        functools.partial(gram_kernel, tuple(map(len, groups)), first, tile),
        out_shape=[jax.ShapeDtypeStruct(cov.shape, cov.dtype), jax.ShapeDtypeStruct(cross.shape, cross.dtype)],
        in_specs=specs,
        out_specs=[ANY, ANY],
        scratch_shapes=[
            pltpu.VMEM((width, total), jnp.bfloat16),
            pltpu.VMEM((slots, tile, chunk), jnp.float32),
            pltpu.VMEM(cross.shape, jnp.float32),
            pltpu.SemaphoreType.DMA((slots,)),
            pltpu.SemaphoreType.DMA,
        ],
        input_output_aliases=aliases,
        compiler_params=params(40),
        cost_estimate=pl.CostEstimate(flops=0, bytes_accessed=2 * MIB, transcendentals=0),
    )(*inputs)


def kernel(body, shapes, inputs, specs=None, mib=8, scratch=(), cost=COST):
    return pl.pallas_call(
        body,
        out_shape=[jax.ShapeDtypeStruct(shape, dtype) for shape, dtype in shapes],
        in_specs=specs or [WHOLE] * len(inputs),
        out_specs=[WHOLE] * len(shapes),
        scratch_shapes=scratch,
        compiler_params=params(mib),
        cost_estimate=cost,
    )(*inputs)


def gather_line(rows, shard, widths):
    with jax.named_scope("planes_far"):
        far = swap_cols(rows, 2)
    with jax.named_scope("planes_near"):
        near = swap_cols(rows, 1)
    with jax.named_scope("chips"):
        shards = [shard] + [swap_rows(shard, 2 * mask) for mask in (1, 2, 3)]
    shards, rows, near, far = lax.optimization_barrier((shards, rows, near, far))
    cuts = kernel(functools.partial(cut_kernel, 2), [((rows.shape[0], width), rows.dtype) for width in widths] * 2, [rows, far])
    (stacked,) = kernel(stack_kernel, [((4 * shard.shape[0], *shard.shape[1:]), shard.dtype)], shards)
    with jax.named_scope("cores"):
        other = swap_rows(stacked, 1)
    groups = []
    for index in range(len(widths)):
        own, passed = cuts[index :: len(widths)]
        with jax.named_scope("planes_last"):
            last = (pair_cols(own, 1), swap_cols(passed, 1))
        groups.append([(rows,), (near,), (far,), last])
    return groups, stacked, other


def gather(rows, shard, widths):
    chips = lax.axis_size("row") // 2
    planes = lax.axis_size("col")
    if chips == 4 and planes == 4:
        return gather_line(rows, shard, widths)
    arrays = [(rows,)] + [(swap_cols(rows, mask),) for mask in range(1, planes)]
    shards = [shard] + [swap_rows(shard, 2 * mask) for mask in range(1, chips)]
    (stacked,) = kernel(stack_kernel, [((chips * shard.shape[0], *shard.shape[1:]), shard.dtype)], shards, mib=40)
    return [arrays] * len(widths), stacked, swap_rows(stacked, 1)


def shards(activations, tenant_ids, concept_labels):
    local, width = activations.shape
    rows = lax.axis_size("row")
    planes = lax.axis_size("col")
    chips = rows // 2
    block = width // rows
    panel_width = width // planes
    total = local * rows * planes
    groups = TENANTS * LABELS
    half = jnp.bfloat16

    dealt = kernel(
        functools.partial(deal_kernel, chips),
        [((local, 2 * block), half)] * chips + [((local, panel_width + LANES), half)] * planes,
        [tenant_ids, concept_labels, activations],
        [ANY, ANY, ANY],
        scratch=[
            pltpu.VMEM((local, width), half),
            pltpu.SMEM((local,), jnp.int32),
            pltpu.SMEM((local,), jnp.int32),
            pltpu.SemaphoreType.DMA((3,)),
        ],
    )
    to_rows, to_cols = dealt[:chips], dealt[chips:]
    col_parts = [to_cols[0]] + [swap_cols(to_cols[mask], mask) for mask in range(1, planes)]
    row_parts = [to_rows[0]] + [swap_rows(to_rows[mask], 2 * mask) for mask in range(1, chips)]
    row_parts, col_parts = lax.optimization_barrier((row_parts, col_parts))
    (shared,) = kernel(share_kernel, [((chips, local, block), half)], row_parts)
    shared = swap_rows(shared, 1)

    slice_width = block // planes
    cut = slice_width * (planes // 2)
    widths = (cut, block - cut)
    (row_shard,) = kernel(rows_kernel, [((rows * local, block), half)], [*row_parts, shared])
    shard_shape = (planes, local, panel_width + LANES)
    col_parts = [part.reshape(1, *part.shape) for part in col_parts]
    (col_shard,) = kernel(stack_kernel, [(shard_shape, half)], col_parts)

    pieces, near, far = gather(row_shard, col_shard, widths)
    panel, mean, member, counts = kernel(
        functools.partial(column_kernel, chips),
        [((total, panel_width), half), ((8, panel_width), jnp.float32), ((total, groups), half), ((groups, LANES), jnp.float32)],
        [near, far],
        mib=40,
    )

    outs = (
        jax.ShapeDtypeStruct((block, panel_width), jnp.float32),
        jax.ShapeDtypeStruct((groups, slice_width), jnp.float32),
    )
    first = 0
    for piece, piece_width in zip(pieces, widths):
        outs = gram(piece, panel, mean, member, counts, first, piece_width, outs)
        first += piece_width
    return tuple(outs)


def solution(mesh):
    placed = (P(("row", "col"), None), P(("row", "col")), P(("row", "col")))
    return jax.shard_map(
        shards,
        mesh=mesh,
        in_specs=placed,
        out_specs=(P("row", "col"), P(None, ("row", "col"))),
        check_vma=False,
    )
```

time: 122 us -> 101 us (0.83)
  waiting for transfers between devices: 67.4 us -> 51.2 us
  Pallas kernels: 23.9 us -> 19.7 us
    ppermute x9 -> x7, waiting for transfers between devices: 56.2 us -> 13.6 us  [swap_cols(): lax.ppermute(x, 'col', [(i, i ^ mask) for i in range(lax.axis_size('col'))])]
    ppermute x12 -> x8, waiting for transfers between devices: 11.1 us -> 37.6 us  [swap_rows(): lax.ppermute(x, 'row', [(i, i ^ mask) for i in range(lax.axis_size('row'))])]
    pallas_call x2, Pallas kernels: 22 us -> 17.4 us  [gram(): pl.pallas_call(functools.partial(gram_kernel, tuple(map(len, groups)), fi...]
    ppermute x9 -> x7, starting transfers between devices: 16.7 us -> 14.8 us  [swap_cols(): lax.ppermute(x, 'col', [(i, i ^ mask) for i in range(lax.axis_size('col'))])]
    ppermute x12 -> x8, starting transfers between devices: 9.11 us -> 9.9 us  [swap_rows(): lax.ppermute(x, 'row', [(i, i ^ mask) for i in range(lax.axis_size('row'))])]
    unnamed x7 -> x6, local copies, waits for them, and re-layouts: 2.47 us -> 2.44 us
  transfers between devices with their start and end apart: 23 -> 17, of which waited for: 11 -> 8; matrix products, arithmetic and copies ran while one was open for 0% -> 0% of each run, Pallas kernels for 6% -> 10%
where the time goes in v2:
time: 101 us; the launch traced here: 100 us
  waiting for transfers between devices  51.2 us (51%)
  starting transfers between devices  26 us (26%)
  Pallas kernels  19.7 us (20%)
  local copies, waits for them, and re-layouts  2.44 us (2%)
    ppermute x8, waiting for transfers between devices, swap_rows(): lax.ppermute(x, 'row', [(i, i ^ mask) for i in range(lax.axis_size('row'))])  37.6 us
    pallas_call x2, Pallas kernels, gram(): pl.pallas_call(functools.partial(gram_kernel, tuple(map(len, groups)), fi...  17.4 us
    ppermute x7, starting transfers between devices, swap_cols(): lax.ppermute(x, 'col', [(i, i ^ mask) for i in range(lax.axis_size('col'))])  14.8 us
    ppermute x7, waiting for transfers between devices, swap_cols(): lax.ppermute(x, 'col', [(i, i ^ mask) for i in range(lax.axis_size('col'))])  13.6 us
    ppermute x8, starting transfers between devices, swap_rows(): lax.ppermute(x, 'row', [(i, i ^ mask) for i in range(lax.axis_size('row'))])  9.9 us
    unnamed x6, local copies, waits for them, and re-layouts  2.44 us
    pallas_call x7, Pallas kernels, kernel(): pl.pallas_call(body, out_shape=[jax.ShapeDtypeStruct(shape, dtype) for sh...  2.35 us
  transfers between devices with their start and end apart: 17, of which 8 were waited for; matrix products, arithmetic and copies ran while one was open for 0% of the time, Pallas kernels for 10%

profile of v2, /device:TPU:0, one launch (start us, length us, event | category | flops | bytes accessed | tf_op | source)
XLA Modules:
  0.0 100.4 jit_solution(9241988126199747490)
XLA Ops:
  0.6 1.1 %copy-done = bf16[24,16384]{1,0:T(8,128)(2,1)S(1)} copy-done((bf16[24,16384]{1,0:T(8,128)(2,1)S(1)}, bf16[24,16384]{1,0:T(8,128)(2,1)}, u32[]{:S(2)}) %copy-start) | copy-done | bytes 786456
  1.8 0.7 copy-done.1
  2.4 0.7 copy-done.2
  3.1 0.7 shard_map.50
  3.8 3.0 %collective-permute-start = (bf16[24,4096]{1,0:T(8,128)(2,1)S(1)}, bf16[24,4096]{1,0:T(8,128)(2,1)S(1)}, u32[]{:S(2)}, u32[]{:S(2)}) collective-permute-start(bf16[24,4096]{1,0:T(8,128)(2,1)S(1)} %get-tuple-element.36), channel_id=1, source_target_pairs={{0,8},{4,12},{8,0},{12,4},{16,24},{20,28},{24,16},{28,20},{1,9},{5... | collective-permute-start | bytes 589832 | tf_op jit(solution)/shard_map/ppermute | solution.py:26
  6.8 1.6 %collective-permute-start.3 = (bf16[24,4224]{1,0:T(8,128)(2,1)S(1)}, bf16[24,4224]{1,0:T(8,128)(2,1)S(1)}, u32[]{:S(2)}, u32[]{:S(2)}) collective-permute-start(bf16[24,4224]{1,0:T(8,128)(2,1)S(1)} %get-tuple-element.40), channel_id=1, source_target_pairs={{0,1},{1,0},{2,3},{3,2},{4,5},{5,4},{6,7},{7,6},{8,9},{9,8},{10,11... | collective-permute-start | bytes 608264 | tf_op jit(solution)/shard_map/ppermute | solution.py:30
  8.4 2.6 %collective-permute-start.4 = (bf16[24,4224]{1,0:T(8,128)(2,1)S(1)}, bf16[24,4224]{1,0:T(8,128)(2,1)S(1)}, u32[]{:S(2)}, u32[]{:S(2)}) collective-permute-start(bf16[24,4224]{1,0:T(8,128)(2,1)S(1)} %get-tuple-element.41), channel_id=1, source_target_pairs={{0,2},{1,3},{2,0},{3,1},{4,6},{5,7},{6,4},{7,5},{8,10},{9,11},{10,... | collective-permute-start | bytes 608264 | tf_op jit(solution)/shard_map/ppermute | solution.py:30
  11.0 0.2 collective-permute-start.5
  11.2 1.5 %collective-permute-start.1 = (bf16[24,4096]{1,0:T(8,128)(2,1)S(1)}, bf16[24,4096]{1,0:T(8,128)(2,1)S(1)}, u32[]{:S(2)}, u32[]{:S(2)}) collective-permute-start(bf16[24,4096]{1,0:T(8,128)(2,1)S(1)} %get-tuple-element.37), channel_id=1, source_target_pairs={{0,16},{4,20},{8,24},{12,28},{16,0},{20,4},{24,8},{28,12},{1,17},{... | collective-permute-start | bytes 589832 | tf_op jit(solution)/shard_map/ppermute | solution.py:26
  12.7 1.7 %collective-permute-start.2 = (bf16[24,4096]{1,0:T(8,128)(2,1)S(1)}, bf16[24,4096]{1,0:T(8,128)(2,1)S(1)}, u32[]{:S(2)}, u32[]{:S(2)}) collective-permute-start(bf16[24,4096]{1,0:T(8,128)(2,1)S(1)} %get-tuple-element.38), channel_id=1, source_target_pairs={{0,24},{4,28},{8,16},{12,20},{16,8},{20,12},{24,0},{28,4},{1,25},{... | collective-permute-start | bytes 589832 | tf_op jit(solution)/shard_map/ppermute | solution.py:26
  14.4 6.6 %collective-permute-done.1.refs_2_ = bf16[24,4096]{1,0:T(8,128)(2,1)S(1)} collective-permute-done((bf16[24,4096]{1,0:T(8,128)(2,1)S(1)}, bf16[24,4096]{1,0:T(8,128)(2,1)S(1)}, u32[]{:S(2)}, u32[]{:S(2)}) %collective-permute-start.1) | collective-permute-done | bytes 196640 | tf_op jit(solution)/shard_map/ppermute | solution.py:26
  21.1 4.9 %collective-permute-done.4 = bf16[24,4224]{1,0:T(8,128)(2,1)S(1)} collective-permute-done((bf16[24,4224]{1,0:T(8,128)(2,1)S(1)}, bf16[24,4224]{1,0:T(8,128)(2,1)S(1)}, u32[]{:S(2)}, u32[]{:S(2)}) %collective-permute-start.4) | collective-permute-done | bytes 202784 | tf_op jit(solution)/shard_map/ppermute | solution.py:30
  26.0 0.1 collective-permute-start.9
  26.1 1.6 %collective-permute-start.8 = (bf16[4,24,4224]{2,1,0:T(8,128)(2,1)S(1)}, bf16[4,24,4224]{2,1,0:T(8,128)(2,1)S(1)}, u32[]{:S(2)}, u32[]{:S(2)}) collective-permute-start(bf16[4,24,4224]{2,1,0:T(8,128)(2,1)S(1)} %shard_map.51.refs_0_), channel_id=1, source_target_pairs={{0,24},{4,28},{8,16},{12,20},{16,8},{20,12},{24,0},{28,4},{1,25},{... | collective-permute-start | bytes 2433032 | tf_op jit(solution)/shard_map/chips/ppermute | solution.py:26
  27.7 0.5 collective-permute-start.7
  28.2 1.5 %collective-permute-start.6 = (bf16[4,24,4224]{2,1,0:T(8,128)(2,1)S(1)}, bf16[4,24,4224]{2,1,0:T(8,128)(2,1)S(1)}, u32[]{:S(2)}, u32[]{:S(2)}) collective-permute-start(bf16[4,24,4224]{2,1,0:T(8,128)(2,1)S(1)} %shard_map.51.refs_0_), channel_id=1, source_target_pairs={{0,8},{4,12},{8,0},{12,4},{16,24},{20,28},{24,16},{28,20},{1,9},{5... | collective-permute-start | bytes 2433032 | tf_op jit(solution)/shard_map/chips/ppermute | solution.py:26
  29.8 4.3 %collective-permute-start.11 = (bf16[192,2048]{1,0:T(8,128)(2,1)S(1)}, bf16[192,2048]{1,0:T(8,128)(2,1)S(1)}, u32[]{:S(2)}, u32[]{:S(2)}) collective-permute-start(bf16[192,2048]{1,0:T(8,128)(2,1)S(1)} %shard_map.53.refs_0_), channel_id=1, source_target_pairs={{0,2},{1,3},{2,0},{3,1},{4,6},{5,7},{6,4},{7,5},{8,10},{9,11},{10,... | collective-permute-start | bytes 2359304 | tf_op jit(solution)/shard_map/planes_far/ppermute | solution.py:30
  34.0 14.0 %collective-permute-done.8.refs_3_ = bf16[4,24,4224]{2,1,0:T(8,128)(2,1)S(1)} collective-permute-done((bf16[4,24,4224]{2,1,0:T(8,128)(2,1)S(1)}, bf16[4,24,4224]{2,1,0:T(8,128)(2,1)S(1)}, u32[]{:S(2)}, u32[]{:S(2)}) %collective-permute-start.8) | collective-permute-done | bytes 811040 | tf_op jit(solution)/shard_map/chips/ppermute | solution.py:26
  48.0 16.9 %collective-permute-done.7.refs_2_ = bf16[4,24,4224]{2,1,0:T(8,128)(2,1)S(1)} collective-permute-done((bf16[4,24,4224]{2,1,0:T(8,128)(2,1)S(1)}, bf16[4,24,4224]{2,1,0:T(8,128)(2,1)S(1)}, u32[]{:S(2)}, u32[]{:S(2)}) %collective-permute-start.7) | collective-permute-done | bytes 811040 | tf_op jit(solution)/shard_map/chips/ppermute | solution.py:26
  65.0 0.1 collective-permute-done.6.refs_1_
  65.1 3.3 %collective-permute-done.11.refs_1_.refs_2_ = bf16[192,2048]{1,0:T(8,128)(2,1)S(1)} collective-permute-done((bf16[192,2048]{1,0:T(8,128)(2,1)S(1)}, bf16[192,2048]{1,0:T(8,128)(2,1)S(1)}, u32[]{:S(2)}, u32[]{:S(2)}) %collective-permute-start.11) | collective-permute-done | bytes 786464 | tf_op jit(solution)/shard_map/planes_far/ppermute | solution.py:30
  68.4 0.2 collective-permute-done.10.refs_1_
  68.5 0.2 shard_map.55.refs_0_
  68.8 0.1 shard_map.54
  69.0 0.7 collective-permute-start.15
  69.7 3.2 %collective-permute-start.16 = (bf16[192,1024]{1,0:T(8,128)(2,1)S(1)}, bf16[192,1024]{1,0:T(8,128)(2,1)S(1)}, u32[]{:S(2)}, u32[]{:S(2)}) collective-permute-start(bf16[192,1024]{1,0:T(8,128)(2,1)S(1)} %get-tuple-element.65), channel_id=1, source_target_pairs={{0,1},{1,0},{2,3},{3,2},{4,5},{5,4},{6,7},{7,6},{8,9},{9,8},{10,11... | collective-permute-start | bytes 1179656 | tf_op jit(solution)/shard_map/planes_last/ppermute | solution.py:30
  72.9 0.7 collective-permute-start.12
  73.6 2.9 %collective-permute-start.13 = (bf16[192,1024]{1,0:T(8,128)(2,1)S(1)}, bf16[192,1024]{1,0:T(8,128)(2,1)S(1)}, u32[]{:S(2)}, u32[]{:S(2)}) collective-permute-start(bf16[192,1024]{1,0:T(8,128)(2,1)S(1)} %get-tuple-element.55), channel_id=1, source_target_pairs={{0,1},{1,0},{2,3},{3,2},{4,5},{5,4},{6,7},{7,6},{8,9},{9,8},{10,11... | collective-permute-start | bytes 1179656 | tf_op jit(solution)/shard_map/planes_last/ppermute | solution.py:30
  76.5 1.1 %shard_map.56 = (bf16[768,4096]{1,0:T(8,128)(2,1)S(1)}, f32[8,4096]{1,0:T(8,128)S(1)}, bf16[768,128]{1,0:T(8,128)(2,1)S(1)}, f32[128,128]{1,0:T(8,128)S(1)}) custom-call(bf16[16,24,4224]{2,1,0:T(8,128)(2,1)S(1)} %shard_map.55.refs_0_, bf16[16,24,4224]{2,1,0:T(8,128)(2,1)S(1)} %collective-permute-done.14.refs_1_), custom_call_target="tpu_custom_call" | custom-call | tf_op jit(solution)/shard_map/pallas_call | solution.py:234
  77.6 5.2 %collective-permute-done.16.refs_4_ = bf16[192,1024]{1,0:T(8,128)(2,1)S(1)} collective-permute-done((bf16[192,1024]{1,0:T(8,128)(2,1)S(1)}, bf16[192,1024]{1,0:T(8,128)(2,1)S(1)}, u32[]{:S(2)}, u32[]{:S(2)}) %collective-permute-start.16) | collective-permute-done | bytes 393248 | tf_op jit(solution)/shard_map/planes_last/ppermute | solution.py:30
  82.8 8.7 %shard_map.57 = (f32[2048,4096]{1,0:T(8,128)}, f32[128,512]{1,0:T(8,128)}) custom-call(bf16[192,2048]{1,0:T(8,128)(2,1)S(1)} %shard_map.53.refs_0_, bf16[192,2048]{1,0:T(8,128)(2,1)S(1)} %collective-permute-done.10.refs_1_, bf16[192,2048]{1,0:T(8,128)(2,1)S(1)} %collective-permute-done.11.refs_1_.refs_2_, ...), custom_call_target="tpu_custom_call" | custom-call | bytes 2097152 | tf_op jit(solution)/shard_map/pallas_call | solution.py:215
  91.5 8.7 %shard_map.58 = (f32[2048,4096]{1,0:T(8,128)}, f32[128,512]{1,0:T(8,128)}) custom-call(bf16[192,2048]{1,0:T(8,128)(2,1)S(1)} %shard_map.53.refs_0_, bf16[192,2048]{1,0:T(8,128)(2,1)S(1)} %collective-permute-done.10.refs_1_, bf16[192,2048]{1,0:T(8,128)(2,1)S(1)} %collective-permute-done.11.refs_1_.refs_2_, ...), custom_call_target="tpu_custom_call", output_to_operand_aliasing={{0}: (9, {}), {1}: (10, {})} | custom-call | bytes 2097152 | tf_op jit(solution)/shard_map/pallas_call | solution.py:215
  (17 shorter events, 0.3 us)
Async XLA Ops:
  0.6 1.1 %copy-start = (bf16[24,16384]{1,0:T(8,128)(2,1)S(1)}, bf16[24,16384]{1,0:T(8,128)(2,1)}, u32[]{:S(2)}) copy-start(bf16[24,16384]{1,0:T(8,128)(2,1)} %features_hbm.1) | copy-start | bytes 2359300
  1.8 0.7 copy-start.1
  2.4 0.7 copy-start.2
  3.8 8.9 %collective-permute-start = (bf16[24,4096]{1,0:T(8,128)(2,1)S(1)}, bf16[24,4096]{1,0:T(8,128)(2,1)S(1)}, u32[]{:S(2)}, u32[]{:S(2)}) collective-permute-start(bf16[24,4096]{1,0:T(8,128)(2,1)S(1)} %get-tuple-element.36), channel_id=1, source_target_pairs={{0,8},{4,12},{8,0},{12,4},{16,24},{20,28},{24,16},{28,20},{1,9},{5... | collective-permute-start | bytes 589832 | tf_op jit(solution)/shard_map/ppermute | solution.py:26
  6.8 14.2 %collective-permute-start.3 = (bf16[24,4224]{1,0:T(8,128)(2,1)S(1)}, bf16[24,4224]{1,0:T(8,128)(2,1)S(1)}, u32[]{:S(2)}, u32[]{:S(2)}) collective-permute-start(bf16[24,4224]{1,0:T(8,128)(2,1)S(1)} %get-tuple-element.40), channel_id=1, source_target_pairs={{0,1},{1,0},{2,3},{3,2},{4,5},{5,4},{6,7},{7,6},{8,9},{9,8},{10,11... | collective-permute-start | bytes 608264 | tf_op jit(solution)/shard_map/ppermute | solution.py:30
  8.4 17.6 %collective-permute-start.4 = (bf16[24,4224]{1,0:T(8,128)(2,1)S(1)}, bf16[24,4224]{1,0:T(8,128)(2,1)S(1)}, u32[]{:S(2)}, u32[]{:S(2)}) collective-permute-start(bf16[24,4224]{1,0:T(8,128)(2,1)S(1)} %get-tuple-element.41), channel_id=1, source_target_pairs={{0,2},{1,3},{2,0},{3,1},{4,6},{5,7},{6,4},{7,5},{8,10},{9,11},{10,... | collective-permute-start | bytes 608264 | tf_op jit(solution)/shard_map/ppermute | solution.py:30
  11.0 15.0 %collective-permute-start.5 = (bf16[24,4224]{1,0:T(8,128)(2,1)S(1)}, bf16[24,4224]{1,0:T(8,128)(2,1)S(1)}, u32[]{:S(2)}, u32[]{:S(2)}) collective-permute-start(bf16[24,4224]{1,0:T(8,128)(2,1)S(1)} %get-tuple-element.42), channel_id=1, source_target_pairs={{0,3},{1,2},{2,1},{3,0},{4,7},{5,6},{6,5},{7,4},{8,11},{9,10},{10,... | collective-permute-start | bytes 608264 | tf_op jit(solution)/shard_map/ppermute | solution.py:30
  11.2 9.8 %collective-permute-start.1 = (bf16[24,4096]{1,0:T(8,128)(2,1)S(1)}, bf16[24,4096]{1,0:T(8,128)(2,1)S(1)}, u32[]{:S(2)}, u32[]{:S(2)}) collective-permute-start(bf16[24,4096]{1,0:T(8,128)(2,1)S(1)} %get-tuple-element.37), channel_id=1, source_target_pairs={{0,16},{4,20},{8,24},{12,28},{16,0},{20,4},{24,8},{28,12},{1,17},{... | collective-permute-start | bytes 589832 | tf_op jit(solution)/shard_map/ppermute | solution.py:26
  12.7 8.3 %collective-permute-start.2 = (bf16[24,4096]{1,0:T(8,128)(2,1)S(1)}, bf16[24,4096]{1,0:T(8,128)(2,1)S(1)}, u32[]{:S(2)}, u32[]{:S(2)}) collective-permute-start(bf16[24,4096]{1,0:T(8,128)(2,1)S(1)} %get-tuple-element.38), channel_id=1, source_target_pairs={{0,24},{4,28},{8,16},{12,20},{16,8},{20,12},{24,0},{28,4},{1,25},{... | collective-permute-start | bytes 589832 | tf_op jit(solution)/shard_map/ppermute | solution.py:26
  26.0 3.7 %collective-permute-start.9 = (bf16[4,24,2048]{2,1,0:T(8,128)(2,1)S(1)}, bf16[4,24,2048]{2,1,0:T(8,128)(2,1)S(1)}, u32[]{:S(2)}, u32[]{:S(2)}) collective-permute-start(bf16[4,24,2048]{2,1,0:T(8,128)(2,1)S(1)} %shard_map.52), channel_id=1, source_target_pairs={{0,4},{4,0},{8,12},{12,8},{16,20},{20,16},{24,28},{28,24},{1,5},{5... | collective-permute-start | bytes 1179656 | tf_op jit(solution)/shard_map/ppermute | solution.py:26
  26.1 21.9 %collective-permute-start.8 = (bf16[4,24,4224]{2,1,0:T(8,128)(2,1)S(1)}, bf16[4,24,4224]{2,1,0:T(8,128)(2,1)S(1)}, u32[]{:S(2)}, u32[]{:S(2)}) collective-permute-start(bf16[4,24,4224]{2,1,0:T(8,128)(2,1)S(1)} %shard_map.51.refs_0_), channel_id=1, source_target_pairs={{0,24},{4,28},{8,16},{12,20},{16,8},{20,12},{24,0},{28,4},{1,25},{... | collective-permute-start | bytes 2433032 | tf_op jit(solution)/shard_map/chips/ppermute | solution.py:26
  27.7 37.3 %collective-permute-start.7 = (bf16[4,24,4224]{2,1,0:T(8,128)(2,1)S(1)}, bf16[4,24,4224]{2,1,0:T(8,128)(2,1)S(1)}, u32[]{:S(2)}, u32[]{:S(2)}) collective-permute-start(bf16[4,24,4224]{2,1,0:T(8,128)(2,1)S(1)} %shard_map.51.refs_0_), channel_id=1, source_target_pairs={{0,16},{4,20},{8,24},{12,28},{16,0},{20,4},{24,8},{28,12},{1,17},{... | collective-permute-start | bytes 2433032 | tf_op jit(solution)/shard_map/chips/ppermute | solution.py:26
  28.2 36.9 %collective-permute-start.6 = (bf16[4,24,4224]{2,1,0:T(8,128)(2,1)S(1)}, bf16[4,24,4224]{2,1,0:T(8,128)(2,1)S(1)}, u32[]{:S(2)}, u32[]{:S(2)}) collective-permute-start(bf16[4,24,4224]{2,1,0:T(8,128)(2,1)S(1)} %shard_map.51.refs_0_), channel_id=1, source_target_pairs={{0,8},{4,12},{8,0},{12,4},{16,24},{20,28},{24,16},{28,20},{1,9},{5... | collective-permute-start | bytes 2433032 | tf_op jit(solution)/shard_map/chips/ppermute | solution.py:26
  29.8 38.6 %collective-permute-start.11 = (bf16[192,2048]{1,0:T(8,128)(2,1)S(1)}, bf16[192,2048]{1,0:T(8,128)(2,1)S(1)}, u32[]{:S(2)}, u32[]{:S(2)}) collective-permute-start(bf16[192,2048]{1,0:T(8,128)(2,1)S(1)} %shard_map.53.refs_0_), channel_id=1, source_target_pairs={{0,2},{1,3},{2,0},{3,1},{4,6},{5,7},{6,4},{7,5},{8,10},{9,11},{10,... | collective-permute-start | bytes 2359304 | tf_op jit(solution)/shard_map/planes_far/ppermute | solution.py:30
  34.0 34.5 %collective-permute-start.10 = (bf16[192,2048]{1,0:T(8,128)(2,1)S(1)}, bf16[192,2048]{1,0:T(8,128)(2,1)S(1)}, u32[]{:S(2)}, u32[]{:S(2)}) collective-permute-start(bf16[192,2048]{1,0:T(8,128)(2,1)S(1)} %shard_map.53.refs_0_), channel_id=1, source_target_pairs={{0,1},{1,0},{2,3},{3,2},{4,5},{5,4},{6,7},{7,6},{8,9},{9,8},{10,11... | collective-permute-start | bytes 2359304 | tf_op jit(solution)/shard_map/planes_near/ppermute | solution.py:30
  68.8 7.7 %collective-permute-start.14 = (bf16[16,24,4224]{2,1,0:T(8,128)(2,1)S(1)}, bf16[16,24,4224]{2,1,0:T(8,128)(2,1)S(1)}, u32[]{:S(2)}, u32[]{:S(2)}) collective-permute-start(bf16[16,24,4224]{2,1,0:T(8,128)(2,1)S(1)} %shard_map.55.refs_0_), channel_id=1, source_target_pairs={{0,4},{4,0},{8,12},{12,8},{16,20},{20,16},{24,28},{28,24},{1,5},{5... | collective-permute-start | bytes 9732104 | tf_op jit(solution)/shard_map/cores/ppermute | solution.py:26
  69.0 8.7 %collective-permute-start.15 = (bf16[192,1024]{1,0:T(8,128)(2,1)S(1)}, bf16[192,1024]{1,0:T(8,128)(2,1)S(1)}, u32[]{:S(2)}, u32[]{:S(2)}) collective-permute-start(bf16[192,1024]{1,0:T(8,128)(2,1)S(1)} %get-tuple-element.64), channel_id=1, source_target_pairs={{0,0},{1,2},{2,1},{3,3},{4,4},{5,6},{6,5},{7,7},{8,8},{9,10},{10,9... | collective-permute-start | bytes 1179656 | tf_op jit(solution)/shard_map/planes_last/ppermute | solution.py:38
  69.7 13.1 %collective-permute-start.16 = (bf16[192,1024]{1,0:T(8,128)(2,1)S(1)}, bf16[192,1024]{1,0:T(8,128)(2,1)S(1)}, u32[]{:S(2)}, u32[]{:S(2)}) collective-permute-start(bf16[192,1024]{1,0:T(8,128)(2,1)S(1)} %get-tuple-element.65), channel_id=1, source_target_pairs={{0,1},{1,0},{2,3},{3,2},{4,5},{5,4},{6,7},{7,6},{8,9},{9,8},{10,11... | collective-permute-start | bytes 1179656 | tf_op jit(solution)/shard_map/planes_last/ppermute | solution.py:30
  72.9 18.6 %collective-permute-start.12 = (bf16[192,1024]{1,0:T(8,128)(2,1)S(1)}, bf16[192,1024]{1,0:T(8,128)(2,1)S(1)}, u32[]{:S(2)}, u32[]{:S(2)}) collective-permute-start(bf16[192,1024]{1,0:T(8,128)(2,1)S(1)} %get-tuple-element.54), channel_id=1, source_target_pairs={{0,0},{1,2},{2,1},{3,3},{4,4},{5,6},{6,5},{7,7},{8,8},{9,10},{10,9... | collective-permute-start | bytes 1179656 | tf_op jit(solution)/shard_map/planes_last/ppermute | solution.py:38
  73.6 17.9 %collective-permute-start.13 = (bf16[192,1024]{1,0:T(8,128)(2,1)S(1)}, bf16[192,1024]{1,0:T(8,128)(2,1)S(1)}, u32[]{:S(2)}, u32[]{:S(2)}) collective-permute-start(bf16[192,1024]{1,0:T(8,128)(2,1)S(1)} %get-tuple-element.55), channel_id=1, source_target_pairs={{0,1},{1,0},{2,3},{3,2},{4,5},{5,4},{6,7},{7,6},{8,9},{9,8},{10,11... | collective-permute-start | bytes 1179656 | tf_op jit(solution)/shard_map/planes_last/ppermute | solution.py:30

commit v3 on v2

--- a/solution.py
+++ b/solution.py
@@ -43,12 +43,11 @@
     return row // 2, row % 2, lax.axis_index("col")
 
 
-def deal_kernel(chips, tenants_hbm, labels_hbm, features_hbm, *refs):
-    *outs, features, tenants, labels, sems = refs
+def deal_kernel(chips, codes_hbm, features_hbm, *refs):
+    *outs, features, groups, sems = refs
     loads = [
         pltpu.make_async_copy(features_hbm, features, sems.at[0]),
-        pltpu.make_async_copy(tenants_hbm, tenants, sems.at[1]),
-        pltpu.make_async_copy(labels_hbm, labels, sems.at[2]),
+        pltpu.make_async_copy(codes_hbm, groups, sems.at[1]),
     ]
     for load in loads:
         load.start()
@@ -61,7 +60,7 @@
     token = lax.broadcasted_iota(jnp.int32, (local, LANES), 0)
     codes = jnp.zeros((local, LANES), jnp.int32)
     for index in range(local):
-        codes = jnp.where(token == index, tenants[index] * LABELS + labels[index], codes)
+        codes = jnp.where(token == index, groups[index], codes)
     codes = codes.astype(jnp.float32).astype(jnp.bfloat16)
     for mask, out in enumerate(col_outs):
         start = pl.multiple_of((col ^ mask) * width, LANES)
@@ -153,7 +152,7 @@
             for part in parts[index : index + count]:
                 offset = first if part.shape[1] > width else 0
                 both.append(part[:, pl.ds(start + offset, size)])
-            blocks.append(both[0] if count == 1 else jnp.where(inside, both[0], both[1]))
+            blocks.append(both[0] if count == 1 else jnp.where(inside, both[1], both[0]))
             index += count
         return jnp.concatenate(blocks, axis=0)
 
@@ -166,17 +165,17 @@
         target = cov.at[pl.ds(first + step // per_row * tile, tile), pl.ds(step % per_row * chunk, chunk)]
         return pltpu.make_async_copy(out_ref.at[slot], target, out_sem.at[slot])
 
-    for start in range(0, width, tile):
-        left_ref[start : start + tile, :] = features(start, tile).T
     ones = jnp.ones((total, LANES), jnp.bfloat16)
     for step in range(steps):
         if step >= slots:
             store(step - slots).wait()
-        left = left_ref[pl.ds(step // per_row * tile, tile), :]
+        rows = pl.ds(step // per_row * tile, tile)
         if step % per_row == 0:
+            left = features(step // per_row * tile, tile).T
+            left_ref[rows, :] = left
             row_mean = jnp.dot(left, ones, preferred_element_type=jnp.float32)[:, :1] / total
         span = pl.ds(step % per_row * chunk, chunk)
-        gram = jnp.dot(left, panel[:, span], preferred_element_type=jnp.float32)
+        gram = jnp.dot(left_ref[rows, :], panel[:, span], preferred_element_type=jnp.float32)
         out_ref[step % slots] = gram * (1.0 / total) - row_mean * mean[:1, span]
         store(step).start()
 
@@ -201,8 +200,8 @@
 def gram(groups, panel, mean, member, counts, first, width, outs):
     total, columns = panel.shape
     tile = min(256, width)
-    chunk = min(2048, columns)
-    slots = min(8, width // tile * (columns // chunk))
+    chunk = min(1024, columns)
+    slots = min(16, width // tile * (columns // chunk))
     parts = [part for group in groups for part in group]
     inputs = [*parts, panel, mean, member, counts]
     specs = [WHOLE] * len(inputs)
@@ -225,7 +224,129 @@
             pltpu.SemaphoreType.DMA,
         ],
         input_output_aliases=aliases,
-        compiler_params=params(40),
+        compiler_params=params(25),
+        cost_estimate=pl.CostEstimate(flops=0, bytes_accessed=2 * MIB, transcendentals=0),
+    )(*inputs)
+
+
+def early_kernel(first, tile, *refs):
+    *parts, panel, acc, sums, left_ref = refs
+    width, depth = left_ref.shape
+    columns = panel.shape[1]
+    chunk = min(1024, columns)
+    ones = jnp.ones((depth, LANES), jnp.bfloat16)
+    for start in range(0, width, tile):
+        rows = pl.ds(start, tile)
+        left = jnp.concatenate([part[:, pl.ds(first + start, tile)] for part in parts], axis=0).T
+        left_ref[rows, :] = left
+        sums[rows, :] = jnp.dot(left, ones, preferred_element_type=jnp.float32)
+    for start in range(0, width, tile):
+        rows = pl.ds(start, tile)
+        for begin in range(0, columns, chunk):
+            span = pl.ds(begin, chunk)
+            acc[rows, span] = jnp.dot(left_ref[rows, :], panel[:depth, span], preferred_element_type=jnp.float32)
+
+
+def early(parts, panel, first, width):
+    shard = parts[0].shape[0]
+    depth = shard * len(parts)
+    return kernel(
+        functools.partial(early_kernel, first, min(256, width)),
+        [((width, panel.shape[1]), jnp.float32), ((width, LANES), jnp.float32)],
+        [*parts, panel],
+        mib=10,
+        scratch=[pltpu.VMEM((width, depth), jnp.bfloat16)],
+    )
+
+
+def late_kernel(count, first, tile, *refs):
+    parts, last, refs = refs[: count[0]], refs[count[0] : sum(count)], refs[sum(count) :]
+    acc, sums, panel, mean, member, counts = refs[:6]
+    cov, cross, left_ref, out_ref, cross_ref, out_sem, cross_sem = refs[-7:]
+    _, _, col = place()
+    total, columns = panel.shape
+    width, depth = left_ref.shape
+    slice_width = cross_ref.shape[1]
+    chunk = out_ref.shape[2]
+    inside = (col > 0) & (col < count[0])
+
+    def latest(start, size):
+        both = [part[:, pl.ds(start, size)] for part in last]
+        return both[0] if len(both) == 1 else jnp.where(inside, both[1], both[0])
+
+    slots = out_ref.shape[0]
+    per_row = columns // chunk
+    steps = width // tile * per_row
+
+    def store(step):
+        slot = step % slots
+        target = cov.at[pl.ds(first + step // per_row * tile, tile), pl.ds(step % per_row * chunk, chunk)]
+        return pltpu.make_async_copy(out_ref.at[slot], target, out_sem.at[slot])
+
+    ones = jnp.ones((depth, LANES), jnp.bfloat16)
+    for step in range(steps):
+        if step >= slots:
+            store(step - slots).wait()
+        rows = pl.ds(step // per_row * tile, tile)
+        if step % per_row == 0:
+            left = latest(step // per_row * tile, tile).T
+            left_ref[rows, :] = left
+            row_sum = sums[rows, :] + jnp.dot(left, ones, preferred_element_type=jnp.float32)
+            row_mean = row_sum[:, :1] / total
+        span = pl.ds(step % per_row * chunk, chunk)
+        gram = acc[rows, span] + jnp.dot(left_ref[rows, :], panel[total - depth :, span], preferred_element_type=jnp.float32)
+        out_ref[step % slots] = gram * (1.0 / total) - row_mean * mean[:1, span]
+        store(step).start()
+
+    begin = col * slice_width - first
+    mine = (begin >= 0) & (begin < width)
+    save = pltpu.make_async_copy(cross_ref, cross, cross_sem)
+
+    @pl.when(mine)
+    def _():
+        place_in_row = pl.multiple_of(col * slice_width, LANES)
+        blocks = [part[:, pl.ds(place_in_row, slice_width)] for part in parts]
+        own = jnp.concatenate([*blocks, latest(pl.multiple_of(begin, LANES), slice_width)], axis=0)
+        group_sums = lax.dot_general(member[...], own, (((0,), (0,)), ((), ())), preferred_element_type=jnp.float32)
+        slice_mean = jnp.dot(jnp.ones((16, total), jnp.bfloat16), own, preferred_element_type=jnp.float32)[:1] / total
+        groups = member.shape[1]
+        cross_ref[...] = (groups / total) * (group_sums - counts[:, :1] * slice_mean)
+        save.start()
+
+    for step in range(max(0, steps - slots), steps):
+        store(step).wait()
+    pl.when(mine)(save.wait)
+
+
+def late(parts, last, part_gram, panel, mean, member, counts, first, outs):
+    acc, sums = part_gram
+    columns = panel.shape[1]
+    width = acc.shape[0]
+    tile = min(256, width)
+    chunk = min(1024, columns)
+    slots = min(8, width // tile * (columns // chunk))
+    inputs = [*parts, *last, acc, sums, panel, mean, member, counts]
+    specs = [WHOLE] * len(inputs)
+    aliases = {}
+    if first:
+        aliases = {len(inputs): 0, len(inputs) + 1: 1}
+        inputs += outs
+        specs += [ANY] * 2
+    cov, cross = outs
+    return pl.pallas_call(
+        functools.partial(late_kernel, (len(parts), len(last)), first, tile),
+        out_shape=[jax.ShapeDtypeStruct(cov.shape, cov.dtype), jax.ShapeDtypeStruct(cross.shape, cross.dtype)],
+        in_specs=specs,
+        out_specs=[ANY, ANY],
+        scratch_shapes=[
+            pltpu.VMEM((width, last[0].shape[0]), jnp.bfloat16),
+            pltpu.VMEM((slots, tile, chunk), jnp.float32),
+            pltpu.VMEM(cross.shape, jnp.float32),
+            pltpu.SemaphoreType.DMA((slots,)),
+            pltpu.SemaphoreType.DMA,
+        ],
+        input_output_aliases=aliases,
+        compiler_params=params(14),
         cost_estimate=pl.CostEstimate(flops=0, bytes_accessed=2 * MIB, transcendentals=0),
     )(*inputs)
 
@@ -248,7 +369,10 @@
     with jax.named_scope("planes_near"):
         near = swap_cols(rows, 1)
     with jax.named_scope("chips"):
-        shards = [shard] + [swap_rows(shard, 2 * mask) for mask in (1, 2, 3)]
+        half = shard.shape[0] // 2
+        sides = [swap_rows(shard, 2), swap_rows(shard, 4)]
+        corner = [swap_rows(sides[1][:half], 2), swap_rows(sides[0][half:], 4)]
+        shards = [shard, *sides, *corner]
     shards, rows, near, far = lax.optimization_barrier((shards, rows, near, far))
     cuts = kernel(functools.partial(cut_kernel, 2), [((rows.shape[0], width), rows.dtype) for width in widths] * 2, [rows, far])
     (stacked,) = kernel(stack_kernel, [((4 * shard.shape[0], *shard.shape[1:]), shard.dtype)], shards)
@@ -258,7 +382,7 @@
     for index in range(len(widths)):
         own, passed = cuts[index :: len(widths)]
         with jax.named_scope("planes_last"):
-            last = (pair_cols(own, 1), swap_cols(passed, 1))
+            last = (swap_cols(passed, 1), pair_cols(own, 1))
         groups.append([(rows,), (near,), (far,), last])
     return groups, stacked, other
 
@@ -269,9 +393,11 @@
     if chips == 4 and planes == 4:
         return gather_line(rows, shard, widths)
     arrays = [(rows,)] + [(swap_cols(rows, mask),) for mask in range(1, planes)]
+    starts = [sum(widths[:index]) for index in range(len(widths))]
+    last = [arrays[-1][0][:, start : start + width] for start, width in zip(starts, widths)]
     shards = [shard] + [swap_rows(shard, 2 * mask) for mask in range(1, chips)]
     (stacked,) = kernel(stack_kernel, [((chips * shard.shape[0], *shard.shape[1:]), shard.dtype)], shards, mib=40)
-    return [arrays] * len(widths), stacked, swap_rows(stacked, 1)
+    return [[*arrays[:-1], (part,)] for part in last], stacked, swap_rows(stacked, 1)
 
 
 def shards(activations, tenant_ids, concept_labels):
@@ -288,13 +414,12 @@
     dealt = kernel(
         functools.partial(deal_kernel, chips),
         [((local, 2 * block), half)] * chips + [((local, panel_width + LANES), half)] * planes,
-        [tenant_ids, concept_labels, activations],
-        [ANY, ANY, ANY],
+        [tenant_ids * LABELS + concept_labels, activations],
+        [ANY, ANY],
         scratch=[
             pltpu.VMEM((local, width), half),
             pltpu.SMEM((local,), jnp.int32),
-            pltpu.SMEM((local,), jnp.int32),
-            pltpu.SemaphoreType.DMA((3,)),
+            pltpu.SemaphoreType.DMA((2,)),
         ],
     )
     to_rows, to_cols = dealt[:chips], dealt[chips:]
@@ -317,17 +442,21 @@
         functools.partial(column_kernel, chips),
         [((total, panel_width), half), ((8, panel_width), jnp.float32), ((total, groups), half), ((groups, LANES), jnp.float32)],
         [near, far],
-        mib=40,
+        mib=10,
     )
 
     outs = (
         jax.ShapeDtypeStruct((block, panel_width), jnp.float32),
         jax.ShapeDtypeStruct((groups, slice_width), jnp.float32),
     )
-    first = 0
-    for piece, piece_width in zip(pieces, widths):
-        outs = gram(piece, panel, mean, member, counts, first, piece_width, outs)
-        first += piece_width
+    (*parts, last), *others = pieces
+    parts = [part for (part,) in parts]
+    part_gram = early(parts, panel, 0, widths[0])
+    outs = late(parts, last, part_gram, panel, mean, member, counts, 0, outs)
+    first = widths[0]
+    for piece, size in zip(others, widths[1:]):
+        outs = gram(piece, panel, mean, member, counts, first, size, outs)
+        first += size
     return tuple(outs)
 
 

time: 101 us -> 98.4 us (0.974)
  Pallas kernels: 19.7 us -> 24.3 us
  starting transfers between devices: 26 us -> 22.5 us
  waiting for transfers between devices: 51.2 us -> 48.4 us
  local copies, waits for them, and re-layouts: 2.44 us -> 1.19 us
    ppermute x8 -> x9, waiting for transfers between devices: 37.6 us -> 21 us  [swap_rows(): lax.ppermute(x, 'row', [(i, i ^ mask) for i in range(lax.axis_size('row'))])]
    ppermute x7, waiting for transfers between devices: 13.6 us -> 27.4 us  [swap_cols(): lax.ppermute(x, 'col', [(i, i ^ mask) for i in range(lax.axis_size('col'))])]
    pallas_call x2 -> x1, Pallas kernels: 17.4 us -> 8.41 us  [gram(): pl.pallas_call(functools.partial(gram_kernel, tuple(map(len, groups)), fi...]
    pallas_call x7 -> x8, Pallas kernels: 2.35 us -> 9.4 us  [kernel(): pl.pallas_call(body, out_shape=[jax.ShapeDtypeStruct(shape, dtype) for sh...]
    pallas_call x0 -> x1, Pallas kernels: none -> 6.44 us  [late(): pl.pallas_call(functools.partial(late_kernel, (len(parts), len(last)), fi...]
    ppermute x7, starting transfers between devices: 14.8 us -> 12.2 us  [swap_cols(): lax.ppermute(x, 'col', [(i, i ^ mask) for i in range(lax.axis_size('col'))])]
    unnamed x6 -> x2, local copies, waits for them, and re-layouts: 2.44 us -> 1.13 us
    ppermute x8 -> x9, starting transfers between devices: 9.9 us -> 8.78 us  [swap_rows(): lax.ppermute(x, 'row', [(i, i ^ mask) for i in range(lax.axis_size('row'))])]
  transfers between devices with their start and end apart: 17 -> 18, of which waited for: 8 -> 8; matrix products, arithmetic and copies ran while one was open for 0% -> 0% of each run, Pallas kernels for 10% -> 15%
where the time goes in v3:
time: 98.4 us; the launch traced here: 98 us
  waiting for transfers between devices  48.4 us (49%)
  Pallas kernels  24.3 us (25%)
  starting transfers between devices  22.5 us (23%)
  local copies, waits for them, and re-layouts  1.19 us (1%)
    ppermute x7, waiting for transfers between devices, swap_cols(): lax.ppermute(x, 'col', [(i, i ^ mask) for i in range(lax.axis_size('col'))])  27.4 us
    ppermute x9, waiting for transfers between devices, swap_rows(): lax.ppermute(x, 'row', [(i, i ^ mask) for i in range(lax.axis_size('row'))])  21 us
    ppermute x7, starting transfers between devices, swap_cols(): lax.ppermute(x, 'col', [(i, i ^ mask) for i in range(lax.axis_size('col'))])  12.2 us
    pallas_call x8, Pallas kernels, kernel(): pl.pallas_call(body, out_shape=[jax.ShapeDtypeStruct(shape, dtype) for sh...  9.4 us
    ppermute x9, starting transfers between devices, swap_rows(): lax.ppermute(x, 'row', [(i, i ^ mask) for i in range(lax.axis_size('row'))])  8.78 us
    pallas_call x1, Pallas kernels, gram(): pl.pallas_call(functools.partial(gram_kernel, tuple(map(len, groups)), fi...  8.41 us
    pallas_call x1, Pallas kernels, late(): pl.pallas_call(functools.partial(late_kernel, (len(parts), len(last)), fi...  6.44 us
  transfers between devices with their start and end apart: 18, of which 8 were waited for; matrix products, arithmetic and copies ran while one was open for 0% of the time, Pallas kernels for 15%

profile of v3, /device:TPU:0, one launch (start us, length us, event | category | flops | bytes accessed | tf_op | source)
XLA Modules:
  0.0 98.0 jit_solution(11305327693929662723)
XLA Ops:
  0.6 0.7 multiply_add_fusion.codes_hbm
  1.3 1.1 %copy-done = bf16[24,16384]{1,0:T(8,128)(2,1)S(1)} copy-done((bf16[24,16384]{1,0:T(8,128)(2,1)S(1)}, bf16[24,16384]{1,0:T(8,128)(2,1)}, u32[]{:S(2)}) %copy-start) | copy-done | bytes 786456
  2.4 0.7 shard_map.50
  3.2 3.0 %collective-permute-start = (bf16[24,4096]{1,0:T(8,128)(2,1)S(1)}, bf16[24,4096]{1,0:T(8,128)(2,1)S(1)}, u32[]{:S(2)}, u32[]{:S(2)}) collective-permute-start(bf16[24,4096]{1,0:T(8,128)(2,1)S(1)} %get-tuple-element.39), channel_id=1, source_target_pairs={{0,8},{4,12},{8,0},{12,4},{16,24},{20,28},{24,16},{28,20},{1,9},{5... | collective-permute-start | bytes 589832 | tf_op jit(solution)/shard_map/ppermute | solution.py:26
  6.2 1.6 %collective-permute-start.3 = (bf16[24,4224]{1,0:T(8,128)(2,1)S(1)}, bf16[24,4224]{1,0:T(8,128)(2,1)S(1)}, u32[]{:S(2)}, u32[]{:S(2)}) collective-permute-start(bf16[24,4224]{1,0:T(8,128)(2,1)S(1)} %get-tuple-element.43), channel_id=1, source_target_pairs={{0,1},{1,0},{2,3},{3,2},{4,5},{5,4},{6,7},{7,6},{8,9},{9,8},{10,11... | collective-permute-start | bytes 608264 | tf_op jit(solution)/shard_map/ppermute | solution.py:30
  7.8 2.6 %collective-permute-start.4 = (bf16[24,4224]{1,0:T(8,128)(2,1)S(1)}, bf16[24,4224]{1,0:T(8,128)(2,1)S(1)}, u32[]{:S(2)}, u32[]{:S(2)}) collective-permute-start(bf16[24,4224]{1,0:T(8,128)(2,1)S(1)} %get-tuple-element.44), channel_id=1, source_target_pairs={{0,2},{1,3},{2,0},{3,1},{4,6},{5,7},{6,4},{7,5},{8,10},{9,11},{10,... | collective-permute-start | bytes 608264 | tf_op jit(solution)/shard_map/ppermute | solution.py:30
  10.3 0.2 collective-permute-start.5
  10.6 1.5 %collective-permute-start.1 = (bf16[24,4096]{1,0:T(8,128)(2,1)S(1)}, bf16[24,4096]{1,0:T(8,128)(2,1)S(1)}, u32[]{:S(2)}, u32[]{:S(2)}) collective-permute-start(bf16[24,4096]{1,0:T(8,128)(2,1)S(1)} %get-tuple-element.40), channel_id=1, source_target_pairs={{0,16},{4,20},{8,24},{12,28},{16,0},{20,4},{24,8},{28,12},{1,17},{... | collective-permute-start | bytes 589832 | tf_op jit(solution)/shard_map/ppermute | solution.py:26
  12.1 1.7 %collective-permute-start.2 = (bf16[24,4096]{1,0:T(8,128)(2,1)S(1)}, bf16[24,4096]{1,0:T(8,128)(2,1)S(1)}, u32[]{:S(2)}, u32[]{:S(2)}) collective-permute-start(bf16[24,4096]{1,0:T(8,128)(2,1)S(1)} %get-tuple-element.41), channel_id=1, source_target_pairs={{0,24},{4,28},{8,16},{12,20},{16,8},{20,12},{24,0},{28,4},{1,25},{... | collective-permute-start | bytes 589832 | tf_op jit(solution)/shard_map/ppermute | solution.py:26
  13.8 6.6 %collective-permute-done.1.refs_2_ = bf16[24,4096]{1,0:T(8,128)(2,1)S(1)} collective-permute-done((bf16[24,4096]{1,0:T(8,128)(2,1)S(1)}, bf16[24,4096]{1,0:T(8,128)(2,1)S(1)}, u32[]{:S(2)}, u32[]{:S(2)}) %collective-permute-start.1) | collective-permute-done | bytes 196640 | tf_op jit(solution)/shard_map/ppermute | solution.py:26
  20.4 4.9 %collective-permute-done.4 = bf16[24,4224]{1,0:T(8,128)(2,1)S(1)} collective-permute-done((bf16[24,4224]{1,0:T(8,128)(2,1)S(1)}, bf16[24,4224]{1,0:T(8,128)(2,1)S(1)}, u32[]{:S(2)}, u32[]{:S(2)}) %collective-permute-start.4) | collective-permute-done | bytes 202784 | tf_op jit(solution)/shard_map/ppermute | solution.py:30
  25.4 1.6 %collective-permute-start.7 = (bf16[4,24,4224]{2,1,0:T(8,128)(2,1)S(1)}, bf16[4,24,4224]{2,1,0:T(8,128)(2,1)S(1)}, u32[]{:S(2)}, u32[]{:S(2)}) collective-permute-start(bf16[4,24,4224]{2,1,0:T(8,128)(2,1)S(1)} %shard_map.51.refs_0_), channel_id=1, source_target_pairs={{0,16},{4,20},{8,24},{12,28},{16,0},{20,4},{24,8},{28,12},{1,17},{... | collective-permute-start | bytes 2433032 | tf_op jit(solution)/shard_map/chips/ppermute | solution.py:26
  27.0 0.5 collective-permute-start.6
  27.5 0.1 collective-permute-start.10
  27.6 1.7 %collective-permute-done.10.refs_4_ = bf16[4,24,2048]{2,1,0:T(8,128)(2,1)S(1)} collective-permute-done((bf16[4,24,2048]{2,1,0:T(8,128)(2,1)S(1)}, bf16[4,24,2048]{2,1,0:T(8,128)(2,1)S(1)}, u32[]{:S(2)}, u32[]{:S(2)}) %collective-permute-start.10) | collective-permute-done | bytes 393248 | tf_op jit(solution)/shard_map/ppermute | solution.py:26
  29.4 4.3 %collective-permute-start.12 = (bf16[192,2048]{1,0:T(8,128)(2,1)S(1)}, bf16[192,2048]{1,0:T(8,128)(2,1)S(1)}, u32[]{:S(2)}, u32[]{:S(2)}) collective-permute-start(bf16[192,2048]{1,0:T(8,128)(2,1)S(1)} %shard_map.53.refs_0_), channel_id=1, source_target_pairs={{0,2},{1,3},{2,0},{3,1},{4,6},{5,7},{6,4},{7,5},{8,10},{9,11},{10,... | collective-permute-start | bytes 2359304 | tf_op jit(solution)/shard_map/planes_far/ppermute | solution.py:30
  33.7 9.0 %collective-permute-done.7.refs_2_ = bf16[4,24,4224]{2,1,0:T(8,128)(2,1)S(1)} collective-permute-done((bf16[4,24,4224]{2,1,0:T(8,128)(2,1)S(1)}, bf16[4,24,4224]{2,1,0:T(8,128)(2,1)S(1)}, u32[]{:S(2)}, u32[]{:S(2)}) %collective-permute-start.7) | collective-permute-done | bytes 811040 | tf_op jit(solution)/shard_map/chips/ppermute | solution.py:26
  42.6 0.2 collective-permute-start.8
  42.9 3.2 %collective-permute-done.6.refs_1_ = bf16[4,24,4224]{2,1,0:T(8,128)(2,1)S(1)} collective-permute-done((bf16[4,24,4224]{2,1,0:T(8,128)(2,1)S(1)}, bf16[4,24,4224]{2,1,0:T(8,128)(2,1)S(1)}, u32[]{:S(2)}, u32[]{:S(2)}) %collective-permute-start.6) | collective-permute-done | bytes 811040 | tf_op jit(solution)/shard_map/chips/ppermute | solution.py:26
  46.2 22.3 %collective-permute-done.12.refs_1_.refs_2_ = bf16[192,2048]{1,0:T(8,128)(2,1)S(1)} collective-permute-done((bf16[192,2048]{1,0:T(8,128)(2,1)S(1)}, bf16[192,2048]{1,0:T(8,128)(2,1)S(1)}, u32[]{:S(2)}, u32[]{:S(2)}) %collective-permute-start.12) | collective-permute-done | bytes 786464 | tf_op jit(solution)/shard_map/planes_far/ppermute | solution.py:30
  68.5 0.2 collective-permute-done.11.refs_1_
  68.6 0.2 shard_map.55.refs_0_
  68.9 0.1 shard_map.54
  69.1 1.6 %collective-permute-start.16 = (bf16[192,1024]{1,0:T(8,128)(2,1)S(1)}, bf16[192,1024]{1,0:T(8,128)(2,1)S(1)}, u32[]{:S(2)}, u32[]{:S(2)}) collective-permute-start(bf16[192,1024]{1,0:T(8,128)(2,1)S(1)} %get-tuple-element.68), channel_id=1, source_target_pairs={{0,1},{1,0},{2,3},{3,2},{4,5},{5,4},{6,7},{7,6},{8,9},{9,8},{10,11... | collective-permute-start | bytes 1179656 | tf_op jit(solution)/shard_map/planes_last/ppermute | solution.py:30
  70.6 0.7 collective-permute-start.17
  71.3 2.0 %collective-permute-start.13 = (bf16[192,1024]{1,0:T(8,128)(2,1)S(1)}, bf16[192,1024]{1,0:T(8,128)(2,1)S(1)}, u32[]{:S(2)}, u32[]{:S(2)}) collective-permute-start(bf16[192,1024]{1,0:T(8,128)(2,1)S(1)} %get-tuple-element.57), channel_id=1, source_target_pairs={{0,1},{1,0},{2,3},{3,2},{4,5},{5,4},{6,7},{7,6},{8,9},{9,8},{10,11... | collective-permute-start | bytes 1179656 | tf_op jit(solution)/shard_map/planes_last/ppermute | solution.py:30
  73.3 0.9 collective-permute-start.14
  74.2 0.6 collective-permute-done.15.refs_1_
  74.7 1.1 %shard_map.56 = (bf16[768,4096]{1,0:T(8,128)(2,1)S(1)}, f32[8,4096]{1,0:T(8,128)S(1)}, bf16[768,128]{1,0:T(8,128)(2,1)S(1)}, f32[128,128]{1,0:T(8,128)S(1)}) custom-call(bf16[16,24,4224]{2,1,0:T(8,128)(2,1)S(1)} %shard_map.55.refs_0_, bf16[16,24,4224]{2,1,0:T(8,128)(2,1)S(1)} %collective-permute-done.15.refs_1_), custom_call_target="tpu_custom_call" | custom-call | tf_op jit(solution)/shard_map/pallas_call | solution.py:355
  75.9 7.1 %shard_map.57 = (f32[1024,4096]{1,0:T(8,128)S(1)}, f32[1024,128]{1,0:T(8,128)S(1)}) custom-call(bf16[192,2048]{1,0:T(8,128)(2,1)S(1)} %shard_map.53.refs_0_, bf16[192,2048]{1,0:T(8,128)(2,1)S(1)} %collective-permute-done.11.refs_1_, bf16[192,2048]{1,0:T(8,128)(2,1)S(1)} %collective-permute-done.12.refs_1_.refs_2_, ...), custom_call_target="tpu_custom_call" | custom-call | tf_op jit(solution)/shard_map/pallas_call | solution.py:355
  83.0 6.4 %shard_map.58 = (f32[2048,4096]{1,0:T(8,128)}, f32[128,512]{1,0:T(8,128)}) custom-call(bf16[192,2048]{1,0:T(8,128)(2,1)S(1)} %shard_map.53.refs_0_, bf16[192,2048]{1,0:T(8,128)(2,1)S(1)} %collective-permute-done.11.refs_1_, bf16[192,2048]{1,0:T(8,128)(2,1)S(1)} %collective-permute-done.12.refs_1_.refs_2_, ...), custom_call_target="tpu_custom_call" | custom-call | bytes 2097152 | tf_op jit(solution)/shard_map/pallas_call | solution.py:336
  89.5 8.4 %shard_map.59 = (f32[2048,4096]{1,0:T(8,128)}, f32[128,512]{1,0:T(8,128)}) custom-call(bf16[192,2048]{1,0:T(8,128)(2,1)S(1)} %shard_map.53.refs_0_, bf16[192,2048]{1,0:T(8,128)(2,1)S(1)} %collective-permute-done.11.refs_1_, bf16[192,2048]{1,0:T(8,128)(2,1)S(1)} %collective-permute-done.12.refs_1_.refs_2_, ...), custom_call_target="tpu_custom_call", output_to_operand_aliasing={{0}: (9, {}), {1}: (10, {})} | custom-call | bytes 2097152 | tf_op jit(solution)/shard_map/pallas_call | solution.py:214
  (19 shorter events, 0.4 us)
Async XLA Ops:
  1.3 1.1 %copy-start = (bf16[24,16384]{1,0:T(8,128)(2,1)S(1)}, bf16[24,16384]{1,0:T(8,128)(2,1)}, u32[]{:S(2)}) copy-start(bf16[24,16384]{1,0:T(8,128)(2,1)} %features_hbm.1) | copy-start | bytes 2359300
  3.2 8.9 %collective-permute-start = (bf16[24,4096]{1,0:T(8,128)(2,1)S(1)}, bf16[24,4096]{1,0:T(8,128)(2,1)S(1)}, u32[]{:S(2)}, u32[]{:S(2)}) collective-permute-start(bf16[24,4096]{1,0:T(8,128)(2,1)S(1)} %get-tuple-element.39), channel_id=1, source_target_pairs={{0,8},{4,12},{8,0},{12,4},{16,24},{20,28},{24,16},{28,20},{1,9},{5... | collective-permute-start | bytes 589832 | tf_op jit(solution)/shard_map/ppermute | solution.py:26
  6.2 14.2 %collective-permute-start.3 = (bf16[24,4224]{1,0:T(8,128)(2,1)S(1)}, bf16[24,4224]{1,0:T(8,128)(2,1)S(1)}, u32[]{:S(2)}, u32[]{:S(2)}) collective-permute-start(bf16[24,4224]{1,0:T(8,128)(2,1)S(1)} %get-tuple-element.43), channel_id=1, source_target_pairs={{0,1},{1,0},{2,3},{3,2},{4,5},{5,4},{6,7},{7,6},{8,9},{9,8},{10,11... | collective-permute-start | bytes 608264 | tf_op jit(solution)/shard_map/ppermute | solution.py:30
  7.8 17.6 %collective-permute-start.4 = (bf16[24,4224]{1,0:T(8,128)(2,1)S(1)}, bf16[24,4224]{1,0:T(8,128)(2,1)S(1)}, u32[]{:S(2)}, u32[]{:S(2)}) collective-permute-start(bf16[24,4224]{1,0:T(8,128)(2,1)S(1)} %get-tuple-element.44), channel_id=1, source_target_pairs={{0,2},{1,3},{2,0},{3,1},{4,6},{5,7},{6,4},{7,5},{8,10},{9,11},{10,... | collective-permute-start | bytes 608264 | tf_op jit(solution)/shard_map/ppermute | solution.py:30
  10.3 15.0 %collective-permute-start.5 = (bf16[24,4224]{1,0:T(8,128)(2,1)S(1)}, bf16[24,4224]{1,0:T(8,128)(2,1)S(1)}, u32[]{:S(2)}, u32[]{:S(2)}) collective-permute-start(bf16[24,4224]{1,0:T(8,128)(2,1)S(1)} %get-tuple-element.45), channel_id=1, source_target_pairs={{0,3},{1,2},{2,1},{3,0},{4,7},{5,6},{6,5},{7,4},{8,11},{9,10},{10,... | collective-permute-start | bytes 608264 | tf_op jit(solution)/shard_map/ppermute | solution.py:30
  10.6 9.8 %collective-permute-start.1 = (bf16[24,4096]{1,0:T(8,128)(2,1)S(1)}, bf16[24,4096]{1,0:T(8,128)(2,1)S(1)}, u32[]{:S(2)}, u32[]{:S(2)}) collective-permute-start(bf16[24,4096]{1,0:T(8,128)(2,1)S(1)} %get-tuple-element.40), channel_id=1, source_target_pairs={{0,16},{4,20},{8,24},{12,28},{16,0},{20,4},{24,8},{28,12},{1,17},{... | collective-permute-start | bytes 589832 | tf_op jit(solution)/shard_map/ppermute | solution.py:26
  12.1 8.3 %collective-permute-start.2 = (bf16[24,4096]{1,0:T(8,128)(2,1)S(1)}, bf16[24,4096]{1,0:T(8,128)(2,1)S(1)}, u32[]{:S(2)}, u32[]{:S(2)}) collective-permute-start(bf16[24,4096]{1,0:T(8,128)(2,1)S(1)} %get-tuple-element.41), channel_id=1, source_target_pairs={{0,24},{4,28},{8,16},{12,20},{16,8},{20,12},{24,0},{28,4},{1,25},{... | collective-permute-start | bytes 589832 | tf_op jit(solution)/shard_map/ppermute | solution.py:26
  25.4 17.2 %collective-permute-start.7 = (bf16[4,24,4224]{2,1,0:T(8,128)(2,1)S(1)}, bf16[4,24,4224]{2,1,0:T(8,128)(2,1)S(1)}, u32[]{:S(2)}, u32[]{:S(2)}) collective-permute-start(bf16[4,24,4224]{2,1,0:T(8,128)(2,1)S(1)} %shard_map.51.refs_0_), channel_id=1, source_target_pairs={{0,16},{4,20},{8,24},{12,28},{16,0},{20,4},{24,8},{28,12},{1,17},{... | collective-permute-start | bytes 2433032 | tf_op jit(solution)/shard_map/chips/ppermute | solution.py:26
  27.0 19.1 %collective-permute-start.6 = (bf16[4,24,4224]{2,1,0:T(8,128)(2,1)S(1)}, bf16[4,24,4224]{2,1,0:T(8,128)(2,1)S(1)}, u32[]{:S(2)}, u32[]{:S(2)}) collective-permute-start(bf16[4,24,4224]{2,1,0:T(8,128)(2,1)S(1)} %shard_map.51.refs_0_), channel_id=1, source_target_pairs={{0,8},{4,12},{8,0},{12,4},{16,24},{20,28},{24,16},{28,20},{1,9},{5... | collective-permute-start | bytes 2433032 | tf_op jit(solution)/shard_map/chips/ppermute | solution.py:26
  27.5 1.8 %collective-permute-start.10 = (bf16[4,24,2048]{2,1,0:T(8,128)(2,1)S(1)}, bf16[4,24,2048]{2,1,0:T(8,128)(2,1)S(1)}, u32[]{:S(2)}, u32[]{:S(2)}) collective-permute-start(bf16[4,24,2048]{2,1,0:T(8,128)(2,1)S(1)} %shard_map.52), channel_id=1, source_target_pairs={{0,4},{4,0},{8,12},{12,8},{16,20},{20,16},{24,28},{28,24},{1,5},{5... | collective-permute-start | bytes 1179656 | tf_op jit(solution)/shard_map/ppermute | solution.py:26
  29.4 39.1 %collective-permute-start.12 = (bf16[192,2048]{1,0:T(8,128)(2,1)S(1)}, bf16[192,2048]{1,0:T(8,128)(2,1)S(1)}, u32[]{:S(2)}, u32[]{:S(2)}) collective-permute-start(bf16[192,2048]{1,0:T(8,128)(2,1)S(1)} %shard_map.53.refs_0_), channel_id=1, source_target_pairs={{0,2},{1,3},{2,0},{3,1},{4,6},{5,7},{6,4},{7,5},{8,10},{9,11},{10,... | collective-permute-start | bytes 2359304 | tf_op jit(solution)/shard_map/planes_far/ppermute | solution.py:30
  33.7 35.0 %collective-permute-start.11 = (bf16[192,2048]{1,0:T(8,128)(2,1)S(1)}, bf16[192,2048]{1,0:T(8,128)(2,1)S(1)}, u32[]{:S(2)}, u32[]{:S(2)}) collective-permute-start(bf16[192,2048]{1,0:T(8,128)(2,1)S(1)} %shard_map.53.refs_0_), channel_id=1, source_target_pairs={{0,1},{1,0},{2,3},{3,2},{4,5},{5,4},{6,7},{7,6},{8,9},{9,8},{10,11... | collective-permute-start | bytes 2359304 | tf_op jit(solution)/shard_map/planes_near/ppermute | solution.py:30
  42.6 26.0 %collective-permute-start.8 = (bf16[2,24,4224]{2,1,0:T(8,128)(2,1)S(1)}, bf16[2,24,4224]{2,1,0:T(8,128)(2,1)S(1)}, u32[]{:S(2)}, u32[]{:S(2)}) collective-permute-start(bf16[2,24,4224]{2,1,0:T(8,128)(2,1)S(1)} %slice.8), channel_id=1, source_target_pairs={{0,8},{4,12},{8,0},{12,4},{16,24},{20,28},{24,16},{28,20},{1,9},{5... | collective-permute-start | bytes 1216520 | tf_op jit(solution)/shard_map/chips/ppermute | solution.py:26
  46.1 22.6 %collective-permute-start.9 = (bf16[2,24,4224]{2,1,0:T(8,128)(2,1)S(1)}, bf16[2,24,4224]{2,1,0:T(8,128)(2,1)S(1)}, u32[]{:S(2)}, u32[]{:S(2)}) collective-permute-start(bf16[2,24,4224]{2,1,0:T(8,128)(2,1)S(1)} %slice.9), channel_id=1, source_target_pairs={{0,16},{4,20},{8,24},{12,28},{16,0},{20,4},{24,8},{28,12},{1,17},{... | collective-permute-start | bytes 1216520 | tf_op jit(solution)/shard_map/chips/ppermute | solution.py:26
  68.9 5.9 %collective-permute-start.15 = (bf16[16,24,4224]{2,1,0:T(8,128)(2,1)S(1)}, bf16[16,24,4224]{2,1,0:T(8,128)(2,1)S(1)}, u32[]{:S(2)}, u32[]{:S(2)}) collective-permute-start(bf16[16,24,4224]{2,1,0:T(8,128)(2,1)S(1)} %shard_map.55.refs_0_), channel_id=1, source_target_pairs={{0,4},{4,0},{8,12},{12,8},{16,20},{20,16},{24,28},{28,24},{1,5},{5... | collective-permute-start | bytes 9732104 | tf_op jit(solution)/shard_map/cores/ppermute | solution.py:26
  69.1 13.9 %collective-permute-start.16 = (bf16[192,1024]{1,0:T(8,128)(2,1)S(1)}, bf16[192,1024]{1,0:T(8,128)(2,1)S(1)}, u32[]{:S(2)}, u32[]{:S(2)}) collective-permute-start(bf16[192,1024]{1,0:T(8,128)(2,1)S(1)} %get-tuple-element.68), channel_id=1, source_target_pairs={{0,1},{1,0},{2,3},{3,2},{4,5},{5,4},{6,7},{7,6},{8,9},{9,8},{10,11... | collective-permute-start | bytes 1179656 | tf_op jit(solution)/shard_map/planes_last/ppermute | solution.py:30
  70.6 12.4 %collective-permute-start.17 = (bf16[192,1024]{1,0:T(8,128)(2,1)S(1)}, bf16[192,1024]{1,0:T(8,128)(2,1)S(1)}, u32[]{:S(2)}, u32[]{:S(2)}) collective-permute-start(bf16[192,1024]{1,0:T(8,128)(2,1)S(1)} %get-tuple-element.69), channel_id=1, source_target_pairs={{0,0},{1,2},{2,1},{3,3},{4,4},{5,6},{6,5},{7,7},{8,8},{9,10},{10,9... | collective-permute-start | bytes 1179656 | tf_op jit(solution)/shard_map/planes_last/ppermute | solution.py:38
  71.3 18.1 %collective-permute-start.13 = (bf16[192,1024]{1,0:T(8,128)(2,1)S(1)}, bf16[192,1024]{1,0:T(8,128)(2,1)S(1)}, u32[]{:S(2)}, u32[]{:S(2)}) collective-permute-start(bf16[192,1024]{1,0:T(8,128)(2,1)S(1)} %get-tuple-element.57), channel_id=1, source_target_pairs={{0,1},{1,0},{2,3},{3,2},{4,5},{5,4},{6,7},{7,6},{8,9},{9,8},{10,11... | collective-permute-start | bytes 1179656 | tf_op jit(solution)/shard_map/planes_last/ppermute | solution.py:30
  73.3 16.2 %collective-permute-start.14 = (bf16[192,1024]{1,0:T(8,128)(2,1)S(1)}, bf16[192,1024]{1,0:T(8,128)(2,1)S(1)}, u32[]{:S(2)}, u32[]{:S(2)}) collective-permute-start(bf16[192,1024]{1,0:T(8,128)(2,1)S(1)} %get-tuple-element.58), channel_id=1, source_target_pairs={{0,0},{1,2},{2,1},{3,3},{4,4},{5,6},{6,5},{7,7},{8,8},{9,10},{10,9... | collective-permute-start | bytes 1179656 | tf_op jit(solution)/shard_map/planes_last/ppermute | solution.py:38

commit v4 on v3

--- a/solution.py
+++ b/solution.py
@@ -72,23 +72,26 @@
         out[...] = features[:, pl.ds(start, block)]
 
 
-def share_kernel(*refs):
-    *parts, out = refs
+def share_kernel(parts, *refs):
     _, core, _ = place()
-    width = out.shape[2]
-    start = pl.multiple_of((1 - core) * width, LANES)
-    for index, part in enumerate(parts):
-        out[index] = part[:, pl.ds(start, width)]
-
-
-def rows_kernel(*refs):
-    *parts, shared, out = refs
+    outs = refs[parts:]
+    width = outs[0].shape[2]
+    for side, out in enumerate(outs):
+        start = pl.multiple_of(((1 - core) * len(outs) + side) * width, LANES)
+        for index, part in enumerate(refs[:parts]):
+            out[index] = part[:, pl.ds(start, width)]
+
+
+def rows_kernel(parts, *refs):
+    *shared, out = refs[parts:]
     _, core, _ = place()
-    local, width = shared.shape[1:]
-    begin = pl.multiple_of(core * width, LANES)
-    for index, part in enumerate(parts):
-        both = jnp.concatenate([part[:, pl.ds(begin, width)], shared[index]], axis=0)
-        out[index * 2 * local : (index + 1) * 2 * local, :] = both
+    local, width = shared[0].shape[1:]
+    begin = pl.multiple_of(core * out.shape[1], LANES)
+    for index, part in enumerate(refs[:parts]):
+        rows = pl.ds(index * 2 * local, 2 * local)
+        for side, other in enumerate(shared):
+            own = part[:, pl.ds(begin + side * width, width)]
+            out[rows, side * width : (side + 1) * width] = jnp.concatenate([own, other[index]], axis=0)
 
 
 def cut_kernel(arrays, *refs):
@@ -425,14 +428,15 @@
     to_rows, to_cols = dealt[:chips], dealt[chips:]
     col_parts = [to_cols[0]] + [swap_cols(to_cols[mask], mask) for mask in range(1, planes)]
     row_parts = [to_rows[0]] + [swap_rows(to_rows[mask], 2 * mask) for mask in range(1, chips)]
-    row_parts, col_parts = lax.optimization_barrier((row_parts, col_parts))
-    (shared,) = kernel(share_kernel, [((chips, local, block), half)], row_parts)
-    shared = swap_rows(shared, 1)
-
+    row_parts, col_parts[2] = lax.optimization_barrier((row_parts, col_parts[2]))
+    half_shape = (chips, local, block // 2)
+    shared = kernel(functools.partial(share_kernel, chips), [(half_shape, half)] * 2, row_parts)
+    shared = [swap_rows(part, 1) for part in shared]
+    shared, col_parts = lax.optimization_barrier((shared, col_parts))
+    (row_shard,) = kernel(functools.partial(rows_kernel, chips), [((rows * local, block), half)], [*row_parts, *shared])
     slice_width = block // planes
     cut = slice_width * (planes // 2)
     widths = (cut, block - cut)
-    (row_shard,) = kernel(rows_kernel, [((rows * local, block), half)], [*row_parts, shared])
     shard_shape = (planes, local, panel_width + LANES)
     col_parts = [part.reshape(1, *part.shape) for part in col_parts]
     (col_shard,) = kernel(stack_kernel, [(shard_shape, half)], col_parts)

time: 98.4 us -> 96.3 us (0.979)
  waiting for transfers between devices: 48.4 us -> 43.9 us
  starting transfers between devices: 22.5 us -> 25 us
    ppermute x9 -> x10, waiting for transfers between devices: 21 us -> 17.9 us  [swap_rows(): lax.ppermute(x, 'row', [(i, i ^ mask) for i in range(lax.axis_size('row'))])]
    ppermute x7, starting transfers between devices: 12.2 us -> 14.5 us  [swap_cols(): lax.ppermute(x, 'col', [(i, i ^ mask) for i in range(lax.axis_size('col'))])]
    ppermute x7, waiting for transfers between devices: 27.4 us -> 26 us  [swap_cols(): lax.ppermute(x, 'col', [(i, i ^ mask) for i in range(lax.axis_size('col'))])]
    ppermute x9 -> x10, starting transfers between devices: 8.78 us -> 8.92 us  [swap_rows(): lax.ppermute(x, 'row', [(i, i ^ mask) for i in range(lax.axis_size('row'))])]
  transfers between devices with their start and end apart: 18 -> 19, of which waited for: 8 -> 8; matrix products, arithmetic and copies ran while one was open for 0% -> 0% of each run, Pallas kernels for 15% -> 15%
where the time goes in v4:
time: 96.3 us; the launch traced here: 95.9 us
  waiting for transfers between devices  43.9 us (46%)
  starting transfers between devices  25 us (26%)
  Pallas kernels  24.3 us (25%)
  local copies, waits for them, and re-layouts  1.19 us (1%)
  between operations  0.97 us (1%)
    ppermute x7, waiting for transfers between devices, swap_cols(): lax.ppermute(x, 'col', [(i, i ^ mask) for i in range(lax.axis_size('col'))])  26 us
    ppermute x10, waiting for transfers between devices, swap_rows(): lax.ppermute(x, 'row', [(i, i ^ mask) for i in range(lax.axis_size('row'))])  17.9 us
    ppermute x7, starting transfers between devices, swap_cols(): lax.ppermute(x, 'col', [(i, i ^ mask) for i in range(lax.axis_size('col'))])  14.5 us
    pallas_call x8, Pallas kernels, kernel(): pl.pallas_call(body, out_shape=[jax.ShapeDtypeStruct(shape, dtype) for sh...  9.41 us
    ppermute x10, starting transfers between devices, swap_rows(): lax.ppermute(x, 'row', [(i, i ^ mask) for i in range(lax.axis_size('row'))])  8.92 us
    pallas_call x1, Pallas kernels, gram(): pl.pallas_call(functools.partial(gram_kernel, tuple(map(len, groups)), fi...  8.41 us
    pallas_call x1, Pallas kernels, late(): pl.pallas_call(functools.partial(late_kernel, (len(parts), len(last)), fi...  6.44 us
  transfers between devices with their start and end apart: 19, of which 8 were waited for; matrix products, arithmetic and copies ran while one was open for 0% of the time, Pallas kernels for 15%

profile of v4, /device:TPU:0, one launch (start us, length us, event | category | flops | bytes accessed | tf_op | source)
XLA Modules:
  0.0 95.9 jit_solution(4345526598883965749)
XLA Ops:
  0.6 0.7 multiply_add_fusion.codes_hbm
  1.3 1.1 %copy-done = bf16[24,16384]{1,0:T(8,128)(2,1)S(1)} copy-done((bf16[24,16384]{1,0:T(8,128)(2,1)S(1)}, bf16[24,16384]{1,0:T(8,128)(2,1)}, u32[]{:S(2)}) %copy-start) | copy-done | bytes 786456
  2.4 0.7 shard_map.50
  3.2 4.1 %collective-permute-start.3 = (bf16[24,4224]{1,0:T(8,128)(2,1)S(1)}, bf16[24,4224]{1,0:T(8,128)(2,1)S(1)}, u32[]{:S(2)}, u32[]{:S(2)}) collective-permute-start(bf16[24,4224]{1,0:T(8,128)(2,1)S(1)} %get-tuple-element.47), channel_id=1, source_target_pairs={{0,2},{1,3},{2,0},{3,1},{4,6},{5,7},{6,4},{7,5},{8,10},{9,11},{10,... | collective-permute-start | bytes 608264 | tf_op jit(solution)/shard_map/ppermute | solution.py:30
  7.3 1.5 %collective-permute-start = (bf16[24,4096]{1,0:T(8,128)(2,1)S(1)}, bf16[24,4096]{1,0:T(8,128)(2,1)S(1)}, u32[]{:S(2)}, u32[]{:S(2)}) collective-permute-start(bf16[24,4096]{1,0:T(8,128)(2,1)S(1)} %get-tuple-element.44), channel_id=1, source_target_pairs={{0,8},{4,12},{8,0},{12,4},{16,24},{20,28},{24,16},{28,20},{1,9},{5... | collective-permute-start | bytes 589832 | tf_op jit(solution)/shard_map/ppermute | solution.py:26
  8.8 1.5 %collective-permute-start.1 = (bf16[24,4096]{1,0:T(8,128)(2,1)S(1)}, bf16[24,4096]{1,0:T(8,128)(2,1)S(1)}, u32[]{:S(2)}, u32[]{:S(2)}) collective-permute-start(bf16[24,4096]{1,0:T(8,128)(2,1)S(1)} %get-tuple-element.45), channel_id=1, source_target_pairs={{0,16},{4,20},{8,24},{12,28},{16,0},{20,4},{24,8},{28,12},{1,17},{... | collective-permute-start | bytes 589832 | tf_op jit(solution)/shard_map/ppermute | solution.py:26
  10.3 0.5 collective-permute-start.2
  10.8 1.6 %collective-permute-start.6 = (bf16[24,4224]{1,0:T(8,128)(2,1)S(1)}, bf16[24,4224]{1,0:T(8,128)(2,1)S(1)}, u32[]{:S(2)}, u32[]{:S(2)}) collective-permute-start(bf16[24,4224]{1,0:T(8,128)(2,1)S(1)} %get-tuple-element.55), channel_id=1, source_target_pairs={{0,1},{1,0},{2,3},{3,2},{4,5},{5,4},{6,7},{7,6},{8,9},{9,8},{10,11... | collective-permute-start | bytes 608264 | tf_op jit(solution)/shard_map/ppermute | solution.py:30
  12.3 2.8 %collective-permute-done.refs_1_ = bf16[24,4096]{1,0:T(8,128)(2,1)S(1)} collective-permute-done((bf16[24,4096]{1,0:T(8,128)(2,1)S(1)}, bf16[24,4096]{1,0:T(8,128)(2,1)S(1)}, u32[]{:S(2)}, u32[]{:S(2)}) %collective-permute-start) | collective-permute-done | bytes 196640 | tf_op jit(solution)/shard_map/ppermute | solution.py:26
  15.1 1.3 %collective-permute-start.7 = (bf16[24,4224]{1,0:T(8,128)(2,1)S(1)}, bf16[24,4224]{1,0:T(8,128)(2,1)S(1)}, u32[]{:S(2)}, u32[]{:S(2)}) collective-permute-start(bf16[24,4224]{1,0:T(8,128)(2,1)S(1)} %get-tuple-element.57), channel_id=1, source_target_pairs={{0,3},{1,2},{2,1},{3,0},{4,7},{5,6},{6,5},{7,4},{8,11},{9,10},{10,... | collective-permute-start | bytes 608264 | tf_op jit(solution)/shard_map/ppermute | solution.py:30
  16.4 2.6 %collective-permute-done.1.refs_2_ = bf16[24,4096]{1,0:T(8,128)(2,1)S(1)} collective-permute-done((bf16[24,4096]{1,0:T(8,128)(2,1)S(1)}, bf16[24,4096]{1,0:T(8,128)(2,1)S(1)}, u32[]{:S(2)}, u32[]{:S(2)}) %collective-permute-start.1) | collective-permute-done | bytes 196640 | tf_op jit(solution)/shard_map/ppermute | solution.py:26
  19.2 0.5 collective-permute-start.5
  19.7 4.3 %collective-permute-done.6 = bf16[24,4224]{1,0:T(8,128)(2,1)S(1)} collective-permute-done((bf16[24,4224]{1,0:T(8,128)(2,1)S(1)}, bf16[24,4224]{1,0:T(8,128)(2,1)S(1)}, u32[]{:S(2)}, u32[]{:S(2)}) %collective-permute-start.6) | collective-permute-done | bytes 202784 | tf_op jit(solution)/shard_map/ppermute | solution.py:30
  24.0 1.6 %collective-permute-start.9 = (bf16[4,24,4224]{2,1,0:T(8,128)(2,1)S(1)}, bf16[4,24,4224]{2,1,0:T(8,128)(2,1)S(1)}, u32[]{:S(2)}, u32[]{:S(2)}) collective-permute-start(bf16[4,24,4224]{2,1,0:T(8,128)(2,1)S(1)} %shard_map.52.refs_0_), channel_id=1, source_target_pairs={{0,16},{4,20},{8,24},{12,28},{16,0},{20,4},{24,8},{28,12},{1,17},{... | collective-permute-start | bytes 2433032 | tf_op jit(solution)/shard_map/chips/ppermute | solution.py:26
  25.7 1.5 %collective-permute-start.8 = (bf16[4,24,4224]{2,1,0:T(8,128)(2,1)S(1)}, bf16[4,24,4224]{2,1,0:T(8,128)(2,1)S(1)}, u32[]{:S(2)}, u32[]{:S(2)}) collective-permute-start(bf16[4,24,4224]{2,1,0:T(8,128)(2,1)S(1)} %shard_map.52.refs_0_), channel_id=1, source_target_pairs={{0,8},{4,12},{8,0},{12,4},{16,24},{20,28},{24,16},{28,20},{1,9},{5... | collective-permute-start | bytes 2433032 | tf_op jit(solution)/shard_map/chips/ppermute | solution.py:26
  27.2 4.1 %collective-permute-start.13 = (bf16[192,2048]{1,0:T(8,128)(2,1)S(1)}, bf16[192,2048]{1,0:T(8,128)(2,1)S(1)}, u32[]{:S(2)}, u32[]{:S(2)}) collective-permute-start(bf16[192,2048]{1,0:T(8,128)(2,1)S(1)} %shard_map.53.refs_0_), channel_id=1, source_target_pairs={{0,2},{1,3},{2,0},{3,1},{4,6},{5,7},{6,4},{7,5},{8,10},{9,11},{10,... | collective-permute-start | bytes 2359304 | tf_op jit(solution)/shard_map/planes_far/ppermute | solution.py:30
  31.3 10.0 %collective-permute-done.9.refs_2_ = bf16[4,24,4224]{2,1,0:T(8,128)(2,1)S(1)} collective-permute-done((bf16[4,24,4224]{2,1,0:T(8,128)(2,1)S(1)}, bf16[4,24,4224]{2,1,0:T(8,128)(2,1)S(1)}, u32[]{:S(2)}, u32[]{:S(2)}) %collective-permute-start.9) | collective-permute-done | bytes 811040 | tf_op jit(solution)/shard_map/chips/ppermute | solution.py:26
  41.3 1.6 %collective-permute-start.10 = (bf16[2,24,4224]{2,1,0:T(8,128)(2,1)S(1)}, bf16[2,24,4224]{2,1,0:T(8,128)(2,1)S(1)}, u32[]{:S(2)}, u32[]{:S(2)}) collective-permute-start(bf16[2,24,4224]{2,1,0:T(8,128)(2,1)S(1)} %slice.8), channel_id=1, source_target_pairs={{0,8},{4,12},{8,0},{12,4},{16,24},{20,28},{24,16},{28,20},{1,9},{5... | collective-permute-start | bytes 1216520 | tf_op jit(solution)/shard_map/chips/ppermute | solution.py:26
  42.9 1.8 %collective-permute-done.8.refs_1_ = bf16[4,24,4224]{2,1,0:T(8,128)(2,1)S(1)} collective-permute-done((bf16[4,24,4224]{2,1,0:T(8,128)(2,1)S(1)}, bf16[4,24,4224]{2,1,0:T(8,128)(2,1)S(1)}, u32[]{:S(2)}, u32[]{:S(2)}) %collective-permute-start.8) | collective-permute-done | bytes 811040 | tf_op jit(solution)/shard_map/chips/ppermute | solution.py:26
  44.8 20.6 %collective-permute-done.13.refs_1_.refs_2_ = bf16[192,2048]{1,0:T(8,128)(2,1)S(1)} collective-permute-done((bf16[192,2048]{1,0:T(8,128)(2,1)S(1)}, bf16[192,2048]{1,0:T(8,128)(2,1)S(1)}, u32[]{:S(2)}, u32[]{:S(2)}) %collective-permute-start.13) | collective-permute-done | bytes 786464 | tf_op jit(solution)/shard_map/planes_far/ppermute | solution.py:30
  65.4 1.1 %collective-permute-done.12.refs_1_ = bf16[192,2048]{1,0:T(8,128)(2,1)S(1)} collective-permute-done((bf16[192,2048]{1,0:T(8,128)(2,1)S(1)}, bf16[192,2048]{1,0:T(8,128)(2,1)S(1)}, u32[]{:S(2)}, u32[]{:S(2)}) %collective-permute-start.12) | collective-permute-done | bytes 786464 | tf_op jit(solution)/shard_map/planes_near/ppermute | solution.py:30
  66.5 0.2 shard_map.55.refs_0_
  66.8 0.1 shard_map.54
  66.9 0.7 collective-permute-start.17
  67.6 0.7 collective-permute-start.18
  68.3 2.7 %collective-permute-start.14 = (bf16[192,1024]{1,0:T(8,128)(2,1)S(1)}, bf16[192,1024]{1,0:T(8,128)(2,1)S(1)}, u32[]{:S(2)}, u32[]{:S(2)}) collective-permute-start(bf16[192,1024]{1,0:T(8,128)(2,1)S(1)} %get-tuple-element.67), channel_id=1, source_target_pairs={{0,1},{1,0},{2,3},{3,2},{4,5},{5,4},{6,7},{7,6},{8,9},{9,8},{10,11... | collective-permute-start | bytes 1179656 | tf_op jit(solution)/shard_map/planes_last/ppermute | solution.py:30
  71.0 0.9 collective-permute-start.15
  71.9 0.7 collective-permute-done.16.refs_1_
  72.6 1.1 %shard_map.56 = (bf16[768,4096]{1,0:T(8,128)(2,1)S(1)}, f32[8,4096]{1,0:T(8,128)S(1)}, bf16[768,128]{1,0:T(8,128)(2,1)S(1)}, f32[128,128]{1,0:T(8,128)S(1)}) custom-call(bf16[16,24,4224]{2,1,0:T(8,128)(2,1)S(1)} %shard_map.55.refs_0_, bf16[16,24,4224]{2,1,0:T(8,128)(2,1)S(1)} %collective-permute-done.16.refs_1_), custom_call_target="tpu_custom_call" | custom-call | tf_op jit(solution)/shard_map/pallas_call | solution.py:358
  73.8 7.1 %shard_map.57 = (f32[1024,4096]{1,0:T(8,128)S(1)}, f32[1024,128]{1,0:T(8,128)S(1)}) custom-call(bf16[192,2048]{1,0:T(8,128)(2,1)S(1)} %shard_map.53.refs_0_, bf16[192,2048]{1,0:T(8,128)(2,1)S(1)} %collective-permute-done.12.refs_1_, bf16[192,2048]{1,0:T(8,128)(2,1)S(1)} %collective-permute-done.13.refs_1_.refs_2_, ...), custom_call_target="tpu_custom_call" | custom-call | tf_op jit(solution)/shard_map/pallas_call | solution.py:358
  80.9 6.4 %shard_map.58 = (f32[2048,4096]{1,0:T(8,128)}, f32[128,512]{1,0:T(8,128)}) custom-call(bf16[192,2048]{1,0:T(8,128)(2,1)S(1)} %shard_map.53.refs_0_, bf16[192,2048]{1,0:T(8,128)(2,1)S(1)} %collective-permute-done.12.refs_1_, bf16[192,2048]{1,0:T(8,128)(2,1)S(1)} %collective-permute-done.13.refs_1_.refs_2_, ...), custom_call_target="tpu_custom_call" | custom-call | bytes 2097152 | tf_op jit(solution)/shard_map/pallas_call | solution.py:339
  87.3 8.4 %shard_map.59 = (f32[2048,4096]{1,0:T(8,128)}, f32[128,512]{1,0:T(8,128)}) custom-call(bf16[192,2048]{1,0:T(8,128)(2,1)S(1)} %shard_map.53.refs_0_, bf16[192,2048]{1,0:T(8,128)(2,1)S(1)} %collective-permute-done.12.refs_1_, bf16[192,2048]{1,0:T(8,128)(2,1)S(1)} %collective-permute-done.13.refs_1_.refs_2_, ...), custom_call_target="tpu_custom_call", output_to_operand_aliasing={{0}: (9, {}), {1}: (10, {})} | custom-call | bytes 2097152 | tf_op jit(solution)/shard_map/pallas_call | solution.py:217
  (21 shorter events, 0.5 us)
Async XLA Ops:
  1.3 1.1 %copy-start = (bf16[24,16384]{1,0:T(8,128)(2,1)S(1)}, bf16[24,16384]{1,0:T(8,128)(2,1)}, u32[]{:S(2)}) copy-start(bf16[24,16384]{1,0:T(8,128)(2,1)} %features_hbm.1) | copy-start | bytes 2359300
  3.2 15.9 %collective-permute-start.3 = (bf16[24,4224]{1,0:T(8,128)(2,1)S(1)}, bf16[24,4224]{1,0:T(8,128)(2,1)S(1)}, u32[]{:S(2)}, u32[]{:S(2)}) collective-permute-start(bf16[24,4224]{1,0:T(8,128)(2,1)S(1)} %get-tuple-element.47), channel_id=1, source_target_pairs={{0,2},{1,3},{2,0},{3,1},{4,6},{5,7},{6,4},{7,5},{8,10},{9,11},{10,... | collective-permute-start | bytes 608264 | tf_op jit(solution)/shard_map/ppermute | solution.py:30
  7.3 7.8 %collective-permute-start = (bf16[24,4096]{1,0:T(8,128)(2,1)S(1)}, bf16[24,4096]{1,0:T(8,128)(2,1)S(1)}, u32[]{:S(2)}, u32[]{:S(2)}) collective-permute-start(bf16[24,4096]{1,0:T(8,128)(2,1)S(1)} %get-tuple-element.44), channel_id=1, source_target_pairs={{0,8},{4,12},{8,0},{12,4},{16,24},{20,28},{24,16},{28,20},{1,9},{5... | collective-permute-start | bytes 589832 | tf_op jit(solution)/shard_map/ppermute | solution.py:26
  8.8 10.3 %collective-permute-start.1 = (bf16[24,4096]{1,0:T(8,128)(2,1)S(1)}, bf16[24,4096]{1,0:T(8,128)(2,1)S(1)}, u32[]{:S(2)}, u32[]{:S(2)}) collective-permute-start(bf16[24,4096]{1,0:T(8,128)(2,1)S(1)} %get-tuple-element.45), channel_id=1, source_target_pairs={{0,16},{4,20},{8,24},{12,28},{16,0},{20,4},{24,8},{28,12},{1,17},{... | collective-permute-start | bytes 589832 | tf_op jit(solution)/shard_map/ppermute | solution.py:26
  10.3 8.8 %collective-permute-start.2 = (bf16[24,4096]{1,0:T(8,128)(2,1)S(1)}, bf16[24,4096]{1,0:T(8,128)(2,1)S(1)}, u32[]{:S(2)}, u32[]{:S(2)}) collective-permute-start(bf16[24,4096]{1,0:T(8,128)(2,1)S(1)} %get-tuple-element.46), channel_id=1, source_target_pairs={{0,24},{4,28},{8,16},{12,20},{16,8},{20,12},{24,0},{28,4},{1,25},{... | collective-permute-start | bytes 589832 | tf_op jit(solution)/shard_map/ppermute | solution.py:26
  10.8 13.2 %collective-permute-start.6 = (bf16[24,4224]{1,0:T(8,128)(2,1)S(1)}, bf16[24,4224]{1,0:T(8,128)(2,1)S(1)}, u32[]{:S(2)}, u32[]{:S(2)}) collective-permute-start(bf16[24,4224]{1,0:T(8,128)(2,1)S(1)} %get-tuple-element.55), channel_id=1, source_target_pairs={{0,1},{1,0},{2,3},{3,2},{4,5},{5,4},{6,7},{7,6},{8,9},{9,8},{10,11... | collective-permute-start | bytes 608264 | tf_op jit(solution)/shard_map/ppermute | solution.py:30
  15.1 8.8 %collective-permute-start.7 = (bf16[24,4224]{1,0:T(8,128)(2,1)S(1)}, bf16[24,4224]{1,0:T(8,128)(2,1)S(1)}, u32[]{:S(2)}, u32[]{:S(2)}) collective-permute-start(bf16[24,4224]{1,0:T(8,128)(2,1)S(1)} %get-tuple-element.57), channel_id=1, source_target_pairs={{0,3},{1,2},{2,1},{3,0},{4,7},{5,6},{6,5},{7,4},{8,11},{9,10},{10,... | collective-permute-start | bytes 608264 | tf_op jit(solution)/shard_map/ppermute | solution.py:30
  19.1 4.8 %collective-permute-start.4 = (bf16[4,24,1024]{2,1,0:T(8,128)(2,1)S(1)}, bf16[4,24,1024]{2,1,0:T(8,128)(2,1)S(1)}, u32[]{:S(2)}, u32[]{:S(2)}) collective-permute-start(bf16[4,24,1024]{2,1,0:T(8,128)(2,1)S(1)} %get-tuple-element.52), channel_id=1, source_target_pairs={{0,4},{4,0},{8,12},{12,8},{16,20},{20,16},{24,28},{28,24},{1,5},{5... | collective-permute-start | bytes 589832 | tf_op jit(solution)/shard_map/ppermute | solution.py:26
  19.2 4.8 %collective-permute-start.5 = (bf16[4,24,1024]{2,1,0:T(8,128)(2,1)S(1)}, bf16[4,24,1024]{2,1,0:T(8,128)(2,1)S(1)}, u32[]{:S(2)}, u32[]{:S(2)}) collective-permute-start(bf16[4,24,1024]{2,1,0:T(8,128)(2,1)S(1)} %get-tuple-element.53), channel_id=1, source_target_pairs={{0,4},{4,0},{8,12},{12,8},{16,20},{20,16},{24,28},{28,24},{1,5},{5... | collective-permute-start | bytes 589832 | tf_op jit(solution)/shard_map/ppermute | solution.py:26
  24.0 17.3 %collective-permute-start.9 = (bf16[4,24,4224]{2,1,0:T(8,128)(2,1)S(1)}, bf16[4,24,4224]{2,1,0:T(8,128)(2,1)S(1)}, u32[]{:S(2)}, u32[]{:S(2)}) collective-permute-start(bf16[4,24,4224]{2,1,0:T(8,128)(2,1)S(1)} %shard_map.52.refs_0_), channel_id=1, source_target_pairs={{0,16},{4,20},{8,24},{12,28},{16,0},{20,4},{24,8},{28,12},{1,17},{... | collective-permute-start | bytes 2433032 | tf_op jit(solution)/shard_map/chips/ppermute | solution.py:26
  25.7 19.0 %collective-permute-start.8 = (bf16[4,24,4224]{2,1,0:T(8,128)(2,1)S(1)}, bf16[4,24,4224]{2,1,0:T(8,128)(2,1)S(1)}, u32[]{:S(2)}, u32[]{:S(2)}) collective-permute-start(bf16[4,24,4224]{2,1,0:T(8,128)(2,1)S(1)} %shard_map.52.refs_0_), channel_id=1, source_target_pairs={{0,8},{4,12},{8,0},{12,4},{16,24},{20,28},{24,16},{28,20},{1,9},{5... | collective-permute-start | bytes 2433032 | tf_op jit(solution)/shard_map/chips/ppermute | solution.py:26
  27.2 38.2 %collective-permute-start.13 = (bf16[192,2048]{1,0:T(8,128)(2,1)S(1)}, bf16[192,2048]{1,0:T(8,128)(2,1)S(1)}, u32[]{:S(2)}, u32[]{:S(2)}) collective-permute-start(bf16[192,2048]{1,0:T(8,128)(2,1)S(1)} %shard_map.53.refs_0_), channel_id=1, source_target_pairs={{0,2},{1,3},{2,0},{3,1},{4,6},{5,7},{6,4},{7,5},{8,10},{9,11},{10,... | collective-permute-start | bytes 2359304 | tf_op jit(solution)/shard_map/planes_far/ppermute | solution.py:30
  31.3 35.2 %collective-permute-start.12 = (bf16[192,2048]{1,0:T(8,128)(2,1)S(1)}, bf16[192,2048]{1,0:T(8,128)(2,1)S(1)}, u32[]{:S(2)}, u32[]{:S(2)}) collective-permute-start(bf16[192,2048]{1,0:T(8,128)(2,1)S(1)} %shard_map.53.refs_0_), channel_id=1, source_target_pairs={{0,1},{1,0},{2,3},{3,2},{4,5},{5,4},{6,7},{7,6},{8,9},{9,8},{10,11... | collective-permute-start | bytes 2359304 | tf_op jit(solution)/shard_map/planes_near/ppermute | solution.py:30
  41.3 25.2 %collective-permute-start.10 = (bf16[2,24,4224]{2,1,0:T(8,128)(2,1)S(1)}, bf16[2,24,4224]{2,1,0:T(8,128)(2,1)S(1)}, u32[]{:S(2)}, u32[]{:S(2)}) collective-permute-start(bf16[2,24,4224]{2,1,0:T(8,128)(2,1)S(1)} %slice.8), channel_id=1, source_target_pairs={{0,8},{4,12},{8,0},{12,4},{16,24},{20,28},{24,16},{28,20},{1,9},{5... | collective-permute-start | bytes 1216520 | tf_op jit(solution)/shard_map/chips/ppermute | solution.py:26
  44.7 21.8 %collective-permute-start.11 = (bf16[2,24,4224]{2,1,0:T(8,128)(2,1)S(1)}, bf16[2,24,4224]{2,1,0:T(8,128)(2,1)S(1)}, u32[]{:S(2)}, u32[]{:S(2)}) collective-permute-start(bf16[2,24,4224]{2,1,0:T(8,128)(2,1)S(1)} %slice.9), channel_id=1, source_target_pairs={{0,16},{4,20},{8,24},{12,28},{16,0},{20,4},{24,8},{28,12},{1,17},{... | collective-permute-start | bytes 1216520 | tf_op jit(solution)/shard_map/chips/ppermute | solution.py:26
  66.8 5.9 %collective-permute-start.16 = (bf16[16,24,4224]{2,1,0:T(8,128)(2,1)S(1)}, bf16[16,24,4224]{2,1,0:T(8,128)(2,1)S(1)}, u32[]{:S(2)}, u32[]{:S(2)}) collective-permute-start(bf16[16,24,4224]{2,1,0:T(8,128)(2,1)S(1)} %shard_map.55.refs_0_), channel_id=1, source_target_pairs={{0,4},{4,0},{8,12},{12,8},{16,20},{20,16},{24,28},{28,24},{1,5},{5... | collective-permute-start | bytes 9732104 | tf_op jit(solution)/shard_map/cores/ppermute | solution.py:26
  66.9 13.9 %collective-permute-start.17 = (bf16[192,1024]{1,0:T(8,128)(2,1)S(1)}, bf16[192,1024]{1,0:T(8,128)(2,1)S(1)}, u32[]{:S(2)}, u32[]{:S(2)}) collective-permute-start(bf16[192,1024]{1,0:T(8,128)(2,1)S(1)} %get-tuple-element.78), channel_id=1, source_target_pairs={{0,1},{1,0},{2,3},{3,2},{4,5},{5,4},{6,7},{7,6},{8,9},{9,8},{10,11... | collective-permute-start | bytes 1179656 | tf_op jit(solution)/shard_map/planes_last/ppermute | solution.py:30
  67.6 13.3 %collective-permute-start.18 = (bf16[192,1024]{1,0:T(8,128)(2,1)S(1)}, bf16[192,1024]{1,0:T(8,128)(2,1)S(1)}, u32[]{:S(2)}, u32[]{:S(2)}) collective-permute-start(bf16[192,1024]{1,0:T(8,128)(2,1)S(1)} %get-tuple-element.79), channel_id=1, source_target_pairs={{0,0},{1,2},{2,1},{3,3},{4,4},{5,6},{6,5},{7,7},{8,8},{9,10},{10,9... | collective-permute-start | bytes 1179656 | tf_op jit(solution)/shard_map/planes_last/ppermute | solution.py:38
  68.3 19.1 %collective-permute-start.14 = (bf16[192,1024]{1,0:T(8,128)(2,1)S(1)}, bf16[192,1024]{1,0:T(8,128)(2,1)S(1)}, u32[]{:S(2)}, u32[]{:S(2)}) collective-permute-start(bf16[192,1024]{1,0:T(8,128)(2,1)S(1)} %get-tuple-element.67), channel_id=1, source_target_pairs={{0,1},{1,0},{2,3},{3,2},{4,5},{5,4},{6,7},{7,6},{8,9},{9,8},{10,11... | collective-permute-start | bytes 1179656 | tf_op jit(solution)/shard_map/planes_last/ppermute | solution.py:30
  71.0 16.3 %collective-permute-start.15 = (bf16[192,1024]{1,0:T(8,128)(2,1)S(1)}, bf16[192,1024]{1,0:T(8,128)(2,1)S(1)}, u32[]{:S(2)}, u32[]{:S(2)}) collective-permute-start(bf16[192,1024]{1,0:T(8,128)(2,1)S(1)} %get-tuple-element.68), channel_id=1, source_target_pairs={{0,0},{1,2},{2,1},{3,3},{4,4},{5,6},{6,5},{7,7},{8,8},{9,10},{10,9... | collective-permute-start | bytes 1179656 | tf_op jit(solution)/shard_map/planes_last/ppermute | solution.py:38

commit v5 on v4

--- a/solution.py
+++ b/solution.py
@@ -236,7 +236,7 @@
     *parts, panel, acc, sums, left_ref = refs
     width, depth = left_ref.shape
     columns = panel.shape[1]
-    chunk = min(1024, columns)
+    chunk = min(2048, columns)
     ones = jnp.ones((depth, LANES), jnp.bfloat16)
     for start in range(0, width, tile):
         rows = pl.ds(start, tile)
@@ -327,7 +327,7 @@
     width = acc.shape[0]
     tile = min(256, width)
     chunk = min(1024, columns)
-    slots = min(8, width // tile * (columns // chunk))
+    slots = min(12, width // tile * (columns // chunk))
     inputs = [*parts, *last, acc, sums, panel, mean, member, counts]
     specs = [WHOLE] * len(inputs)
     aliases = {}
@@ -349,7 +349,7 @@
             pltpu.SemaphoreType.DMA,
         ],
         input_output_aliases=aliases,
-        compiler_params=params(14),
+        compiler_params=params(18),
         cost_estimate=pl.CostEstimate(flops=0, bytes_accessed=2 * MIB, transcendentals=0),
     )(*inputs)
 

time: 96.3 us -> 108 us (1.12)
  local copies, waits for them, and re-layouts: 1.19 us -> 13.1 us
    unnamed x2 -> x6, local copies, waits for them, and re-layouts: 1.13 us -> 13.1 us
  transfers between devices with their start and end apart: 19 -> 19, of which waited for: 8 -> 8; matrix products, arithmetic and copies ran while one was open for 0% -> 0% of each run, Pallas kernels for 15% -> 14%
where the time goes in v5:
time: 108 us
  waiting for transfers between devices  43.9 us (41%)
  starting transfers between devices  25 us (23%)
  Pallas kernels  24.3 us (22%)
  local copies, waits for them, and re-layouts  13.1 us (12%)
    ppermute x7, waiting for transfers between devices, swap_cols(): lax.ppermute(x, 'col', [(i, i ^ mask) for i in range(lax.axis_size('col'))])  26 us
    ppermute x10, waiting for transfers between devices, swap_rows(): lax.ppermute(x, 'row', [(i, i ^ mask) for i in range(lax.axis_size('row'))])  17.9 us
    ppermute x7, starting transfers between devices, swap_cols(): lax.ppermute(x, 'col', [(i, i ^ mask) for i in range(lax.axis_size('col'))])  14.5 us
    unnamed x6, local copies, waits for them, and re-layouts  13.1 us
    pallas_call x8, Pallas kernels, kernel(): pl.pallas_call(body, out_shape=[jax.ShapeDtypeStruct(shape, dtype) for sh...  9.41 us
    ppermute x10, starting transfers between devices, swap_rows(): lax.ppermute(x, 'row', [(i, i ^ mask) for i in range(lax.axis_size('row'))])  8.92 us
    pallas_call x1, Pallas kernels, gram(): pl.pallas_call(functools.partial(gram_kernel, tuple(map(len, groups)), fi...  8.41 us
    pallas_call x1, Pallas kernels, late(): pl.pallas_call(functools.partial(late_kernel, (len(parts), len(last)), fi...  6.49 us
  transfers between devices with their start and end apart: 19, of which 8 were waited for; matrix products, arithmetic and copies ran while one was open for 0% of the time, Pallas kernels for 14%

profile of v5, /device:TPU:0, one launch (start us, length us, event | category | flops | bytes accessed | tf_op | source)
XLA Modules:
  0.0 107.9 jit_solution(15134734750684925)
XLA Ops:
  0.6 0.7 multiply_add_fusion.codes_hbm
  1.3 1.1 %copy-done.2 = bf16[24,16384]{1,0:T(8,128)(2,1)S(1)} copy-done((bf16[24,16384]{1,0:T(8,128)(2,1)S(1)}, bf16[24,16384]{1,0:T(8,128)(2,1)}, u32[]{:S(2)}) %copy-start.2) | copy-done | bytes 786456
  2.4 0.7 shard_map.50
  3.2 4.1 %collective-permute-start.3 = (bf16[24,4224]{1,0:T(8,128)(2,1)S(1)}, bf16[24,4224]{1,0:T(8,128)(2,1)S(1)}, u32[]{:S(2)}, u32[]{:S(2)}) collective-permute-start(bf16[24,4224]{1,0:T(8,128)(2,1)S(1)} %get-tuple-element.47), channel_id=1, source_target_pairs={{0,2},{1,3},{2,0},{3,1},{4,6},{5,7},{6,4},{7,5},{8,10},{9,11},{10,... | collective-permute-start | bytes 608264 | tf_op jit(solution)/shard_map/ppermute | solution.py:30
  7.3 1.5 %collective-permute-start = (bf16[24,4096]{1,0:T(8,128)(2,1)S(1)}, bf16[24,4096]{1,0:T(8,128)(2,1)S(1)}, u32[]{:S(2)}, u32[]{:S(2)}) collective-permute-start(bf16[24,4096]{1,0:T(8,128)(2,1)S(1)} %get-tuple-element.44), channel_id=1, source_target_pairs={{0,8},{4,12},{8,0},{12,4},{16,24},{20,28},{24,16},{28,20},{1,9},{5... | collective-permute-start | bytes 589832 | tf_op jit(solution)/shard_map/ppermute | solution.py:26
  8.8 1.5 %collective-permute-start.1 = (bf16[24,4096]{1,0:T(8,128)(2,1)S(1)}, bf16[24,4096]{1,0:T(8,128)(2,1)S(1)}, u32[]{:S(2)}, u32[]{:S(2)}) collective-permute-start(bf16[24,4096]{1,0:T(8,128)(2,1)S(1)} %get-tuple-element.45), channel_id=1, source_target_pairs={{0,16},{4,20},{8,24},{12,28},{16,0},{20,4},{24,8},{28,12},{1,17},{... | collective-permute-start | bytes 589832 | tf_op jit(solution)/shard_map/ppermute | solution.py:26
  10.3 0.5 collective-permute-start.2
  10.8 1.6 %collective-permute-start.6 = (bf16[24,4224]{1,0:T(8,128)(2,1)S(1)}, bf16[24,4224]{1,0:T(8,128)(2,1)S(1)}, u32[]{:S(2)}, u32[]{:S(2)}) collective-permute-start(bf16[24,4224]{1,0:T(8,128)(2,1)S(1)} %get-tuple-element.55), channel_id=1, source_target_pairs={{0,1},{1,0},{2,3},{3,2},{4,5},{5,4},{6,7},{7,6},{8,9},{9,8},{10,11... | collective-permute-start | bytes 608264 | tf_op jit(solution)/shard_map/ppermute | solution.py:30
  12.3 2.8 %collective-permute-done.refs_1_ = bf16[24,4096]{1,0:T(8,128)(2,1)S(1)} collective-permute-done((bf16[24,4096]{1,0:T(8,128)(2,1)S(1)}, bf16[24,4096]{1,0:T(8,128)(2,1)S(1)}, u32[]{:S(2)}, u32[]{:S(2)}) %collective-permute-start) | collective-permute-done | bytes 196640 | tf_op jit(solution)/shard_map/ppermute | solution.py:26
  15.1 1.3 %collective-permute-start.7 = (bf16[24,4224]{1,0:T(8,128)(2,1)S(1)}, bf16[24,4224]{1,0:T(8,128)(2,1)S(1)}, u32[]{:S(2)}, u32[]{:S(2)}) collective-permute-start(bf16[24,4224]{1,0:T(8,128)(2,1)S(1)} %get-tuple-element.57), channel_id=1, source_target_pairs={{0,3},{1,2},{2,1},{3,0},{4,7},{5,6},{6,5},{7,4},{8,11},{9,10},{10,... | collective-permute-start | bytes 608264 | tf_op jit(solution)/shard_map/ppermute | solution.py:30
  16.4 2.6 %collective-permute-done.1.refs_2_ = bf16[24,4096]{1,0:T(8,128)(2,1)S(1)} collective-permute-done((bf16[24,4096]{1,0:T(8,128)(2,1)S(1)}, bf16[24,4096]{1,0:T(8,128)(2,1)S(1)}, u32[]{:S(2)}, u32[]{:S(2)}) %collective-permute-start.1) | collective-permute-done | bytes 196640 | tf_op jit(solution)/shard_map/ppermute | solution.py:26
  19.2 0.5 collective-permute-start.5
  19.7 4.3 %collective-permute-done.6 = bf16[24,4224]{1,0:T(8,128)(2,1)S(1)} collective-permute-done((bf16[24,4224]{1,0:T(8,128)(2,1)S(1)}, bf16[24,4224]{1,0:T(8,128)(2,1)S(1)}, u32[]{:S(2)}, u32[]{:S(2)}) %collective-permute-start.6) | collective-permute-done | bytes 202784 | tf_op jit(solution)/shard_map/ppermute | solution.py:30
  24.0 1.6 %collective-permute-start.9 = (bf16[4,24,4224]{2,1,0:T(8,128)(2,1)S(1)}, bf16[4,24,4224]{2,1,0:T(8,128)(2,1)S(1)}, u32[]{:S(2)}, u32[]{:S(2)}) collective-permute-start(bf16[4,24,4224]{2,1,0:T(8,128)(2,1)S(1)} %shard_map.52.refs_0_), channel_id=1, source_target_pairs={{0,16},{4,20},{8,24},{12,28},{16,0},{20,4},{24,8},{28,12},{1,17},{... | collective-permute-start | bytes 2433032 | tf_op jit(solution)/shard_map/chips/ppermute | solution.py:26
  25.7 1.5 %collective-permute-start.8 = (bf16[4,24,4224]{2,1,0:T(8,128)(2,1)S(1)}, bf16[4,24,4224]{2,1,0:T(8,128)(2,1)S(1)}, u32[]{:S(2)}, u32[]{:S(2)}) collective-permute-start(bf16[4,24,4224]{2,1,0:T(8,128)(2,1)S(1)} %shard_map.52.refs_0_), channel_id=1, source_target_pairs={{0,8},{4,12},{8,0},{12,4},{16,24},{20,28},{24,16},{28,20},{1,9},{5... | collective-permute-start | bytes 2433032 | tf_op jit(solution)/shard_map/chips/ppermute | solution.py:26
  27.2 4.1 %collective-permute-start.13 = (bf16[192,2048]{1,0:T(8,128)(2,1)S(1)}, bf16[192,2048]{1,0:T(8,128)(2,1)S(1)}, u32[]{:S(2)}, u32[]{:S(2)}) collective-permute-start(bf16[192,2048]{1,0:T(8,128)(2,1)S(1)} %shard_map.53.refs_0_), channel_id=1, source_target_pairs={{0,2},{1,3},{2,0},{3,1},{4,6},{5,7},{6,4},{7,5},{8,10},{9,11},{10,... | collective-permute-start | bytes 2359304 | tf_op jit(solution)/shard_map/planes_far/ppermute | solution.py:30
  31.3 10.0 %collective-permute-done.9.refs_2_ = bf16[4,24,4224]{2,1,0:T(8,128)(2,1)S(1)} collective-permute-done((bf16[4,24,4224]{2,1,0:T(8,128)(2,1)S(1)}, bf16[4,24,4224]{2,1,0:T(8,128)(2,1)S(1)}, u32[]{:S(2)}, u32[]{:S(2)}) %collective-permute-start.9) | collective-permute-done | bytes 811040 | tf_op jit(solution)/shard_map/chips/ppermute | solution.py:26
  41.3 1.6 %collective-permute-start.10 = (bf16[2,24,4224]{2,1,0:T(8,128)(2,1)S(1)}, bf16[2,24,4224]{2,1,0:T(8,128)(2,1)S(1)}, u32[]{:S(2)}, u32[]{:S(2)}) collective-permute-start(bf16[2,24,4224]{2,1,0:T(8,128)(2,1)S(1)} %slice.8), channel_id=1, source_target_pairs={{0,8},{4,12},{8,0},{12,4},{16,24},{20,28},{24,16},{28,20},{1,9},{5... | collective-permute-start | bytes 1216520 | tf_op jit(solution)/shard_map/chips/ppermute | solution.py:26
  42.9 1.8 %collective-permute-done.8.refs_1_ = bf16[4,24,4224]{2,1,0:T(8,128)(2,1)S(1)} collective-permute-done((bf16[4,24,4224]{2,1,0:T(8,128)(2,1)S(1)}, bf16[4,24,4224]{2,1,0:T(8,128)(2,1)S(1)}, u32[]{:S(2)}, u32[]{:S(2)}) %collective-permute-start.8) | collective-permute-done | bytes 811040 | tf_op jit(solution)/shard_map/chips/ppermute | solution.py:26
  44.8 20.6 %collective-permute-done.13.refs_1_.refs_2_ = bf16[192,2048]{1,0:T(8,128)(2,1)S(1)} collective-permute-done((bf16[192,2048]{1,0:T(8,128)(2,1)S(1)}, bf16[192,2048]{1,0:T(8,128)(2,1)S(1)}, u32[]{:S(2)}, u32[]{:S(2)}) %collective-permute-start.13) | collective-permute-done | bytes 786464 | tf_op jit(solution)/shard_map/planes_far/ppermute | solution.py:30
  65.4 1.1 %collective-permute-done.12.refs_1_ = bf16[192,2048]{1,0:T(8,128)(2,1)S(1)} collective-permute-done((bf16[192,2048]{1,0:T(8,128)(2,1)S(1)}, bf16[192,2048]{1,0:T(8,128)(2,1)S(1)}, u32[]{:S(2)}, u32[]{:S(2)}) %collective-permute-start.12) | collective-permute-done | bytes 786464 | tf_op jit(solution)/shard_map/planes_near/ppermute | solution.py:30
  66.9 0.7 collective-permute-start.17
  67.6 0.7 collective-permute-start.18
  68.3 2.7 %collective-permute-start.14 = (bf16[192,1024]{1,0:T(8,128)(2,1)S(1)}, bf16[192,1024]{1,0:T(8,128)(2,1)S(1)}, u32[]{:S(2)}, u32[]{:S(2)}) collective-permute-start(bf16[192,1024]{1,0:T(8,128)(2,1)S(1)} %get-tuple-element.67), channel_id=1, source_target_pairs={{0,1},{1,0},{2,3},{3,2},{4,5},{5,4},{6,7},{7,6},{8,9},{9,8},{10,11... | collective-permute-start | bytes 1179656 | tf_op jit(solution)/shard_map/planes_last/ppermute | solution.py:30
  71.0 0.9 collective-permute-start.15
  71.9 0.7 collective-permute-done.16.refs_1_
  72.6 1.1 %shard_map.56 = (bf16[768,4096]{1,0:T(8,128)(2,1)S(1)}, f32[8,4096]{1,0:T(8,128)S(1)}, bf16[768,128]{1,0:T(8,128)(2,1)S(1)}, f32[128,128]{1,0:T(8,128)S(1)}) custom-call(bf16[16,24,4224]{2,1,0:T(8,128)(2,1)S(1)} %shard_map.55.refs_0_, bf16[16,24,4224]{2,1,0:T(8,128)(2,1)S(1)} %collective-permute-done.16.refs_1_), custom_call_target="tpu_custom_call" | custom-call | tf_op jit(solution)/shard_map/pallas_call | solution.py:358
  73.8 7.1 %shard_map.57 = (f32[1024,4096]{1,0:T(8,128)S(1)}, f32[1024,128]{1,0:T(8,128)S(1)}) custom-call(bf16[192,2048]{1,0:T(8,128)(2,1)S(1)} %shard_map.53.refs_0_, bf16[192,2048]{1,0:T(8,128)(2,1)S(1)} %collective-permute-done.12.refs_1_, bf16[192,2048]{1,0:T(8,128)(2,1)S(1)} %collective-permute-done.13.refs_1_.refs_2_, ...), custom_call_target="tpu_custom_call" | custom-call | tf_op jit(solution)/shard_map/pallas_call | solution.py:358
  80.9 6.2 %copy-done = f32[1024,4096]{1,0:T(8,128)} copy-done((f32[1024,4096]{1,0:T(8,128)}, f32[1024,4096]{1,0:T(8,128)S(1)}, u32[]{:S(2)}) %copy-start) | copy-done | bytes 16777240
  87.0 5.8 %copy-done.1 = f32[1024,4096]{1,0:T(8,128)S(1)} copy-done((f32[1024,4096]{1,0:T(8,128)S(1)}, f32[1024,4096]{1,0:T(8,128)}, u32[]{:S(2)}) %copy-start.1) | copy-done | bytes 16777240
  92.8 6.5 %shard_map.58 = (f32[2048,4096]{1,0:T(8,128)}, f32[128,512]{1,0:T(8,128)}) custom-call(bf16[192,2048]{1,0:T(8,128)(2,1)S(1)} %shard_map.53.refs_0_, bf16[192,2048]{1,0:T(8,128)(2,1)S(1)} %collective-permute-done.12.refs_1_, bf16[192,2048]{1,0:T(8,128)(2,1)S(1)} %collective-permute-done.13.refs_1_.refs_2_, ...), custom_call_target="tpu_custom_call" | custom-call | bytes 2097152 | tf_op jit(solution)/shard_map/pallas_call | solution.py:339
  99.3 8.4 %shard_map.59 = (f32[2048,4096]{1,0:T(8,128)}, f32[128,512]{1,0:T(8,128)}) custom-call(bf16[192,2048]{1,0:T(8,128)(2,1)S(1)} %shard_map.53.refs_0_, bf16[192,2048]{1,0:T(8,128)(2,1)S(1)} %collective-permute-done.12.refs_1_, bf16[192,2048]{1,0:T(8,128)(2,1)S(1)} %collective-permute-done.13.refs_1_.refs_2_, ...), custom_call_target="tpu_custom_call", output_to_operand_aliasing={{0}: (9, {}), {1}: (10, {})} | custom-call | bytes 2097152 | tf_op jit(solution)/shard_map/pallas_call | solution.py:217
  (25 shorter events, 0.8 us)
Async XLA Ops:
  1.3 1.1 %copy-start.2 = (bf16[24,16384]{1,0:T(8,128)(2,1)S(1)}, bf16[24,16384]{1,0:T(8,128)(2,1)}, u32[]{:S(2)}) copy-start(bf16[24,16384]{1,0:T(8,128)(2,1)} %features_hbm.1) | copy-start | bytes 2359300
  3.2 15.9 %collective-permute-start.3 = (bf16[24,4224]{1,0:T(8,128)(2,1)S(1)}, bf16[24,4224]{1,0:T(8,128)(2,1)S(1)}, u32[]{:S(2)}, u32[]{:S(2)}) collective-permute-start(bf16[24,4224]{1,0:T(8,128)(2,1)S(1)} %get-tuple-element.47), channel_id=1, source_target_pairs={{0,2},{1,3},{2,0},{3,1},{4,6},{5,7},{6,4},{7,5},{8,10},{9,11},{10,... | collective-permute-start | bytes 608264 | tf_op jit(solution)/shard_map/ppermute | solution.py:30
  7.3 7.8 %collective-permute-start = (bf16[24,4096]{1,0:T(8,128)(2,1)S(1)}, bf16[24,4096]{1,0:T(8,128)(2,1)S(1)}, u32[]{:S(2)}, u32[]{:S(2)}) collective-permute-start(bf16[24,4096]{1,0:T(8,128)(2,1)S(1)} %get-tuple-element.44), channel_id=1, source_target_pairs={{0,8},{4,12},{8,0},{12,4},{16,24},{20,28},{24,16},{28,20},{1,9},{5... | collective-permute-start | bytes 589832 | tf_op jit(solution)/shard_map/ppermute | solution.py:26
  8.8 10.3 %collective-permute-start.1 = (bf16[24,4096]{1,0:T(8,128)(2,1)S(1)}, bf16[24,4096]{1,0:T(8,128)(2,1)S(1)}, u32[]{:S(2)}, u32[]{:S(2)}) collective-permute-start(bf16[24,4096]{1,0:T(8,128)(2,1)S(1)} %get-tuple-element.45), channel_id=1, source_target_pairs={{0,16},{4,20},{8,24},{12,28},{16,0},{20,4},{24,8},{28,12},{1,17},{... | collective-permute-start | bytes 589832 | tf_op jit(solution)/shard_map/ppermute | solution.py:26
  10.3 8.8 %collective-permute-start.2 = (bf16[24,4096]{1,0:T(8,128)(2,1)S(1)}, bf16[24,4096]{1,0:T(8,128)(2,1)S(1)}, u32[]{:S(2)}, u32[]{:S(2)}) collective-permute-start(bf16[24,4096]{1,0:T(8,128)(2,1)S(1)} %get-tuple-element.46), channel_id=1, source_target_pairs={{0,24},{4,28},{8,16},{12,20},{16,8},{20,12},{24,0},{28,4},{1,25},{... | collective-permute-start | bytes 589832 | tf_op jit(solution)/shard_map/ppermute | solution.py:26
  10.8 13.2 %collective-permute-start.6 = (bf16[24,4224]{1,0:T(8,128)(2,1)S(1)}, bf16[24,4224]{1,0:T(8,128)(2,1)S(1)}, u32[]{:S(2)}, u32[]{:S(2)}) collective-permute-start(bf16[24,4224]{1,0:T(8,128)(2,1)S(1)} %get-tuple-element.55), channel_id=1, source_target_pairs={{0,1},{1,0},{2,3},{3,2},{4,5},{5,4},{6,7},{7,6},{8,9},{9,8},{10,11... | collective-permute-start | bytes 608264 | tf_op jit(solution)/shard_map/ppermute | solution.py:30
  15.1 8.8 %collective-permute-start.7 = (bf16[24,4224]{1,0:T(8,128)(2,1)S(1)}, bf16[24,4224]{1,0:T(8,128)(2,1)S(1)}, u32[]{:S(2)}, u32[]{:S(2)}) collective-permute-start(bf16[24,4224]{1,0:T(8,128)(2,1)S(1)} %get-tuple-element.57), channel_id=1, source_target_pairs={{0,3},{1,2},{2,1},{3,0},{4,7},{5,6},{6,5},{7,4},{8,11},{9,10},{10,... | collective-permute-start | bytes 608264 | tf_op jit(solution)/shard_map/ppermute | solution.py:30
  19.1 4.8 %collective-permute-start.4 = (bf16[4,24,1024]{2,1,0:T(8,128)(2,1)S(1)}, bf16[4,24,1024]{2,1,0:T(8,128)(2,1)S(1)}, u32[]{:S(2)}, u32[]{:S(2)}) collective-permute-start(bf16[4,24,1024]{2,1,0:T(8,128)(2,1)S(1)} %get-tuple-element.52), channel_id=1, source_target_pairs={{0,4},{4,0},{8,12},{12,8},{16,20},{20,16},{24,28},{28,24},{1,5},{5... | collective-permute-start | bytes 589832 | tf_op jit(solution)/shard_map/ppermute | solution.py:26
  19.2 4.8 %collective-permute-start.5 = (bf16[4,24,1024]{2,1,0:T(8,128)(2,1)S(1)}, bf16[4,24,1024]{2,1,0:T(8,128)(2,1)S(1)}, u32[]{:S(2)}, u32[]{:S(2)}) collective-permute-start(bf16[4,24,1024]{2,1,0:T(8,128)(2,1)S(1)} %get-tuple-element.53), channel_id=1, source_target_pairs={{0,4},{4,0},{8,12},{12,8},{16,20},{20,16},{24,28},{28,24},{1,5},{5... | collective-permute-start | bytes 589832 | tf_op jit(solution)/shard_map/ppermute | solution.py:26
  24.0 17.3 %collective-permute-start.9 = (bf16[4,24,4224]{2,1,0:T(8,128)(2,1)S(1)}, bf16[4,24,4224]{2,1,0:T(8,128)(2,1)S(1)}, u32[]{:S(2)}, u32[]{:S(2)}) collective-permute-start(bf16[4,24,4224]{2,1,0:T(8,128)(2,1)S(1)} %shard_map.52.refs_0_), channel_id=1, source_target_pairs={{0,16},{4,20},{8,24},{12,28},{16,0},{20,4},{24,8},{28,12},{1,17},{... | collective-permute-start | bytes 2433032 | tf_op jit(solution)/shard_map/chips/ppermute | solution.py:26
  25.7 19.0 %collective-permute-start.8 = (bf16[4,24,4224]{2,1,0:T(8,128)(2,1)S(1)}, bf16[4,24,4224]{2,1,0:T(8,128)(2,1)S(1)}, u32[]{:S(2)}, u32[]{:S(2)}) collective-permute-start(bf16[4,24,4224]{2,1,0:T(8,128)(2,1)S(1)} %shard_map.52.refs_0_), channel_id=1, source_target_pairs={{0,8},{4,12},{8,0},{12,4},{16,24},{20,28},{24,16},{28,20},{1,9},{5... | collective-permute-start | bytes 2433032 | tf_op jit(solution)/shard_map/chips/ppermute | solution.py:26
  27.2 38.2 %collective-permute-start.13 = (bf16[192,2048]{1,0:T(8,128)(2,1)S(1)}, bf16[192,2048]{1,0:T(8,128)(2,1)S(1)}, u32[]{:S(2)}, u32[]{:S(2)}) collective-permute-start(bf16[192,2048]{1,0:T(8,128)(2,1)S(1)} %shard_map.53.refs_0_), channel_id=1, source_target_pairs={{0,2},{1,3},{2,0},{3,1},{4,6},{5,7},{6,4},{7,5},{8,10},{9,11},{10,... | collective-permute-start | bytes 2359304 | tf_op jit(solution)/shard_map/planes_far/ppermute | solution.py:30
  31.3 35.2 %collective-permute-start.12 = (bf16[192,2048]{1,0:T(8,128)(2,1)S(1)}, bf16[192,2048]{1,0:T(8,128)(2,1)S(1)}, u32[]{:S(2)}, u32[]{:S(2)}) collective-permute-start(bf16[192,2048]{1,0:T(8,128)(2,1)S(1)} %shard_map.53.refs_0_), channel_id=1, source_target_pairs={{0,1},{1,0},{2,3},{3,2},{4,5},{5,4},{6,7},{7,6},{8,9},{9,8},{10,11... | collective-permute-start | bytes 2359304 | tf_op jit(solution)/shard_map/planes_near/ppermute | solution.py:30
  41.3 25.2 %collective-permute-start.10 = (bf16[2,24,4224]{2,1,0:T(8,128)(2,1)S(1)}, bf16[2,24,4224]{2,1,0:T(8,128)(2,1)S(1)}, u32[]{:S(2)}, u32[]{:S(2)}) collective-permute-start(bf16[2,24,4224]{2,1,0:T(8,128)(2,1)S(1)} %slice.8), channel_id=1, source_target_pairs={{0,8},{4,12},{8,0},{12,4},{16,24},{20,28},{24,16},{28,20},{1,9},{5... | collective-permute-start | bytes 1216520 | tf_op jit(solution)/shard_map/chips/ppermute | solution.py:26
  44.7 21.8 %collective-permute-start.11 = (bf16[2,24,4224]{2,1,0:T(8,128)(2,1)S(1)}, bf16[2,24,4224]{2,1,0:T(8,128)(2,1)S(1)}, u32[]{:S(2)}, u32[]{:S(2)}) collective-permute-start(bf16[2,24,4224]{2,1,0:T(8,128)(2,1)S(1)} %slice.9), channel_id=1, source_target_pairs={{0,16},{4,20},{8,24},{12,28},{16,0},{20,4},{24,8},{28,12},{1,17},{... | collective-permute-start | bytes 1216520 | tf_op jit(solution)/shard_map/chips/ppermute | solution.py:26
  66.8 5.9 %collective-permute-start.16 = (bf16[16,24,4224]{2,1,0:T(8,128)(2,1)S(1)}, bf16[16,24,4224]{2,1,0:T(8,128)(2,1)S(1)}, u32[]{:S(2)}, u32[]{:S(2)}) collective-permute-start(bf16[16,24,4224]{2,1,0:T(8,128)(2,1)S(1)} %shard_map.55.refs_0_), channel_id=1, source_target_pairs={{0,4},{4,0},{8,12},{12,8},{16,20},{20,16},{24,28},{28,24},{1,5},{5... | collective-permute-start | bytes 9732104 | tf_op jit(solution)/shard_map/cores/ppermute | solution.py:26
  66.9 20.1 %collective-permute-start.17 = (bf16[192,1024]{1,0:T(8,128)(2,1)S(1)}, bf16[192,1024]{1,0:T(8,128)(2,1)S(1)}, u32[]{:S(2)}, u32[]{:S(2)}) collective-permute-start(bf16[192,1024]{1,0:T(8,128)(2,1)S(1)} %get-tuple-element.78), channel_id=1, source_target_pairs={{0,1},{1,0},{2,3},{3,2},{4,5},{5,4},{6,7},{7,6},{8,9},{9,8},{10,11... | collective-permute-start | bytes 1179656 | tf_op jit(solution)/shard_map/planes_last/ppermute | solution.py:30
  67.6 19.4 %collective-permute-start.18 = (bf16[192,1024]{1,0:T(8,128)(2,1)S(1)}, bf16[192,1024]{1,0:T(8,128)(2,1)S(1)}, u32[]{:S(2)}, u32[]{:S(2)}) collective-permute-start(bf16[192,1024]{1,0:T(8,128)(2,1)S(1)} %get-tuple-element.79), channel_id=1, source_target_pairs={{0,0},{1,2},{2,1},{3,3},{4,4},{5,6},{6,5},{7,7},{8,8},{9,10},{10,9... | collective-permute-start | bytes 1179656 | tf_op jit(solution)/shard_map/planes_last/ppermute | solution.py:38
  68.3 31.0 %collective-permute-start.14 = (bf16[192,1024]{1,0:T(8,128)(2,1)S(1)}, bf16[192,1024]{1,0:T(8,128)(2,1)S(1)}, u32[]{:S(2)}, u32[]{:S(2)}) collective-permute-start(bf16[192,1024]{1,0:T(8,128)(2,1)S(1)} %get-tuple-element.67), channel_id=1, source_target_pairs={{0,1},{1,0},{2,3},{3,2},{4,5},{5,4},{6,7},{7,6},{8,9},{9,8},{10,11... | collective-permute-start | bytes 1179656 | tf_op jit(solution)/shard_map/planes_last/ppermute | solution.py:30
  71.0 28.3 %collective-permute-start.15 = (bf16[192,1024]{1,0:T(8,128)(2,1)S(1)}, bf16[192,1024]{1,0:T(8,128)(2,1)S(1)}, u32[]{:S(2)}, u32[]{:S(2)}) collective-permute-start(bf16[192,1024]{1,0:T(8,128)(2,1)S(1)} %get-tuple-element.68), channel_id=1, source_target_pairs={{0,0},{1,2},{2,1},{3,3},{4,4},{5,6},{6,5},{7,7},{8,8},{9,10},{10,9... | collective-permute-start | bytes 1179656 | tf_op jit(solution)/shard_map/planes_last/ppermute | solution.py:38
  80.9 6.2 %copy-start = (f32[1024,4096]{1,0:T(8,128)}, f32[1024,4096]{1,0:T(8,128)S(1)}, u32[]{:S(2)}) copy-start(f32[1024,4096]{1,0:T(8,128)S(1)} %get-tuple-element.80.refs_5_) | copy-start | bytes 50331652
  87.0 5.8 %copy-start.1 = (f32[1024,4096]{1,0:T(8,128)S(1)}, f32[1024,4096]{1,0:T(8,128)}, u32[]{:S(2)}) copy-start(f32[1024,4096]{1,0:T(8,128)} %copy-done) | copy-start | bytes 50331652
